TPU v7x, 128 devices: a whole 4x4x4 slice. The times are simulated.
128 devices in a mesh: lon: 32 (over y, z, x_lo), lat: 4 (over x_hi, core).
Axes of the slice: x: 4 (x_hi: 2, x_lo: 2; x = x_hi * 2 + x_lo), y: 4, z: 4, core: 2. Of those that a mesh axis runs over, the one named last changes fastest.
Arguments:
- inputs: bfloat16 [1, 8, 48, 384, 192], P(None, None, 'lat', 'lon'), may hold values from -6 to 6
- upstream: bfloat16 [1, 8, 48, 384, 192], P(None, None, 'lat', 'lon'), may hold values from -6 to 6
- land_ids: int32 [48, 384], P('lat', 'lon'), may hold values from 0 to 3
- window_kinds: int32 [32], P('lat'), may hold values from 0 to 31, each once
- class_table: float32 [4, 192], replicated, may hold values from -3 to 3
- norm_gain: float32 [192], replicated, may hold values from 0.5 to 1.5
- norm_bias: float32 [192], replicated, may hold values from -3 to 3
- qkv_weight: bfloat16 [192, 576], replicated, may hold values from -0.4375 to 0.4375
- qkv_bias: float32 [576], replicated, may hold values from -3 to 3
- out_weight: bfloat16 [192, 192], replicated, may hold values from -0.4375 to 0.4375
- bias_table: float32 [32, 6, 3312], replicated, may hold values from -8 to 330
Outputs:
- grad_inputs: bfloat16 [1, 8, 48, 384, 192], P(None, None, 'lat', 'lon')
- grad_class: float32 [4, 192], replicated
- grad_gain: float32 [192], replicated
- grad_norm_bias: float32 [192], replicated
- grad_qkv_weight: float32 [192, 576], replicated
- grad_qkv_bias: float32 [576], replicated
- grad_out_weight: float32 [192, 192], replicated
- grad_out_bias: float32 [192], replicated
- grad_table: float32 [32, 6, 3312], replicated
Inputs may be any that keep to these rules, and one draw needn't show every extreme that they name: `window_kinds`: each row of bias_table serves exactly one window position.
All inputs are finite; a program needn't handle non-finite values.
Results may differ from a plain program's by a relative error of at most 0.0095.
Values may be sent and summed in bfloat16 or wider, within the bound.
No kernel may reach another device: no remote copies, remote signals or barrier semaphores. Data moves between devices by JAX's collectives and lax.ppermute only.
A program may use at most 256 MiB of HBM per device.

v0:
```python
import math

import jax
import jax.numpy as jnp
from jax import lax
from jax.sharding import PartitionSpec as P

WIDTH = 192
HEADS = 6
HEAD_DIM = 32
WIN_LEVELS = 2
WIN_LAT = 6
WIN_LON = 12
CLASSES = 4
WIN_TOKENS = 144
POSITIONS = 3312


HIGHEST_PRECISION = lax.Precision.HIGHEST
MASKED_SCORE = -1000000000.0
NORM_EPS = 1e-05


def passed_along(array, axis, by):
    peers = lax.axis_size(axis)
    return lax.ppermute(array, axis, [(i, (i + by) % peers) for i in range(peers)])


def position_table():
    first_col = jnp.arange(WIN_LON)[:, None, None]
    second_col = jnp.arange(WIN_LON)[None, :, None]
    spread = jnp.arange(2 * WIN_LON - 1)[None, None, :]
    return (first_col - second_col + WIN_LON - 1 == spread).astype(jnp.float32)


def expand_bias(table_rows, offsets):
    win_count = table_rows.shape[0]
    shaped = table_rows.reshape(
        win_count, HEADS, WIN_LEVELS, WIN_LEVELS, WIN_LAT, WIN_LAT, 2 * WIN_LON - 1
    )
    expanded = jnp.einsum("nhpqabd,ijd->nhpaiqbj", shaped, offsets, precision=HIGHEST_PRECISION)
    return expanded.reshape(win_count, HEADS, WIN_TOKENS, WIN_TOKENS)


def fold_bias(grad_rows, offsets):
    win_count = grad_rows.shape[0]
    shaped = grad_rows.reshape(
        win_count, HEADS, WIN_LEVELS, WIN_LAT, WIN_LON, WIN_LEVELS, WIN_LAT, WIN_LON
    )
    folded = jnp.einsum("nhpaiqbj,ijd->nhpqabd", shaped, offsets, precision=HIGHEST_PRECISION)
    return folded.reshape(win_count, HEADS, POSITIONS)


def region_of(places, extent, window_len):
    half_len = window_len // 2
    return jnp.where(
        places < extent - window_len, 0, jnp.where(places < extent - half_len, 1, 2)
    ).astype(jnp.int32)


def layer_norm(hidden, norm_gain, norm_bias):
    average = jnp.mean(hidden, axis=-1, keepdims=True)
    centred = hidden - average
    inv_std = lax.rsqrt(jnp.mean(centred * centred, axis=-1, keepdims=True) + NORM_EPS)
    normal_hat = centred * inv_std
    return (normal_hat, inv_std, (normal_hat * norm_gain + norm_bias).astype(jnp.bfloat16))


def norm_backward(grad_normal, normal_hat, inv_std, norm_gain):
    scaled = grad_normal * norm_gain
    centred = scaled - jnp.mean(scaled, axis=-1, keepdims=True)
    return inv_std * (centred - normal_hat * jnp.mean(scaled * normal_hat, axis=-1, keepdims=True))


def split_windows(grid_field):
    leading, batch_size, levels, lat_rows, lon_cols, channels = grid_field.shape
    shaped = grid_field.reshape(
        leading,
        batch_size,
        levels // WIN_LEVELS,
        WIN_LEVELS,
        lat_rows // WIN_LAT,
        WIN_LAT,
        lon_cols // WIN_LON,
        WIN_LON,
        channels,
    )
    shaped = shaped.transpose(0, 1, 2, 4, 6, 3, 5, 7, 8)
    return shaped.reshape(leading, -1, WIN_TOKENS, channels)


def merge_windows(windows, batch_size, levels, lat_rows, lon_cols):
    channels = windows.shape[-1]
    shaped = windows.reshape(
        batch_size,
        levels // WIN_LEVELS,
        lat_rows // WIN_LAT,
        lon_cols // WIN_LON,
        WIN_LEVELS,
        WIN_LAT,
        WIN_LON,
        channels,
    )
    shaped = shaped.transpose(0, 1, 4, 2, 5, 3, 6, 7)
    return shaped.reshape(batch_size, levels, lat_rows, lon_cols, channels)


def window_backward(
    normed, upstream, bias_local, batch_size, lon_windows, qkv_weight, qkv_bias, out_weight
):
    win_count = normed.shape[0]
    row_count = win_count * WIN_TOKENS
    score_scale = HEAD_DIM ** (-0.5)
    flat_rows = normed.reshape(row_count, WIDTH)
    packed = (jnp.dot(flat_rows, qkv_weight, preferred_element_type=jnp.float32) + qkv_bias).astype(
        jnp.bfloat16
    )
    packed = packed.reshape(win_count, WIN_TOKENS, 3, HEADS, HEAD_DIM).transpose(2, 0, 3, 1, 4)
    query_heads = packed[0]
    key_heads = packed[1]
    value_heads = packed[2]
    scores = (
        jnp.einsum("nhta,nhsa->nhts", query_heads, key_heads, preferred_element_type=jnp.float32)
        * score_scale
    )
    scores = (
        scores.reshape(batch_size, bias_local.shape[0], lon_windows, HEADS, WIN_TOKENS, WIN_TOKENS)
        + bias_local[None, :, None]
    )
    scores = scores.reshape(win_count, HEADS, WIN_TOKENS, WIN_TOKENS)
    highest = jnp.max(scores, axis=-1, keepdims=True)
    powers = jnp.exp(scores - highest)
    attention = powers / jnp.sum(powers, axis=-1, keepdims=True)
    attention_low = attention.astype(jnp.bfloat16)
    mixed_heads = jnp.einsum(
        "nhts,nhsa->nhta", attention_low, value_heads, preferred_element_type=jnp.float32
    ).astype(jnp.bfloat16)
    mixed_rows = mixed_heads.transpose(0, 2, 1, 3).reshape(row_count, WIDTH)
    grad_rows = upstream.reshape(row_count, WIDTH)
    grad_wout = jnp.dot(mixed_rows.T, grad_rows, preferred_element_type=jnp.float32)
    grad_bout = jnp.sum(grad_rows.astype(jnp.float32), axis=0)
    grad_mixed = jnp.dot(grad_rows, out_weight.T, preferred_element_type=jnp.float32).astype(
        jnp.bfloat16
    )
    grad_mixed = grad_mixed.reshape(win_count, WIN_TOKENS, HEADS, HEAD_DIM).transpose(0, 2, 1, 3)
    grad_attention = jnp.einsum(
        "nhta,nhsa->nhts", grad_mixed, value_heads, preferred_element_type=jnp.float32
    )
    grad_values = jnp.einsum(
        "nhts,nhta->nhsa", attention_low, grad_mixed, preferred_element_type=jnp.float32
    )
    grad_scores = attention * (
        grad_attention - jnp.sum(grad_attention * attention, axis=-1, keepdims=True)
    )
    grad_scores_low = grad_scores.astype(jnp.bfloat16)
    grad_query = (
        jnp.einsum(
            "nhts,nhsa->nhta", grad_scores_low, key_heads, preferred_element_type=jnp.float32
        )
        * score_scale
    )
    grad_keys = (
        jnp.einsum(
            "nhts,nhta->nhsa", grad_scores_low, query_heads, preferred_element_type=jnp.float32
        )
        * score_scale
    )
    grad_packed = (
        jnp.stack([grad_query, grad_keys, grad_values], axis=0)
        .transpose(1, 3, 0, 2, 4)
        .reshape(row_count, 3 * WIDTH)
    )
    grad_bqkv = jnp.sum(grad_packed, axis=0)
    grad_packed_low = grad_packed.astype(jnp.bfloat16)
    grad_wqkv = jnp.dot(flat_rows.T, grad_packed_low, preferred_element_type=jnp.float32)
    grad_normed = jnp.dot(grad_packed_low, qkv_weight.T, preferred_element_type=jnp.float32)
    return (
        grad_normed.reshape(win_count, WIN_TOKENS, WIDTH),
        grad_scores,
        grad_wqkv,
        grad_bqkv,
        grad_wout,
        grad_bout,
    )


def shards(
    inputs,
    upstream,
    land_ids,
    window_kinds,
    class_table,
    norm_gain,
    norm_bias,
    qkv_weight,
    qkv_bias,
    out_weight,
    bias_table,
):
    batch_size, levels, lat_rows, lon_cols, channels = inputs.shape
    table_count = bias_table.shape[0]
    level_windows = levels // WIN_LEVELS
    lat_windows = lat_rows // WIN_LAT
    lon_windows = lon_cols // WIN_LON
    level_shift = WIN_LEVELS // 2
    lat_shift = WIN_LAT // 2
    lon_shift = WIN_LON // 2
    offsets = position_table()
    classes_hot = (land_ids[:, :, None] == jnp.arange(CLASSES)[None, None, :]).astype(jnp.float32)
    embedded = jnp.einsum("yxk,kc->yxc", classes_hot, class_table, precision=HIGHEST_PRECISION)
    hidden = inputs.astype(jnp.float32) + embedded
    normal_hat, inv_std, normed = layer_norm(hidden, norm_gain, norm_bias)
    stacked = jnp.stack([normed, upstream])
    arriving = passed_along(stacked[:, :, :, :, :lon_shift], "lon", -1)
    stacked = jnp.concatenate([stacked[:, :, :, :, lon_shift:], arriving], axis=4)
    arriving = passed_along(stacked[:, :, :, :lat_shift], "lat", -1)
    stacked = jnp.concatenate([stacked[:, :, :, lat_shift:], arriving], axis=3)
    stacked = jnp.roll(stacked, -level_shift, axis=2)
    windows = split_windows(stacked)
    total_lat = lat_rows * lax.axis_size("lat")
    lat_places = lax.axis_index("lat") * lat_rows + jnp.arange(lat_rows)
    level_region = region_of(jnp.arange(levels), levels, WIN_LEVELS).reshape(
        level_windows, WIN_LEVELS
    )
    lat_region = region_of(lat_places, total_lat, WIN_LAT).reshape(lat_windows, WIN_LAT)
    token_region = (
        level_region[:, None, :, None, None] * 3
        + lat_region[None, :, None, :, None]
        + jnp.zeros((1, 1, 1, 1, WIN_LON), jnp.int32)
    )
    token_region = token_region.reshape(level_windows * lat_windows, WIN_TOKENS)
    same_region = token_region[:, :, None] == token_region[:, None, :]
    kinds_grid = window_kinds.reshape(lat_windows, level_windows).T.reshape(-1)
    table_rows = jnp.take(bias_table, kinds_grid, axis=0)
    bias_local = jnp.where(same_region[:, None], expand_bias(table_rows, offsets), MASKED_SCORE)
    grad_windows, grad_scores, grad_wqkv, grad_bqkv, grad_wout, grad_bout = window_backward(
        windows[0],
        windows[1],
        bias_local,
        batch_size,
        lon_windows,
        qkv_weight,
        qkv_bias,
        out_weight,
    )
    score_sum = grad_scores.reshape(
        batch_size, level_windows, lat_windows, lon_windows, HEADS, WIN_TOKENS, WIN_TOKENS
    ).sum(axis=(0, 3))
    compact = fold_bias(score_sum.reshape(-1, HEADS, WIN_TOKENS, WIN_TOKENS), offsets)
    grad_shifted = merge_windows(grad_windows, batch_size, levels, lat_rows, lon_cols)
    grad_shifted = jnp.roll(grad_shifted, level_shift, axis=1)
    returning = passed_along(grad_shifted[:, :, -lat_shift:].astype(jnp.bfloat16), "lat", 1).astype(
        jnp.float32
    )
    grad_shifted = jnp.concatenate([returning, grad_shifted[:, :, :-lat_shift]], axis=2)
    returning = passed_along(grad_shifted[:, :, :, -lon_shift:], "lon", 1)
    grad_normal = jnp.concatenate([returning, grad_shifted[:, :, :, :-lon_shift]], axis=3)
    grad_hidden = upstream.astype(jnp.float32) + norm_backward(
        grad_normal, normal_hat, inv_std, norm_gain
    )
    grad_inputs = grad_hidden.astype(jnp.bfloat16)
    grad_gain = jnp.sum(grad_normal * normal_hat, axis=(0, 1, 2, 3))
    grad_shift_sum = jnp.sum(grad_normal, axis=(0, 1, 2, 3))
    grad_class = jnp.einsum(
        "yxk,yxc->kc", classes_hot, jnp.sum(grad_hidden, axis=(0, 1)), precision=HIGHEST_PRECISION
    )
    token_root = math.sqrt(batch_size * levels * total_lat * lon_cols * lax.axis_size("lon"))
    kinds_hot = (kinds_grid[:, None] == jnp.arange(table_count)[None, :]).astype(jnp.float32)
    local_table = jnp.einsum("wt,whp->thp", kinds_hot, compact, precision=HIGHEST_PRECISION)
    summed = lax.psum(
        (
            grad_class,
            grad_gain,
            grad_shift_sum,
            grad_wqkv,
            grad_bqkv,
            grad_wout,
            grad_bout,
            local_table,
        ),
        ("lon", "lat"),
    )
    grad_table = summed[7]
    return (
        grad_inputs,
        summed[0] / token_root,
        summed[1] / token_root,
        summed[2] / token_root,
        summed[3] / token_root,
        summed[4] / token_root,
        summed[5] / token_root,
        summed[6] / token_root,
        grad_table / token_root,
    )


def solution(mesh):
    placed = (
        P(None, None, "lat", "lon", None),
        P(None, None, "lat", "lon", None),
        P("lat", "lon"),
        P("lat"),
        P(),
        P(),
        P(),
        P(),
        P(),
        P(),
        P(),
    )
    return jax.shard_map(
        shards,
        mesh=mesh,
        in_specs=placed,
        out_specs=(P(None, None, "lat", "lon", None), P(), P(), P(), P(), P(), P(), P(), P()),
        check_vma=False,
    )
```

profile of v0, /device:TPU:1, one launch (start us, length us, event | category | flops | bytes accessed | tf_op | source)
XLA Modules:
  0.0 578.9 jit_solution(2386496982477800376)
XLA Ops:
  13.9 8.0 %collective-permute-start = (bf16[2,1,8,12,6,192]{5,2,4,3,1,0:T(8,128)(2,1)}, bf16[2,1,8,12,6,192]{5,2,4,3,1,0:T(8,128)(2,1)}, u32[]{:S(2)}, u32[]{:S(2)}) collective-permute-start(bf16[2,1,8,12,6,192]{5,2,4,3,1,0:T(8,128)(2,1)} %get-tuple-element.37), channel_id=1, source_target_pairs={{0,124},{4,0},{8,4},{12,8},{16,12},{20,16},{24,20},{28,24},{32,28}... | collective-permute-start | bytes 1327112 | tf_op jit(solution)/shard_map/ppermute | solution.py:26
  22.4 2.3 gather_fusion
  24.6 5.5 gather.7
  30.1 3.0 broadcast_select_fusion
  33.2 21.7 %convolution_bitcast_fusion = f32[8,6,2,6,12,2,6,12]{7,0,6,3,5,2,1,4:T(8,128)} fusion(f32[8,6,2,2,6,6,23]{6,5,4,3,2,0,1:T(8,128)S(1)} %broadcast_select_fusion, s32[12,12]{1,0:T(8,128)S(1)} %subtract_add_fusion), kind=kOutput, calls=%fused_computation.2 | convolution fusion | flops 274713856 | bytes 4617792 | tf_op jit(solution)/shard_map/nhpqabd,ijd->nhpaiqbj/dot_general | solution.py:41
  57.8 71.4 %copy.116 = f32[8,6,2,6,12,2,6,12]{4,3,2,7,6,5,1,0:T(8,128)} copy(f32[8,6,2,6,12,2,6,12]{7,0,6,3,5,2,1,4:T(8,128)} %convolution_bitcast_fusion) | data formatting | bytes 7962624 | tf_op jit(solution)/shard_map/reshape | solution.py:42
  129.2 37.7 %reshape.292 = f32[8,6,144,144]{2,3,1,0:T(8,128)} reshape(f32[8,6,2,6,12,2,6,12]{4,3,2,7,6,5,1,0:T(8,128)} %copy.116) | data formatting | bytes 7962624 | tf_op jit(solution)/shard_map/reshape | solution.py:42
  175.9 2.9 reshape.273
  180.9 4.1 reshape.268
  185.0 2.2 copy.142
  187.2 5.3 select_add_fusion
  192.6 4.7 fusion.62
  197.6 8.2 %fusion.18 = f32[1,8,6,144,32]{3,4,2,1,0:T(8,128)} fusion(bf16[8,144,6,32]{1,0,3,2:T(8,128)(2,1)} %reshape.273, f32[8,6,144]{2,1,0:T(8,128)S(1)} %get-tuple-element.38, f32[8,6,144,144]{2,3,1,0:T(8,128)} %copy-done.3), kind=kOutput, calls=%fused_computation.31 | convolution fusion | flops 66694032 | bytes 5336064 | tf_op jit(solution)/shard_map/nhts,nhta->nhsa/dot_general | solution.py:149
  205.8 7.5 %multiply_reduce_fusion = (f32[8,6,144]{2,1,0:T(8,128)S(1)}, f32[8,6,144,144]{2,3,1,0:T(8,128)}) fusion(f32[8,6,144,144]{2,3,1,0:T(8,128)} %get-tuple-element.39, f32[8,6,144]{2,1,0:T(8,128)S(1)} %get-tuple-element.38, bf16[3,8,6,144,32]{3,4,2,1,0:T(8,128)(2,1)S(1)} %bitcast.133, bf16[8,144,6,32]{1,0,3,2:T(8,128)(2,1)} %reshape.273), kind=kOutput, calls=%fused_computation.4 | convolution fusion | flops 66680064 | bytes 9284608 | tf_op jit(solution)/shard_map/nhta,nhsa->nhts/dot_general | solution.py:146
  213.3 7.0 %subtract_multiply_fusion = f32[8,6,144,144]{2,3,1,0:T(8,128)S(1)} fusion(f32[8,6,144,144]{2,3,1,0:T(8,128)} %get-tuple-element.41, f32[8,6,144]{2,1,0:T(8,128)S(1)} %get-tuple-element.40, f32[8,6,144,144]{2,3,1,0:T(8,128)} %get-tuple-element.39, f32[8,6,144]{2,1,0:T(8,128)S(1)} %get-tuple-element.38), kind=kLoop, calls=%fused_computation.3 | loop fusion | flops 2985984 | bytes 11999232 | tf_op jit(solution)/shard_map/mul | solution.py:152
  225.9 5.7 copy.117
  231.6 9.0 %reshape.293 = bf16[4,2,2,6,12,576]{5,4,3,2,1,0:T(8,128)(2,1)} reshape(bf16[8,144,3,6,32]{4,3,2,1,0:T(8,128)(2,1)} %copy.117) | data formatting | bytes 2654208 | tf_op jit(solution)/shard_map/convert_element_type | solution.py:174
  240.6 2.4 convolution_bitcast_fusion.2
  246.0 3.0 copy.102
  249.0 7.9 %fusion.24 = bf16[8,144,6,32]{1,3,2,0:T(8,128)(2,1)} fusion(bf16[3,8,6,144,32]{3,4,2,1,0:T(8,128)(2,1)} %bitcast.136, f32[8,6,144]{2,1,0:T(8,128)S(1)} %get-tuple-element.38, f32[8,6,144,144]{2,3,1,0:T(8,128)} %copy-done.3), kind=kOutput, calls=%fused_computation.34 | convolution fusion | flops 66915216 | bytes 15412224 | tf_op jit(solution)/shard_map/nhts,nhsa->nhta/dot_general | solution.py:135
  256.9 35.1 %reshape.294 = f32[8,6,2,6,12,2,6,12]{4,3,2,7,6,5,1,0:T(8,128)} reshape(f32[8,6,144,144]{2,3,1,0:T(8,128)} %copy-done.2) | data formatting | bytes 7962624 | tf_op jit(solution)/shard_map/reshape;reshape | solution.py:47
  292.7 2.4 collective-permute-start.2
  297.3 60.1 %copy.106 = f32[8,6,2,6,12,2,6,12]{7,0,4,6,5,3,2,1:T(8,128)} copy(f32[8,6,2,6,12,2,6,12]{4,3,2,7,6,5,1,0:T(8,128)} %reshape.294) | data formatting | bytes 7962624 | tf_op jit(solution)/shard_map/reshape;reshape | solution.py:47
  357.4 33.0 %convolution_bitcast_fusion.1 = f32[8,6,2,2,6,6,23]{6,0,5,3,4,2,1:T(8,128)S(1)} fusion(f32[8,6,2,6,12,2,6,12]{7,0,4,6,5,3,2,1:T(8,128)} %copy.106, s32[12,12]{1,0:T(8,128)S(1)} %copy-done.31), kind=kOutput, calls=%fused_computation.18 | convolution fusion | flops 274713856 | bytes 4617792 | tf_op jit(solution)/shard_map/nhpaiqbj,ijd->nhpqabd/dot_general | solution.py:50
  390.4 3.0 copy.107
  393.3 3.2 reshape.276
  396.6 2.7 fusion.53
  401.2 4.7 convert_element_type.66
  409.6 18.3 %collective-permute-done.3 = f32[1,8,12,6,192]{4,1,3,2,0:T(8,128)S(1)} collective-permute-done((f32[1,8,12,6,192]{4,1,3,2,0:T(8,128)}, f32[1,8,12,6,192]{4,1,3,2,0:T(8,128)S(1)}, u32[]{:S(2)}, u32[]{:S(2)}) %collective-permute-start.3) | collective-permute-done | bytes 442400 | tf_op jit(solution)/shard_map/ppermute | solution.py:26
  432.0 63.0 %all-reduce = (f32[4,192]{1,0:T(4,128)S(1)}, f32[192]{0:T(256)S(1)}, f32[192]{0:T(256)S(1)}, f32[576]{0:T(1024)S(1)}, f32[192]{0:T(256)S(1)}) all-reduce(f32[4,192]{1,0:T(4,128)S(1)} %convolution_bitcast_fusion.3, f32[192]{0:T(256)S(1)} %get-tuple-element.18, ...), channel_id=1, replica_groups=mesh['lon'=32,'lat'=4] {'lon','lat'}, use_global_device_ids=true, to_apply=%region_8.9 | all-reduce | flops 1920 | bytes 15360 | tf_op jit(solution)/shard_map/psum | solution.py:270
  497.8 66.8 %all-reduce.4.cloned.1.call-done = (f32[192,576]{1,0:T(8,128)}, f32[192,192]{1,0:T(8,128)}, f32[32,6,3312]{2,0,1:T(8,128)}) async-done(((f32[192,576]{1,0:T(8,128)}, f32[192,192]{1,0:T(8,128)}, f32[32,6,3312]{2,0,1:T(8,128)}), (f32[192,576]{1,0:T(8,128)}, f32[192,192]{1,0:T(8,128)}, f32[32,6,3312]{2,0,1:T(8,128)})) %all-reduce.4.cloned.1.call-update) | async-done | bytes 3133456 | tf_op jit(solution)/shard_map/psum | solution.py:270
  568.1 3.6 broadcast_multiply_fusion
  (159 shorter events, 48.4 us)
Async XLA Ops:
  7.2 15.2 %copy-start = (f32[32,6,3312]{2,0,1:T(8,128)S(1)}, f32[32,6,3312]{2,0,1:T(8,128)}, u32[]{:S(2)}) copy-start(f32[32,6,3312]{2,0,1:T(8,128)} %param.21) | copy-start | bytes 7630852
  7.2 5.3 copy-start.4
  7.2 5.3 copy-start.40
  7.2 5.3 copy-start.36
  7.2 557.4 %all-reduce.4.cloned.1.call-start = ((), (), s32[]{:S(2)}) async-start(), calls=%async_computation | async-start | bytes 6488064 | tf_op jit(solution)/shard_map/psum | solution.py:270
  8.2 5.7 copy-start.34
  8.4 4.5 copy-start.23
  9.4 4.5 copy-start.15
  10.8 11.1 %copy-start.42 = (s32[8]{0:T(128)S(1)}, s32[8]{0:T(128)}, u32[]{:S(2)}) copy-start(s32[8]{0:T(128)} %param.14) | copy-start | bytes 100
  13.9 41.2 %collective-permute-start = (bf16[2,1,8,12,6,192]{5,2,4,3,1,0:T(8,128)(2,1)}, bf16[2,1,8,12,6,192]{5,2,4,3,1,0:T(8,128)(2,1)}, u32[]{:S(2)}, u32[]{:S(2)}) collective-permute-start(bf16[2,1,8,12,6,192]{5,2,4,3,1,0:T(8,128)(2,1)} %get-tuple-element.37), channel_id=1, source_target_pairs={{0,124},{4,0},{8,4},{12,8},{16,12},{20,16},{24,20},{28,24},{32,28}... | collective-permute-start | bytes 1327112 | tf_op jit(solution)/shard_map/ppermute | solution.py:26
  22.3 7.8 %copy-start.38 = (s32[8]{0:T(128)}, s32[8]{0:T(128)S(1)}, u32[]{:S(2)}) copy-start(s32[8]{0:T(128)S(1)} %reshape.270) | copy-start | bytes 100
  22.3 10.8 %copy-start.30 = (s32[12,12]{1,0:T(8,128)}, s32[12,12]{1,0:T(8,128)S(1)}, u32[]{:S(2)}) copy-start(s32[12,12]{1,0:T(8,128)S(1)} %subtract_add_fusion) | copy-start | bytes 1732
  56.1 112.0 %collective-permute-start.1 = (bf16[2,1,8,3,12,192]{5,2,4,3,1,0:T(8,128)(2,1)S(1)}, bf16[2,1,8,3,12,192]{5,2,4,3,1,0:T(8,128)(2,1)S(1)}, u32[]{:S(2)}, u32[]{:S(2)}) collective-permute-start(bf16[2,1,8,3,12,192]{5,2,4,3,1,0:T(8,128)(2,1)S(1)} %pad_maximum_fusion.4), channel_id=1, source_target_pairs={{0,3},{1,0},{2,1},{3,2},{4,7},{5,4},{6,5},{7,6},{8,11},{9,8},{10,9... | collective-permute-start | bytes 663560 | tf_op jit(solution)/shard_map/ppermute | solution.py:26
  172.1 3.8 copy-start.13
  173.3 5.8 copy-start.41
  187.2 34.4 %copy-start.10 = (bf16[8,144,3,6,32]{1,4,3,0,2:T(8,128)(2,1)}, bf16[8,144,3,6,32]{1,4,3,0,2:T(8,128)(2,1)S(1)}, u32[]{:S(2)}) copy-start(bf16[8,144,3,6,32]{1,4,3,0,2:T(8,128)(2,1)S(1)} %copy.142) | copy-start | bytes 3981316
  192.6 5.0 copy-start.3
  231.6 9.0 %copy-start.32 = (bf16[192,576]{1,0:T(8,128)(2,1)S(1)}, bf16[192,576]{1,0:T(8,128)(2,1)}, u32[]{:S(2)}) copy-start(bf16[192,576]{1,0:T(8,128)(2,1)} %param.18) | copy-start | bytes 663556
  256.9 35.1 %copy-start.20 = (f32[1,7,12,12,192]{4,0,3,2,1:T(1,128)S(1)}, f32[1,7,12,12,192]{4,0,3,2,1:T(1,128)}, u32[]{:S(2)}) copy-start(f32[1,7,12,12,192]{4,0,3,2,1:T(1,128)} %slice.89) | copy-start | bytes 2322436
  292.6 4.6 copy-start.11
  292.7 113.2 %collective-permute-start.2 = (bf16[1,8,3,12,192]{4,1,3,2,0:T(8,128)(2,1)S(1)}, bf16[1,8,3,12,192]{4,1,3,2,0:T(8,128)(2,1)S(1)}, u32[]{:S(2)}, u32[]{:S(2)}) collective-permute-start(bf16[1,8,3,12,192]{4,1,3,2,0:T(8,128)(2,1)S(1)} %fusion.41), channel_id=1, source_target_pairs={{0,1},{1,2},{2,3},{3,0},{4,5},{5,6},{6,7},{7,4},{8,9},{9,10},{10,1... | collective-permute-start | bytes 331784 | tf_op jit(solution)/shard_map/ppermute | solution.py:26
  297.3 60.1 %copy-start.31 = (s32[12,12]{1,0:T(8,128)S(1)}, s32[12,12]{1,0:T(8,128)}, u32[]{:S(2)}) copy-start(s32[12,12]{1,0:T(8,128)} %copy-done.30) | copy-start | bytes 1732
  401.1 4.8 copy-start.12
  407.3 20.6 %collective-permute-start.3 = (f32[1,8,12,6,192]{4,1,3,2,0:T(8,128)}, f32[1,8,12,6,192]{4,1,3,2,0:T(8,128)S(1)}, u32[]{:S(2)}, u32[]{:S(2)}) collective-permute-start(f32[1,8,12,6,192]{4,1,3,2,0:T(8,128)} %get-tuple-element.35), channel_id=1, source_target_pairs={{0,4},{4,8},{8,12},{12,16},{16,20},{20,24},{24,28},{28,32},{32,36}... | collective-permute-start | bytes 1327112 | tf_op jit(solution)/shard_map/ppermute | solution.py:26
  409.3 18.6 %copy-start.5 = (bf16[1,8,12,12,192]{4,1,3,2,0:T(8,128)(2,1)S(1)}, bf16[1,8,12,12,192]{4,1,3,2,0:T(8,128)(2,1)}, u32[]{:S(2)}) copy-start(bf16[1,8,12,12,192]{4,1,3,2,0:T(8,128)(2,1)} %param.11) | copy-start | bytes 1327108
  409.3 18.6 %copy-start.16 = (f32[12,12,192]{2,1,0:T(8,128)S(1)}, f32[12,12,192]{2,1,0:T(8,128)}, u32[]{:S(2)}) copy-start(f32[12,12,192]{2,1,0:T(8,128)} %copy-done.15) | copy-start | bytes 331780
  409.4 18.6 %copy-start.22 = (f32[8,12,12]{0,2,1:T(8,128)S(1)}, f32[8,12,12]{0,2,1:T(8,128)}, u32[]{:S(2)}) copy-start(f32[8,12,12]{0,2,1:T(8,128)} %copy-done.21) | copy-start | bytes 13828
  409.4 18.6 %copy-start.28 = (f32[8,12,12]{0,2,1:T(8,128)S(1)}, f32[8,12,12]{0,2,1:T(8,128)}, u32[]{:S(2)}) copy-start(f32[8,12,12]{0,2,1:T(8,128)} %copy-done.27) | copy-start | bytes 13828
  409.4 18.6 %copy-start.37 = (f32[192]{0:T(256)S(1)}, f32[192]{0:T(256)}, u32[]{:S(2)}) copy-start(f32[192]{0:T(256)} %param.16) | copy-start | bytes 2308
  409.6 20.4 %copy-start.19 = (f32[1,8,12,6,192]{4,1,3,2,0:T(8,128)S(1)}, f32[1,8,12,6,192]{4,1,3,2,0:T(8,128)}, u32[]{:S(2)}) copy-start(f32[1,8,12,6,192]{4,1,3,2,0:T(8,128)} %get-tuple-element.34) | copy-start | bytes 1327108
  409.6 20.4 %copy-start.24 = (bf16[1,8,12,12,192]{4,1,3,2,0:T(8,128)(2,1)S(1)}, bf16[1,8,12,12,192]{4,1,3,2,0:T(8,128)(2,1)}, u32[]{:S(2)}) copy-start(bf16[1,8,12,12,192]{4,1,3,2,0:T(8,128)(2,1)} %param.12) | copy-start | bytes 1327108
  568.1 3.6 copy-start.1
  (16 other events, 35.6 us)
Sparse Core Ops, SparseCore 0:
  409.5 155.0 all-reduce.3
where the time goes:
time: 589 us; the launch traced here: 579 us
  local copies, waits for them, and re-layouts  267 us (45%)
  matrix products  97.2 us (17%)
  waiting for transfers between devices  85.1 us (14%)
  blocking collectives  63 us (11%)
  other arithmetic  40 us (7%)
  between operations  15.1 us (3%)
  starting transfers between devices  12 us (2%)
    reshape x2, local copies, waits for them, and re-layouts, expand_bias(): return expanded.reshape(win_count, HEADS, WIN_TOKENS, WIN_TOKENS)  109 us
    another operation x2, local copies, waits for them, and re-layouts, fold_bias(): grad_rows.reshape(win_count, HEADS, WIN_LEVELS, WIN_LAT, WIN_LON, WIN_LEV...  95.2 us
    psum x1, waiting for transfers between devices, shards(): lax.psum((grad_class, grad_gain, grad_shift_sum, grad_wqkv, grad_bqkv, gr...  66.8 us
    psum x1, blocking collectives, shards(): lax.psum((grad_class, grad_gain, grad_shift_sum, grad_wqkv, grad_bqkv, gr...  63 us
    dot_general x1, matrix products, fold_bias(): jnp.einsum('nhpaiqbj,ijd->nhpqabd', shaped, offsets, precision=HIGHEST_PR...  33 us
    convert_element_type x4, local copies, waits for them, and re-layouts, window_backward(): grad_packed_low = grad_packed.astype(jnp.bfloat16)  22.4 us
    dot_general x1, matrix products, expand_bias(): jnp.einsum('nhpqabd,ijd->nhpaiqbj', shaped, offsets, precision=HIGHEST_PR...  21.7 us
    ppermute x4, waiting for transfers between devices, passed_along(): lax.ppermute(array, axis, [(i, (i + by) % peers) for i in range(peers)])  18.3 us
  transfers between devices with their start and end apart: 5, of which 2 were waited for; matrix products, arithmetic and copies ran while one was open for 45% of the time, Pallas kernels for 0%

commit v1 on v0

v1 whole, which is shorter than its diff:
```python
import math

import jax
import jax.numpy as jnp
import numpy as np
from jax import lax
from jax.experimental import pallas as pl
from jax.experimental.pallas import tpu as pltpu
from jax.sharding import PartitionSpec as P

WIDTH = 192
HEADS = 6
HEAD_DIM = 32
CLASSES = 4
WIN_TOKENS = 144
POSITIONS = 3312
SPREAD = 23
GROUP = 138
PAIRS = 864
MASKED_SCORE = -1000000000.0
NORM_EPS = 1e-05
LOG2E = 1.4426950408889634
SCALE = HEAD_DIM ** (-0.5)
VMEM = 56 * 1024 * 1024
SEND_ROWS = 24
GATHER_ROWS = 56
BOTH = ("lon", "lat")

f32 = jnp.float32
bf16 = jnp.bfloat16


def dot(a, b):
    return lax.dot_general(a, b, (((1,), (0,)), ((), ())), preferred_element_type=f32)


def dot_nt(a, b):
    return lax.dot_general(a, b, (((1,), (1,)), ((), ())), preferred_element_type=f32)


def dot_tn(a, b):
    return lax.dot_general(a, b, (((0,), (0,)), ((), ())), preferred_element_type=f32)


def iota(shape, axis):
    return lax.broadcasted_iota(jnp.int32, shape, axis)


def quotient(a, b):
    return jnp.floor((a.astype(f32) + 0.5) * (1.0 / b)).astype(jnp.int32)


def bias_kernel(scal_ref, tab_ref, out_ref, sel_ref, t_ref, e_ref):
    for w in range(8):
        kind = scal_ref[w]
        for h in range(HEADS):
            sel_ref[h, w : w + 1, :] = tab_ref[h, pl.ds(kind, 1), :]
    last_lat = scal_ref[8]
    for lu in range(2):
        for lt in range(2):
            for a in range(6):
                g = (lt * 2 + lu) * 6 + a
                for h in range(HEADS):
                    row = ((lt * 6 + a) * 6 + h) * 8
                    t_ref[lu, row : row + 8, 0:GROUP] = sel_ref[h, :, g * GROUP : (g + 1) * GROUP]
    row = iota((576, GROUP), 0)
    lane = iota((576, GROUP), 1)
    win = row & 7
    la = quotient(row, 48)
    late = (la >= 6).astype(jnp.int32)
    low_lat = ((la - 6 * late) < 3).astype(jnp.int32)
    low_key = (lane < 3 * SPREAD).astype(jnp.int32)
    cut_lat = jnp.where(win >= 4, last_lat, 0) * (low_lat ^ low_key)
    cut_lev = ((win & 3) == 3).astype(jnp.int32)
    srow = iota((GROUP, 256), 0)
    scol = iota((GROUP, 256), 1)
    col_hi = (scol >= 128).astype(jnp.int32)
    col = scol - 128 * col_hi
    a_u = quotient(col, 12)
    base = a_u * SPREAD - (col - 12 * a_u) + 11
    base = jnp.where(col < 72, base + col_hi, -1000)
    for lu in range(2):
        cut = cut_lat + cut_lev * (late if lu == 0 else 1 - late)
        t = jnp.where(cut > 0, MASKED_SCORE, t_ref[lu, :, 0:GROUP] * LOG2E)
        hi = t.astype(bf16)
        rest = t - hi.astype(f32)
        mid = rest.astype(bf16)
        low = (rest - mid.astype(f32)).astype(bf16)
        for ip in range(6):
            spread = jnp.where(srow == base + 2 * ip, 1.0, 0.0).astype(bf16)
            acc = dot(hi, spread) + dot(mid, spread) + dot(low, spread)
            e_ref[2 * ip] = acc[:, 0:128]
            e_ref[2 * ip + 1] = acc[:, 128:256]
        for w in range(8):
            rows = jnp.concatenate([e_ref[i, pl.ds(w, 72, stride=8), :] for i in range(12)], axis=0)
            out_ref[w, lu * 72 : (lu + 1) * 72, :] = rows.T[0:72, :]


def expand_bias(table, scal):
    return pl.pallas_call(
        bias_kernel,
        out_shape=jax.ShapeDtypeStruct((8, WIN_TOKENS, PAIRS), f32),
        in_specs=[
            pl.BlockSpec(memory_space=pltpu.SMEM),
            pl.BlockSpec(memory_space=pltpu.VMEM),
        ],
        out_specs=pl.BlockSpec(memory_space=pltpu.VMEM),
        scratch_shapes=[
            pltpu.VMEM((HEADS, 8, POSITIONS), f32),
            pltpu.VMEM((2, 576, 256), f32),
            pltpu.VMEM((12, 576, 128), f32),
        ],
        compiler_params=pltpu.CompilerParams(vmem_limit_bytes=VMEM),
        cost_estimate=pl.CostEstimate(flops=2 * 10**9, bytes_accessed=7 * 10**6, transcendentals=0),
        name="bias",
    )(scal, table)


def window_kernel(
    x_ref,
    u_ref,
    e_ref,
    s_ref,
    d_ref,
    ids_ref,
    ct_ref,
    gain_ref,
    nb_ref,
    w_ref,
    bq_ref,
    wo_ref,
    b_ref,
    own_ref,
    eo_ref,
    so_ref,
    do_ref,
    send_ref,
    xs,
    us,
    os,
    idc,
    rep,
    rept,
    mask,
    maskt,
    fold,
    gw,
    gwo,
    sm,
    snd,
):
    w = pl.program_id(0)

    @pl.when(w == 0)
    def _():
        for half in range(2):
            lanes = slice(0, 128) if half == 0 else slice(128, 192)
            far = slice(192, 320) if half == 0 else slice(320, 384)
            width = 128 if half == 0 else 64
            for lat in range(12):
                at = lat * 96
                if lat < 9:
                    src = (lat + 3) * 96 + 48
                    xs[half, at : at + 48, 0:width] = x_ref[src : src + 48, lanes].astype(f32)
                    us[half, at : at + 48, 0:width] = u_ref[src : src + 48, lanes].astype(f32)
                    east, esrc = e_ref, lat * 48
                else:
                    src = (lat - 9) * 48
                    xs[half, at : at + 48, 0:width] = s_ref[src : src + 48, lanes].astype(f32)
                    us[half, at : at + 48, 0:width] = s_ref[src : src + 48, far].astype(f32)
                    east, esrc = d_ref, (lat - 9) * 48
                xs[half, at + 48 : at + 96, 0:width] = east[esrc : esrc + 48, lanes].astype(f32)
                us[half, at + 48 : at + 96, 0:width] = east[esrc : esrc + 48, far].astype(f32)
        id_row = (
            ids_ref[0:1, 0:WIN_TOKENS]
            + e_ref[432:440, 0:WIN_TOKENS].astype(f32)[0:1]
            + s_ref[144:152, 0:WIN_TOKENS].astype(f32)[0:1]
            + d_ref[144:152, 0:WIN_TOKENS].astype(f32)[0:1]
        )
        same = iota((WIN_TOKENS, WIN_TOKENS), 0) == iota((WIN_TOKENS, WIN_TOKENS), 1)
        column = jnp.sum(jnp.where(same, id_row, 0.0), axis=1, keepdims=True)
        idc[...] = jnp.broadcast_to(column, (WIN_TOKENS, WIDTH))
        r = iota((PAIRS, WIN_TOKENS), 0)
        i = quotient(r, 72)
        la = quotient(r - 72 * i, 6)
        rep[...] = jnp.where(la * 12 + i == iota((PAIRS, WIN_TOKENS), 1), 1.0, 0.0).astype(bf16)
        r = iota((WIN_TOKENS, PAIRS), 1)
        i = quotient(r, 72)
        la = quotient(r - 72 * i, 6)
        rept[...] = jnp.where(la * 12 + i == iota((WIN_TOKENS, PAIRS), 0), 1.0, 0.0).astype(bf16)
        r = iota((PAIRS, WIDTH), 0)
        head = r - 6 * quotient(r, 6)
        mask[...] = jnp.where(head == (iota((PAIRS, WIDTH), 1) >> 5), 1.0, 0.0).astype(bf16)
        r = iota((WIDTH, PAIRS), 1)
        head = r - 6 * quotient(r, 6)
        maskt[...] = jnp.where(head == (iota((WIDTH, PAIRS), 0) >> 5), 1.0, 0.0).astype(bf16)
        gw[...] = jnp.zeros_like(gw)
        gwo[...] = jnp.zeros_like(gwo)
        sm[...] = jnp.zeros_like(sm)

    wa = w // 4
    wl = w % 4
    first = wa * 576 + 2 * wl + 1
    second = wa * 576 + lax.rem(2 * wl + 2, 8)

    def window_of(ref):
        parts = []
        for half in range(2):
            rows = jnp.concatenate(
                [ref[half, pl.ds(first, 72, stride=8), :], ref[half, pl.ds(second, 72, stride=8), :]],
                axis=0,
            )
            parts.append(rows)
        return jnp.concatenate(parts, axis=1)[:, 0:WIDTH]

    x = window_of(xs)
    up = window_of(us)
    up_low = up.astype(bf16)
    cell = idc[pl.ds(pl.multiple_of(wa * 72, 8), 72), :]
    cell = jnp.concatenate([cell, cell], axis=0)
    embedded = jnp.where(
        cell < 1.5,
        jnp.where(cell < 0.5, ct_ref[0:1, :], ct_ref[1:2, :]),
        jnp.where(cell < 2.5, ct_ref[2:3, :], ct_ref[3:4, :]),
    )
    hidden = x + embedded
    centred = hidden - jnp.mean(hidden, axis=1, keepdims=True)
    inv_std = lax.rsqrt(jnp.mean(centred * centred, axis=1, keepdims=True) + NORM_EPS)
    normal_hat = centred * inv_std
    normed = (normal_hat * gain_ref[...] + nb_ref[...]).astype(bf16)

    query = (dot(normed, w_ref[0]) + bq_ref[0]).astype(bf16)
    key = (dot(normed, w_ref[1]) + bq_ref[1]).astype(bf16)
    value = (dot(normed, w_ref[2]) + bq_ref[2]).astype(bf16)
    grad_mixed = dot_nt(up_low, wo_ref[...]).astype(bf16)
    query_pairs = dot(rep[...], query).astype(bf16) * mask[...]
    grad_pairs = dot(rep[...], grad_mixed).astype(bf16) * mask[...]

    scores = dot_nt(key, query_pairs) * (SCALE * LOG2E) + b_ref[0]
    powers = jnp.exp2(scores - jnp.max(scores, axis=0, keepdims=True))
    attention = powers * (1.0 / jnp.sum(powers, axis=0, keepdims=True))
    attention_low = attention.astype(bf16)
    mixed_pairs = dot_tn(value, attention_low).astype(bf16) * maskt[...]
    mixed = dot(mixed_pairs, rep[...]).astype(bf16)
    gwo[...] += dot(mixed, up_low)
    grad_attention = dot_nt(value, grad_pairs)
    grad_value = dot(attention_low, grad_pairs)
    row_sum = jnp.sum(grad_attention * attention, axis=0, keepdims=True)
    grad_scores = attention * (grad_attention - row_sum)
    grad_scores_low = grad_scores.astype(bf16)
    grad_key = dot(grad_scores_low, query_pairs) * SCALE
    grad_query_pairs = (dot_tn(key, grad_scores_low) * SCALE).astype(bf16) * maskt[...]
    grad_query = dot_nt(rept[...], grad_query_pairs)
    for lu in range(2):
        turned = grad_scores[lu * 72 : (lu + 1) * 72, :].T
        turned = jnp.concatenate([turned, jnp.zeros((PAIRS, 56), f32)], axis=1)
        for i in range(12):
            fold[lu, i, pl.ds(w, 72, stride=8), :] = turned[i * 72 : (i + 1) * 72, :]

    grad_normed = jnp.zeros((WIN_TOKENS, WIDTH), f32)
    for part, grad in enumerate((grad_query, grad_key, grad_value)):
        sm[6 + part : 7 + part, :] += jnp.sum(grad, axis=0, keepdims=True)
        grad_low = grad.astype(bf16)
        gw[part] += dot_tn(normed, grad_low)
        grad_normed = grad_normed + dot_nt(grad_low, w_ref[part])

    scaled = grad_normed * gain_ref[...]
    scaled_mean = jnp.mean(scaled, axis=1, keepdims=True)
    hat_mean = jnp.mean(scaled * normal_hat, axis=1, keepdims=True)
    grad_hidden = up + inv_std * (scaled - scaled_mean - normal_hat * hat_mean)
    for k in range(CLASSES):
        picked = jnp.where(cell == float(k), grad_hidden, 0.0)
        sm[k : k + 1, :] += jnp.sum(picked, axis=0, keepdims=True)
    sm[4:5, :] += jnp.sum(grad_normed * normal_hat, axis=0, keepdims=True)
    sm[5:6, :] += jnp.sum(grad_normed, axis=0, keepdims=True)
    sm[9:10, :] += jnp.sum(up, axis=0, keepdims=True)
    for half in range(2):
        if half == 0:
            part = grad_hidden[:, 0:128]
        else:
            part = jnp.concatenate([grad_hidden[:, 128:192], jnp.zeros((WIN_TOKENS, 64), f32)], axis=1)
        os[half, pl.ds(first, 72, stride=8), :] = part[0:72]
        os[half, pl.ds(second, 72, stride=8), :] = part[72:144]

    @pl.when(w == 7)
    def _():
        for half in range(2):
            lanes = slice(0, 128) if half == 0 else slice(128, 192)
            width = 128 if half == 0 else 64
            for lat in range(12):
                at = lat * 96
                west, east = (own_ref, eo_ref) if lat < 9 else (so_ref, do_ref)
                to = (lat if lat < 9 else lat - 9) * 48
                west[to : to + 48, lanes] = os[half, at : at + 48, 0:width].astype(bf16)
                east[to : to + 48, lanes] = os[half, at + 48 : at + 96, 0:width].astype(bf16)
        srow = iota((256, 256), 0)
        scol = iota((256, 256), 1)
        row_hi = (srow >= 128).astype(jnp.int32)
        pos = srow - 128 * row_hi
        a_u = quotient(pos, 12)
        target = a_u * SPREAD - (pos - 12 * a_u) + 11 + row_hi
        target = jnp.where(pos < 72, target, -1000)
        tail = scol - 128
        tail = tail - 10 * quotient(tail, 10) + 128
        wanted = jnp.where(scol < 128, scol, jnp.where(scol < 218, tail, -1))
        mains = []
        tails = []
        for lu in range(2):
            acc = jnp.zeros((576, 256), f32)
            for ip in range(6):
                sums = jnp.where(target + 2 * ip == wanted, 1.0, 0.0).astype(bf16)
                both = jnp.concatenate([fold[lu, 2 * ip], fold[lu, 2 * ip + 1]], axis=1).astype(bf16)
                acc = acc + dot(both, sums)
            mains.append(acc[:, 0:128])
            tails.append(acc[:, 128:256])
        main = jnp.concatenate(mains, axis=0)
        tail = jnp.concatenate(tails, axis=0)
        for k in range(9):
            snd[pl.ds(k, 128, stride=SEND_ROWS), :] = main[k * 128 : (k + 1) * 128]
        lane = iota((128, 128), 1)
        slot = quotient(lane, 10)
        plane = jnp.zeros((128, 128), f32)
        for k in range(9):
            plane = jnp.where(slot == k, tail[k * 128 : (k + 1) * 128], plane)
        small = sm[...]
        small = jnp.concatenate(
            [
                jnp.zeros((96, 128), f32),
                small[:, 0:128],
                jnp.concatenate([small[:, 128:192], jnp.zeros((16, 64), f32)], axis=1),
            ],
            axis=0,
        )
        snd[pl.ds(9, 128, stride=SEND_ROWS), :] = jnp.where(lane < 96, plane, small.T)
        weights = jnp.concatenate([gw[0], gw[1], gw[2], gwo[...]], axis=1)
        weights = jnp.concatenate([weights[:, b * 128 : (b + 1) * 128] for b in range(6)], axis=0)
        for k in range(9):
            snd[pl.ds(10 + k, 128, stride=SEND_ROWS), :] = weights[k * 128 : (k + 1) * 128]
        for k in range(19, SEND_ROWS):
            snd[pl.ds(k, 128, stride=SEND_ROWS), :] = jnp.zeros((128, 128), f32)
        send_ref[...] = snd[...].astype(bf16)


def attend(x, u, east, south, diag, ids, ct, gain, nb, w3, bq, wo, bias):
    def whole(shape):
        return pl.BlockSpec(shape, lambda w: (0,) * len(shape))

    ins = [x, u, east, south, diag, ids, ct, gain, nb, w3, bq, wo]
    outs = [(432, WIDTH), (432, WIDTH), (144, WIDTH), (144, WIDTH), (128 * SEND_ROWS, 128)]
    return pl.pallas_call(
        window_kernel,
        grid=(8,),
        out_shape=[jax.ShapeDtypeStruct(o, bf16) for o in outs],
        in_specs=[whole(a.shape) for a in ins]
        + [pl.BlockSpec((1, WIN_TOKENS, PAIRS), lambda w: (w, 0, 0))],
        out_specs=[whole(o) for o in outs],
        scratch_shapes=[
            pltpu.VMEM((2, 1152, 128), f32),
            pltpu.VMEM((2, 1152, 128), f32),
            pltpu.VMEM((2, 1152, 128), f32),
            pltpu.VMEM((WIN_TOKENS, WIDTH), f32),
            pltpu.VMEM((PAIRS, WIN_TOKENS), bf16),
            pltpu.VMEM((WIN_TOKENS, PAIRS), bf16),
            pltpu.VMEM((PAIRS, WIDTH), bf16),
            pltpu.VMEM((WIDTH, PAIRS), bf16),
            pltpu.VMEM((2, 12, 576, 128), f32),
            pltpu.VMEM((3, WIDTH, WIDTH), f32),
            pltpu.VMEM((WIDTH, WIDTH), f32),
            pltpu.VMEM((16, WIDTH), f32),
            pltpu.VMEM((128 * SEND_ROWS, 128), f32),
        ],
        compiler_params=pltpu.CompilerParams(
            vmem_limit_bytes=VMEM, dimension_semantics=("arbitrary",)
        ),
        cost_estimate=pl.CostEstimate(flops=4 * 10**9, bytes_accessed=8 * 10**6, transcendentals=10**6),
        name="windows",
    )(*ins, bias)


def sum_kernel(root, in_ref, kinds_ref, out_ref):
    total = jnp.sum(in_ref[...].astype(f32).reshape(32, 4 * SEND_ROWS, 128), axis=0) * (1.0 / root)
    parts = [total[lat * SEND_ROWS : (lat + 1) * SEND_ROWS] for lat in range(4)]
    weights = (parts[0] + parts[1]) + (parts[2] + parts[3])
    lane = iota((1, 128), 1)
    tails = [jnp.where(lane < 96, p[9:10], weights[9:10]) for p in parts]
    rows = [p[0:9] for p in parts] + [weights[10:19]] + tails
    rows = rows + [kinds_ref[...], jnp.zeros((GATHER_ROWS - 50, 128), f32)]
    out_ref[...] = jnp.concatenate(rows, axis=0).astype(bf16)


def summed(received, kinds, root):
    def body(in_ref, kinds_ref, out_ref):
        sum_kernel(root, in_ref, kinds_ref, out_ref)

    return pl.pallas_call(
        body,
        out_shape=jax.ShapeDtypeStruct((GATHER_ROWS, 128), bf16),
        in_specs=[pl.BlockSpec(memory_space=pltpu.VMEM)] * 2,
        out_specs=pl.BlockSpec(memory_space=pltpu.VMEM),
        compiler_params=pltpu.CompilerParams(vmem_limit_bytes=VMEM),
        name="sums",
    )(received, kinds)


def spread_kernel(kinds_ref, in_ref, tab_ref, wqkv_ref, wo_ref, sm_ref, g, p):
    g[...] = in_ref[...].astype(f32)
    for lat in range(4):
        for w in range(8):
            kind = kinds_ref[lat * 8 + w]
            for q in range(16):
                src = (q * 8 + w) * GATHER_ROWS
                to = pl.multiple_of((q * 32 + kind) * 16, 16)
                p[pl.ds(to, 9), :] = g[src + lat * 9 : src + lat * 9 + 9, :]
                p[pl.ds(to + 9, 1), :] = g[src + 45 + lat : src + 46 + lat, :]
    for m in range(144):
        k, q = m // 16, m % 16
        lu, c = m // 72, m % 72
        la, h = c // 6, c % 6
        at = (((la // 6) * 2 + lu) * 6 + la % 6) * GROUP
        tab_ref[h, :, at : at + 128] = p[pl.ds(q * 512 + k, 32, stride=16), :]
        tail = p[pl.ds(q * 512 + 9, 32, stride=16), :]
        tab_ref[h, :, at + 128 : at + GROUP] = tail[:, k * 10 : k * 10 + 10]
    weights = jnp.concatenate(
        [g[pl.ds(36 + k, 128, stride=GATHER_ROWS), :] for k in range(9)], axis=0
    )
    weights = jnp.concatenate([weights[b * 192 : (b + 1) * 192] for b in range(6)], axis=1)
    wqkv_ref[...] = weights[:, 0:576]
    wo_ref[...] = weights[:, 576:768]
    small = g[pl.ds(45, 128, stride=GATHER_ROWS), :].T
    sm_ref[...] = jnp.concatenate([small[96:112], small[112:128]], axis=1)[:, 0:WIDTH]


def spread(gathered, kinds):
    return pl.pallas_call(
        spread_kernel,
        out_shape=[
            jax.ShapeDtypeStruct((HEADS, 32, POSITIONS), f32),
            jax.ShapeDtypeStruct((WIDTH, 3 * WIDTH), f32),
            jax.ShapeDtypeStruct((WIDTH, WIDTH), f32),
            jax.ShapeDtypeStruct((16, WIDTH), f32),
        ],
        in_specs=[
            pl.BlockSpec(memory_space=pltpu.SMEM),
            pl.BlockSpec(memory_space=pltpu.VMEM),
        ],
        out_specs=[pl.BlockSpec(memory_space=pltpu.VMEM)] * 4,
        scratch_shapes=[
            pltpu.VMEM((128 * GATHER_ROWS, 128), f32),
            pltpu.VMEM((16 * 32 * 16, 128), f32),
        ],
        compiler_params=pltpu.CompilerParams(vmem_limit_bytes=VMEM),
        name="spread",
    )(kinds, gathered)


def moved(array, lon_by, lat_by):
    lon, lat = lax.axis_size("lon"), lax.axis_size("lat")
    pairs = [
        (i * lat + j, ((i + lon_by) % lon) * lat + (j + lat_by) % lat)
        for i in range(lon)
        for j in range(lat)
    ]
    return lax.ppermute(array, BOTH, pairs)


def shards(
    inputs,
    upstream,
    land_ids,
    window_kinds,
    class_table,
    norm_gain,
    norm_bias,
    qkv_weight,
    qkv_bias,
    out_weight,
    bias_table,
):
    x = inputs[0].transpose(1, 2, 0, 3)
    u = upstream[0].transpose(1, 2, 0, 3)
    both = jnp.concatenate([x, u], axis=-1)
    ids = land_ids.astype(bf16)

    def frame_row(piece, before, after):
        row = jnp.pad(piece, (before, after)).reshape(1, WIN_TOKENS)
        return jnp.pad(row, ((0, 7), (0, 2 * WIDTH - WIN_TOKENS)))

    def packet(rows, row):
        return jnp.concatenate([rows.reshape(-1, 2 * WIDTH), row], axis=0)

    east = packet(both[3:12, 0:6], frame_row(ids[3:12, 0:6], (0, 3), (6, 0)))
    south = packet(both[0:3, 6:12], frame_row(ids[0:3, 6:12], (9, 0), (0, 6)))
    diag = packet(both[0:3, 0:6], frame_row(ids[0:3, 0:6], (9, 0), (6, 0)))
    east = moved(east, -1, 0)
    south = moved(south, 0, -1)
    diag = moved(diag, -1, -1)
    own_ids = frame_row(ids[3:12, 6:12], (0, 3), (0, 6)).astype(f32)

    last_lat = (lax.axis_index("lat") == lax.axis_size("lat") - 1).astype(jnp.int32)
    scal = jnp.concatenate([window_kinds, last_lat.reshape(1)])
    bias = expand_bias(bias_table.transpose(1, 0, 2), scal)

    own, east_out, south_out, diag_out, send = attend(
        x.reshape(1152, WIDTH),
        u.reshape(1152, WIDTH),
        east,
        south,
        diag,
        own_ids,
        class_table,
        norm_gain.reshape(1, WIDTH),
        norm_bias.reshape(1, WIDTH),
        qkv_weight.reshape(WIDTH, 3, WIDTH).transpose(1, 0, 2),
        qkv_bias.reshape(3, 1, WIDTH),
        out_weight,
        bias,
    )
    east_back = moved(east_out, 1, 0).reshape(9, 6, 8, WIDTH)
    south_back = moved(south_out, 0, 1).reshape(3, 6, 8, WIDTH)
    diag_back = moved(diag_out, 1, 1).reshape(3, 6, 8, WIDTH)
    own = own.reshape(9, 6, 8, WIDTH)

    root = math.sqrt(inputs.size // WIDTH * lax.axis_size("lon") * lax.axis_size("lat"))
    received = lax.all_to_all(send.reshape(128, SEND_ROWS, 128), BOTH, 0, 0)
    kinds_row = jnp.pad(window_kinds.astype(f32).reshape(1, 8), ((0, 0), (0, 120)))
    part = summed(received.reshape(128 * SEND_ROWS, 128), kinds_row, root)
    gathered = lax.all_to_all(
        jnp.broadcast_to(part, (128, GATHER_ROWS, 128)), BOTH, 0, 0
    )
    kinds = gathered[0:4, 49, 0:8].astype(jnp.int32).reshape(32)
    table, grad_wqkv, grad_wout, small = spread(gathered.reshape(128 * GATHER_ROWS, 128), kinds)

    grad_x = jnp.concatenate(
        [
            jnp.concatenate([diag_back, south_back], axis=1),
            jnp.concatenate([east_back, own], axis=1),
        ],
        axis=0,
    )
    return (
        grad_x.transpose(2, 0, 1, 3)[None],
        small[0:4],
        small[4],
        small[5],
        grad_wqkv,
        small[6:9].reshape(3 * WIDTH),
        grad_wout,
        small[9],
        table.transpose(1, 0, 2),
    )


def solution(mesh):
    placed = (
        P(None, None, "lat", "lon", None),
        P(None, None, "lat", "lon", None),
        P("lat", "lon"),
        P("lat"),
        P(),
        P(),
        P(),
        P(),
        P(),
        P(),
        P(),
    )
    return jax.shard_map(
        shards,
        mesh=mesh,
        in_specs=placed,
        out_specs=(P(None, None, "lat", "lon", None), P(), P(), P(), P(), P(), P(), P(), P()),
        check_vma=False,
    )
```

time: 589 us -> 134 us (0.23); the launches traced: 579 us -> 134 us
  local copies, waits for them, and re-layouts: 267 us -> 12.1 us
  matrix products: 97.2 us -> 0 us
  blocking collectives: 63 us -> 0 us
  Pallas kernels: 0 us -> 43.9 us
  waiting for transfers between devices: 85.1 us -> 44.3 us
  other arithmetic: 40 us -> 5.21 us
  starting transfers between devices: 12 us -> 27.3 us
  between operations: 15.1 us -> 0.82 us
    reshape x12 -> x7, local copies, waits for them, and re-layouts: 126 us -> 2.56 us  [the longest x1 0.89 us: shards(): qkv_weight.reshape(WIDTH, 3, WIDTH).transpose(1, 0, 2)]
    dot_general x16 -> x0, matrix products: 97.2 us -> none  [the longest x1 33 us: fold_bias(): jnp.einsum('nhpaiqbj,ijd->nhpqabd', shaped, offsets, precision=HIGHEST_PR...]
    another operation x4 -> x0, local copies, waits for them, and re-layouts: 96.9 us -> none  [the longest x2 95.2 us: fold_bias(): grad_rows.reshape(win_count, HEADS, WIN_LEVELS, WIN_LAT, WIN_LON, WIN_LEV...]
    psum x1 -> x0, waiting for transfers between devices: 66.8 us -> none  [shards(): lax.psum((grad_class, grad_gain, grad_shift_sum, grad_wqkv, grad_bqkv, gr...]
    psum x1 -> x0, blocking collectives: 63 us -> none  [shards(): lax.psum((grad_class, grad_gain, grad_shift_sum, grad_wqkv, grad_bqkv, gr...]
    pallas_call x0 -> x4, Pallas kernels: none -> 43.9 us  [the longest x1 29 us: attend(): pl.pallas_call(window_kernel, grid=(8,), out_shape=[jax.ShapeDtypeStruct(...]
    convert_element_type x5 -> x1, local copies, waits for them, and re-layouts: 22.9 us -> 0.7 us  [shards(): kinds = gathered[0:4, 49, 0:8].astype(jnp.int32).reshape(32)]
    all_to_all x0 -> x2, waiting for transfers between devices: none -> 15.7 us  [the longest x1 15.7 us: shards(): received = lax.all_to_all(send.reshape(128, SEND_ROWS, 128), BOTH, 0, 0)]
  transfers between devices with their start and end apart: 5 -> 8, of which waited for: 2 -> 2; matrix products, arithmetic and copies ran while one was open for 45% -> 5% of each run, Pallas kernels for 0% -> 6%
where the time goes in v1:
time: 134 us
  waiting for transfers between devices  44.3 us (33%)
  Pallas kernels  43.9 us (33%)
  starting transfers between devices  27.3 us (20%)
  local copies, waits for them, and re-layouts  12.1 us (9%)
  other arithmetic  5.21 us (4%)
    pallas_call x1, Pallas kernels, attend(): pl.pallas_call(window_kernel, grid=(8,), out_shape=[jax.ShapeDtypeStruct(...  29 us
    ppermute x6, waiting for transfers between devices, moved(): return lax.ppermute(array, BOTH, pairs)  28.6 us
    ppermute x6, starting transfers between devices, moved(): return lax.ppermute(array, BOTH, pairs)  17.3 us
    all_to_all x1, waiting for transfers between devices, shards(): received = lax.all_to_all(send.reshape(128, SEND_ROWS, 128), BOTH, 0, 0)  15.7 us
    pallas_call x1, Pallas kernels, expand_bias(): pl.pallas_call(bias_kernel, out_shape=jax.ShapeDtypeStruct((8, WIN_TOKENS...  7.55 us
    pallas_call x1, Pallas kernels, spread(): pl.pallas_call(spread_kernel, out_shape=[jax.ShapeDtypeStruct((HEADS, 32,...  5.42 us
    all_to_all x1, starting transfers between devices, shards(): received = lax.all_to_all(send.reshape(128, SEND_ROWS, 128), BOTH, 0, 0)  5.41 us
    all_to_all x1, starting transfers between devices, shards(): lax.all_to_all(jnp.broadcast_to(part, (128, GATHER_ROWS, 128)), BOTH, 0, 0)  4.53 us
  transfers between devices with their start and end apart: 8, of which 2 were waited for; matrix products, arithmetic and copies ran while one was open for 5% of the time, Pallas kernels for 6%

profile of v1, /device:TPU:1, one launch (start us, length us, event | category | flops | bytes accessed | tf_op | source)
XLA Modules:
  0.0 133.6 jit_solution(1629709402244217816)
XLA Ops:
  0.7 0.7 convert_element_type.32
  1.5 1.1 pad_maximum_fusion
  2.7 1.5 %collective-permute-start.1 = (bf16[152,384]{1,0:T(8,128)(2,1)S(1)}, bf16[152,384]{1,0:T(8,128)(2,1)S(1)}, u32[]{:S(2)}, u32[]{:S(2)}) collective-permute-start(bf16[152,384]{1,0:T(8,128)(2,1)S(1)} %fusion.5), channel_id=1, source_target_pairs={{0,3},{1,0},{2,1},{3,2},{4,7},{5,4},{6,5},{7,6},{8,11},{9,8},{10,9... | collective-permute-start | bytes 350216 | tf_op jit(solution)/shard_map/ppermute | solution.py:463
  4.4 8.7 %collective-permute-start.2 = (bf16[152,384]{1,0:T(8,128)(2,1)S(1)}, bf16[152,384]{1,0:T(8,128)(2,1)S(1)}, u32[]{:S(2)}, u32[]{:S(2)}) collective-permute-start(bf16[152,384]{1,0:T(8,128)(2,1)S(1)} %fusion.6), channel_id=1, source_target_pairs={{0,127},{1,124},{2,125},{3,126},{4,3},{5,0},{6,1},{7,2},{8,7},{9,4... | collective-permute-start | bytes 350216 | tf_op jit(solution)/shard_map/ppermute | solution.py:463
  13.1 1.2 fusion.2
  14.6 1.2 collective-permute-start
  15.8 0.6 pad_add_fusion.scal_ref
  16.4 7.6 %bias.1.b_ref = f32[8,144,864]{2,1,0:T(8,128)} custom-call(s32[9]{0:T(128)} %pad_add_fusion.scal_ref, f32[6,32,3312]{2,1,0:T(8,128)} %bitcast.57), custom_call_target="tpu_custom_call" | custom-call | flops 2000000000 | bytes 7000000 | tf_op jit(solution)/shard_map/bias/pallas_call | solution.py:100
  24.2 0.9 copy.25
  25.1 0.7 reshape.106.bq_ref
  25.8 0.6 pad_convert_fusion.ids_ref
  26.4 0.6 copy-done.7
  27.2 29.0 %windows.1 = (bf16[432,192]{1,0:T(8,128)(2,1)}, bf16[432,192]{1,0:T(8,128)(2,1)}, bf16[144,192]{1,0:T(8,128)(2,1)}, bf16[144,192]{1,0:T(8,128)(2,1)}, bf16[3072,128]{1,0:T(8,128)(2,1)}) custom-call(bf16[1152,192]{1,0:T(8,128)(2,1)} %bitcast.40, bf16[1152,192]{1,0:T(8,128)(2,1)} %bitcast.43, bf16[440,384]{1,0:T(8,128)(2,1)} %copy-done.5, ...), custom_call_target="tpu_custom_call" | custom-call | flops 4000000000 | bytes 8000000 | tf_op jit(solution)/shard_map/windows/pallas_call | solution.py:350
  56.2 5.4 %all-to-all-start = ((bf16[128,24,128]{2,1,0:T(8,128)(2,1)}), bf16[128,24,128]{2,1,0:T(8,128)(2,1)S(1)}, u32[]{:S(2)}, u32[]{:S(2)}) async-start(bf16[128,24,128]{2,1,0:T(8,128)(2,1)} %bitcast.46), calls=%async_computation | async-start | bytes 1572864 | tf_op jit(solution)/shard_map/all_to_all | solution.py:524
  61.6 0.5 pad.41.kinds_ref
  62.1 15.7 %all-to-all-done = bf16[128,24,128]{2,1,0:T(8,128)(2,1)S(1)} async-done(((bf16[128,24,128]{2,1,0:T(8,128)(2,1)}), bf16[128,24,128]{2,1,0:T(8,128)(2,1)S(1)}, u32[]{:S(2)}, u32[]{:S(2)}) %all-to-all-start) | async-done | bytes 786464 | tf_op jit(solution)/shard_map/all_to_all | solution.py:524
  77.9 0.9 copy-done.1
  78.8 1.9 %sums.1 = bf16[56,128]{1,0:T(8,128)(2,1)} custom-call(bf16[3072,128]{1,0:T(8,128)(2,1)} %bitcast.37, f32[1,128]{1,0:T(1,128)} %pad.41.kinds_ref), custom_call_target="tpu_custom_call" | custom-call | tf_op jit(solution)/shard_map/sums/pallas_call | solution.py:395
  80.6 2.2 %broadcast_in_dim.7 = bf16[128,56,128]{2,1,0:T(8,128)(2,1)} broadcast(bf16[56,128]{1,0:T(8,128)(2,1)} %sums.1), dimensions={1,2} | broadcast | bytes 1849344 | tf_op jit(solution)/shard_map/broadcast_in_dim | solution.py:528
  82.9 4.5 %all-to-all-start.1 = ((bf16[128,56,128]{2,1,0:T(8,128)(2,1)}), bf16[128,56,128]{2,1,0:T(8,128)(2,1)S(1)}, u32[]{:S(2)}, u32[]{:S(2)}) async-start(bf16[128,56,128]{2,1,0:T(8,128)(2,1)} %broadcast_in_dim.7), calls=%async_computation.1 | async-start | bytes 3670016 | tf_op jit(solution)/shard_map/all_to_all | solution.py:527
  87.4 1.5 %collective-permute-start.5 = (bf16[432,192]{1,0:T(8,128)(2,1)S(1)}, bf16[432,192]{1,0:T(8,128)(2,1)S(1)}, u32[]{:S(2)}, u32[]{:S(2)}) collective-permute-start(bf16[432,192]{1,0:T(8,128)(2,1)S(1)} %copy-done.6), channel_id=1, source_target_pairs={{0,4},{1,5},{2,6},{3,7},{4,8},{5,9},{6,10},{7,11},{8,12},{9,13},{1... | collective-permute-start | bytes 497672 | tf_op jit(solution)/shard_map/ppermute | solution.py:463
  88.9 3.5 %collective-permute-start.3 = (bf16[144,192]{1,0:T(8,128)(2,1)S(1)}, bf16[144,192]{1,0:T(8,128)(2,1)S(1)}, u32[]{:S(2)}, u32[]{:S(2)}) collective-permute-start(bf16[144,192]{1,0:T(8,128)(2,1)S(1)} %copy-done.10), channel_id=1, source_target_pairs={{0,5},{1,6},{2,7},{3,4},{4,9},{5,10},{6,11},{7,8},{8,13},{9,14},{1... | collective-permute-start | bytes 165896 | tf_op jit(solution)/shard_map/ppermute | solution.py:463
  92.4 0.9 collective-permute-start.4
  93.3 28.6 %collective-permute-done.3 = bf16[144,192]{1,0:T(8,128)(2,1)S(1)} collective-permute-done((bf16[144,192]{1,0:T(8,128)(2,1)S(1)}, bf16[144,192]{1,0:T(8,128)(2,1)S(1)}, u32[]{:S(2)}, u32[]{:S(2)}) %collective-permute-start.3) | collective-permute-done | bytes 55328 | tf_op jit(solution)/shard_map/ppermute | solution.py:463
  121.9 0.9 maximum_bitcast_fusion
  122.9 0.7 reshape.120.kinds_ref
  123.6 0.5 copy-done
  124.1 5.4 %spread.1 = (f32[6,32,3312]{2,1,0:T(8,128)}, f32[192,576]{1,0:T(8,128)}, f32[192,192]{1,0:T(8,128)}, f32[16,192]{1,0:T(8,128)}) custom-call(s32[32]{0:T(128)} %reshape.120.kinds_ref, bf16[7168,128]{1,0:T(8,128)(2,1)} %bitcast.36), custom_call_target="tpu_custom_call" | custom-call | tf_op jit(solution)/shard_map/spread/pallas_call | solution.py:434
  129.6 1.3 %fusion.9 = (f32[1,192]{1,0:T(1,128)}, f32[1,192]{1,0:T(1,128)}, f32[1,192]{1,0:T(1,128)}) fusion(f32[16,192]{1,0:T(8,128)} %get-tuple-element.23), kind=kLoop, calls=%fused_computation.21 | loop fusion | bytes 4608 | tf_op jit(solution)/shard_map/slice | solution.py:548
  130.9 0.7 slice.50
  131.6 1.3 slice.47
  132.9 0.7 reshape.117
  (43 shorter events, 1.1 us)
Async XLA Ops:
  0.6 15.2 %copy-start.11 = (s32[8]{0:T(128)S(1)}, s32[8]{0:T(128)}, u32[]{:S(2)}) copy-start(s32[8]{0:T(128)} %param.14) | copy-start | bytes 100
  2.7 23.7 %collective-permute-start.1 = (bf16[152,384]{1,0:T(8,128)(2,1)S(1)}, bf16[152,384]{1,0:T(8,128)(2,1)S(1)}, u32[]{:S(2)}, u32[]{:S(2)}) collective-permute-start(bf16[152,384]{1,0:T(8,128)(2,1)S(1)} %fusion.5), channel_id=1, source_target_pairs={{0,3},{1,0},{2,1},{3,2},{4,7},{5,4},{6,5},{7,6},{8,11},{9,8},{10,9... | collective-permute-start | bytes 350216 | tf_op jit(solution)/shard_map/ppermute | solution.py:463
  4.4 22.0 %collective-permute-start.2 = (bf16[152,384]{1,0:T(8,128)(2,1)S(1)}, bf16[152,384]{1,0:T(8,128)(2,1)S(1)}, u32[]{:S(2)}, u32[]{:S(2)}) collective-permute-start(bf16[152,384]{1,0:T(8,128)(2,1)S(1)} %fusion.6), channel_id=1, source_target_pairs={{0,127},{1,124},{2,125},{3,126},{4,3},{5,0},{6,1},{7,2},{8,7},{9,4... | collective-permute-start | bytes 350216 | tf_op jit(solution)/shard_map/ppermute | solution.py:463
  14.6 11.8 %collective-permute-start = (bf16[440,384]{1,0:T(8,128)(2,1)S(1)}, bf16[440,384]{1,0:T(8,128)(2,1)S(1)}, u32[]{:S(2)}, u32[]{:S(2)}) collective-permute-start(bf16[440,384]{1,0:T(8,128)(2,1)S(1)} %fusion.1), channel_id=1, source_target_pairs={{0,124},{1,125},{2,126},{3,127},{4,0},{5,1},{6,2},{7,3},{8,4},{9,5... | collective-permute-start | bytes 1013768 | tf_op jit(solution)/shard_map/ppermute | solution.py:463
  16.4 7.7 %copy-start.2 = (bf16[192,576]{1,0:T(8,128)(2,1)S(1)}, bf16[192,576]{1,0:T(8,128)(2,1)}, u32[]{:S(2)}) copy-start(bf16[192,576]{1,0:T(8,128)(2,1)} %param.18) | copy-start | bytes 663556
  16.4 8.7 %copy-start.4 = (f32[576]{0:T(1024)S(1)}, f32[576]{0:T(1024)}, u32[]{:S(2)}) copy-start(f32[576]{0:T(1024)} %param.19) | copy-start | bytes 6916
  26.4 0.6 copy-start.7
  26.4 0.7 copy-start.8
  26.4 0.8 copy-start.5
  56.2 21.7 %all-to-all-start = ((bf16[128,24,128]{2,1,0:T(8,128)(2,1)}), bf16[128,24,128]{2,1,0:T(8,128)(2,1)S(1)}, u32[]{:S(2)}, u32[]{:S(2)}) async-start(bf16[128,24,128]{2,1,0:T(8,128)(2,1)} %bitcast.46), calls=%async_computation | async-start | bytes 1572864 | tf_op jit(solution)/shard_map/all_to_all | solution.py:524
  77.9 0.9 copy-start.1
  80.6 6.8 %copy-start.6 = (bf16[432,192]{1,0:T(8,128)(2,1)S(1)}, bf16[432,192]{1,0:T(8,128)(2,1)}, u32[]{:S(2)}) copy-start(bf16[432,192]{1,0:T(8,128)(2,1)} %get-tuple-element.20) | copy-start | bytes 497668
  80.6 8.3 %copy-start.10 = (bf16[144,192]{1,0:T(8,128)(2,1)S(1)}, bf16[144,192]{1,0:T(8,128)(2,1)}, u32[]{:S(2)}) copy-start(bf16[144,192]{1,0:T(8,128)(2,1)} %get-tuple-element.18) | copy-start | bytes 165892
  80.6 11.8 %copy-start.9 = (bf16[144,192]{1,0:T(8,128)(2,1)S(1)}, bf16[144,192]{1,0:T(8,128)(2,1)}, u32[]{:S(2)}) copy-start(bf16[144,192]{1,0:T(8,128)(2,1)} %get-tuple-element.19) | copy-start | bytes 165892
  80.6 41.3 %copy-start.3 = (bf16[432,192]{1,0:T(8,128)(2,1)S(1)}, bf16[432,192]{1,0:T(8,128)(2,1)}, u32[]{:S(2)}) copy-start(bf16[432,192]{1,0:T(8,128)(2,1)} %get-tuple-element.21) | copy-start | bytes 497668
  82.9 40.0 %all-to-all-start.1 = ((bf16[128,56,128]{2,1,0:T(8,128)(2,1)}), bf16[128,56,128]{2,1,0:T(8,128)(2,1)S(1)}, u32[]{:S(2)}, u32[]{:S(2)}) async-start(bf16[128,56,128]{2,1,0:T(8,128)(2,1)} %broadcast_in_dim.7), calls=%async_computation.1 | async-start | bytes 3670016 | tf_op jit(solution)/shard_map/all_to_all | solution.py:527
  87.4 34.5 %collective-permute-start.5 = (bf16[432,192]{1,0:T(8,128)(2,1)S(1)}, bf16[432,192]{1,0:T(8,128)(2,1)S(1)}, u32[]{:S(2)}, u32[]{:S(2)}) collective-permute-start(bf16[432,192]{1,0:T(8,128)(2,1)S(1)} %copy-done.6), channel_id=1, source_target_pairs={{0,4},{1,5},{2,6},{3,7},{4,8},{5,9},{6,10},{7,11},{8,12},{9,13},{1... | collective-permute-start | bytes 497672 | tf_op jit(solution)/shard_map/ppermute | solution.py:463
  88.9 33.0 %collective-permute-start.3 = (bf16[144,192]{1,0:T(8,128)(2,1)S(1)}, bf16[144,192]{1,0:T(8,128)(2,1)S(1)}, u32[]{:S(2)}, u32[]{:S(2)}) collective-permute-start(bf16[144,192]{1,0:T(8,128)(2,1)S(1)} %copy-done.10), channel_id=1, source_target_pairs={{0,5},{1,6},{2,7},{3,4},{4,9},{5,10},{6,11},{7,8},{8,13},{9,14},{1... | collective-permute-start | bytes 165896 | tf_op jit(solution)/shard_map/ppermute | solution.py:463
  92.4 29.5 %collective-permute-start.4 = (bf16[144,192]{1,0:T(8,128)(2,1)S(1)}, bf16[144,192]{1,0:T(8,128)(2,1)S(1)}, u32[]{:S(2)}, u32[]{:S(2)}) collective-permute-start(bf16[144,192]{1,0:T(8,128)(2,1)S(1)} %copy-done.9), channel_id=1, source_target_pairs={{0,1},{1,2},{2,3},{3,0},{4,5},{5,6},{6,7},{7,4},{8,9},{9,10},{10,1... | collective-permute-start | bytes 165896 | tf_op jit(solution)/shard_map/ppermute | solution.py:463
  122.9 1.3 copy-start

commit v2 on v1

v2 whole, which is shorter than its diff:
```python
import math

import jax
import jax.numpy as jnp
import numpy as np
from jax import lax
from jax.experimental import pallas as pl
from jax.experimental.pallas import tpu as pltpu
from jax.sharding import PartitionSpec as P

WIDTH = 192
HEADS = 6
HEAD_DIM = 32
CLASSES = 4
WIN_TOKENS = 144
POSITIONS = 3312
SPREAD = 23
GROUP = 138
PAIRS = 864
MASKED_SCORE = -1000000000.0
NORM_EPS = 1e-05
LOG2E = 1.4426950408889634
SCALE = HEAD_DIM ** (-0.5)
VMEM = 56 * 1024 * 1024
SEND_ROWS = 24
GATHER_ROWS = 48
BOTH = ("lon", "lat")
PER_STEP = 2

f32 = jnp.float32
bf16 = jnp.bfloat16


def dot(a, b):
    return lax.dot_general(a, b, (((1,), (0,)), ((), ())), preferred_element_type=f32)


def dot_nt(a, b):
    return lax.dot_general(a, b, (((1,), (1,)), ((), ())), preferred_element_type=f32)


def dot_tn(a, b):
    return lax.dot_general(a, b, (((0,), (0,)), ((), ())), preferred_element_type=f32)


def iota(shape, axis):
    return lax.broadcasted_iota(jnp.int32, shape, axis)


def quotient(a, b):
    return jnp.floor((a.astype(f32) + 0.5) * (1.0 / b)).astype(jnp.int32)


def bias_kernel(scal_ref, tab_ref, out_ref, sel_ref, t_ref, e_ref):
    for w in range(8):
        kind = scal_ref[w]
        for h in range(HEADS):
            sel_ref[h, w : w + 1, 0:POSITIONS] = tab_ref[h, pl.ds(kind, 1), :]
    last_lat = scal_ref[8]
    for lu in range(2):
        for lt in range(2):
            for a in range(6):
                g = (lt * 2 + lu) * 6 + a
                for h in range(HEADS):
                    at = h * 12 + lt * 6 + a
                    piece = sel_ref[h, :, g * GROUP : g * GROUP + 256]
                    t_ref[lu, 0, pl.ds(at, 8, stride=72), :] = piece[:, 0:128]
                    t_ref[lu, 1, pl.ds(at, 8, stride=72), :] = piece[:, 128:256]
    row = iota((576, GROUP), 0)
    lane = iota((576, GROUP), 1)
    win = quotient(row, 72)
    la = row - 12 * quotient(row, 12)
    late = (la >= 6).astype(jnp.int32)
    low_lat = ((la - 6 * late) < 3).astype(jnp.int32)
    low_key = (lane < 3 * SPREAD).astype(jnp.int32)
    cut_lat = jnp.where(win >= 4, last_lat, 0) * (low_lat ^ low_key)
    cut_lev = ((win & 3) == 3).astype(jnp.int32)
    srow = iota((GROUP, 256), 0)
    scol = iota((GROUP, 256), 1)
    col_hi = (scol >= 128).astype(jnp.int32)
    col = scol - 128 * col_hi
    a_u = quotient(col, 12)
    base = a_u * SPREAD - (col - 12 * a_u) + 11
    base = jnp.where(col < 72, base + col_hi, -1000)
    for lu in range(2):
        cut = cut_lat + cut_lev * (late if lu == 0 else 1 - late)
        t = jnp.concatenate([t_ref[lu, 0], t_ref[lu, 1]], axis=1)[:, 0:GROUP]
        t = jnp.where(cut > 0, MASKED_SCORE, t * LOG2E)
        hi = t.astype(bf16)
        rest = t - hi.astype(f32)
        mid = rest.astype(bf16)
        low = (rest - mid.astype(f32)).astype(bf16)
        for ip in range(6):
            spread = jnp.where(srow == base + 2 * ip, 1.0, 0.0).astype(bf16)
            acc = dot(hi, spread) + dot(mid, spread) + dot(low, spread)
            e_ref[pl.ds(2 * ip, 576, stride=12), :] = acc[:, 0:128]
            e_ref[pl.ds(2 * ip + 1, 576, stride=12), :] = acc[:, 128:256]
        for w in range(8):
            for h in range(HEADS):
                at = (w * HEADS + h) * WIN_TOKENS
                turned = e_ref[at : at + WIN_TOKENS, :].T
                to = h * WIN_TOKENS + lu * 72
                out_ref[w, to : to + 72, :] = turned[0:72, :]


def expand_bias(table, scal):
    return pl.pallas_call(
        bias_kernel,
        out_shape=jax.ShapeDtypeStruct((8, PAIRS, WIN_TOKENS), f32),
        in_specs=[
            pl.BlockSpec(memory_space=pltpu.SMEM),
            pl.BlockSpec(memory_space=pltpu.VMEM),
        ],
        out_specs=pl.BlockSpec(memory_space=pltpu.VMEM),
        scratch_shapes=[
            pltpu.VMEM((HEADS, 8, 3456), f32),
            pltpu.VMEM((2, 2, 576, 128), f32),
            pltpu.VMEM((8 * PAIRS, 128), f32),
        ],
        compiler_params=pltpu.CompilerParams(vmem_limit_bytes=VMEM),
        cost_estimate=pl.CostEstimate(flops=2 * 10**9, bytes_accessed=7 * 10**6, transcendentals=0),
        name="bias",
    )(scal, table)


def window_kernel(
    x_ref,
    u_ref,
    e_ref,
    s_ref,
    d_ref,
    ids_ref,
    ct_ref,
    gain_ref,
    nb_ref,
    w_ref,
    bq_ref,
    wo_ref,
    b_ref,
    own_ref,
    eo_ref,
    so_ref,
    do_ref,
    send_ref,
    xs,
    us,
    os,
    idc,
    w3,
    mask,
    fold,
    gw,
    gwo,
    sm,
    folded,
    snd,
):
    step = pl.program_id(0)

    @pl.when(step == 0)
    def _():
        for half in range(2):
            lanes = slice(0, 128) if half == 0 else slice(128, 192)
            far = slice(192, 320) if half == 0 else slice(320, 384)
            width = 128 if half == 0 else 64
            for lat in range(12):
                at = lat * 96
                if lat < 9:
                    src = (lat + 3) * 96 + 48
                    xs[half, at : at + 48, 0:width] = x_ref[src : src + 48, lanes].astype(f32)
                    us[half, at : at + 48, 0:width] = u_ref[src : src + 48, lanes].astype(f32)
                    east, esrc = e_ref, lat * 48
                else:
                    src = (lat - 9) * 48
                    xs[half, at : at + 48, 0:width] = s_ref[src : src + 48, lanes].astype(f32)
                    us[half, at : at + 48, 0:width] = s_ref[src : src + 48, far].astype(f32)
                    east, esrc = d_ref, (lat - 9) * 48
                xs[half, at + 48 : at + 96, 0:width] = east[esrc : esrc + 48, lanes].astype(f32)
                us[half, at + 48 : at + 96, 0:width] = east[esrc : esrc + 48, far].astype(f32)
        id_row = (
            ids_ref[0:1, 0:WIN_TOKENS]
            + e_ref[432:440, 0:WIN_TOKENS].astype(f32)[0:1]
            + s_ref[144:152, 0:WIN_TOKENS].astype(f32)[0:1]
            + d_ref[144:152, 0:WIN_TOKENS].astype(f32)[0:1]
        )
        same = iota((WIN_TOKENS, WIN_TOKENS), 0) == iota((WIN_TOKENS, WIN_TOKENS), 1)
        column = jnp.sum(jnp.where(same, id_row, 0.0), axis=1, keepdims=True)
        idc[...] = jnp.broadcast_to(column, (WIN_TOKENS, WIDTH))
        head = quotient(iota((PAIRS, WIDTH), 0), WIN_TOKENS)
        mask[...] = jnp.where(head == (iota((PAIRS, WIDTH), 1) >> 5), 1.0, 0.0).astype(bf16)
        for part in range(3):
            w3[part] = w_ref[:, part * WIDTH : (part + 1) * WIDTH]
        gw[...] = jnp.zeros_like(gw)
        gwo[...] = jnp.zeros_like(gwo)
        sm[...] = jnp.zeros_like(sm)

    for sub in range(PER_STEP):
        w = step * PER_STEP + sub
        wa = w // 4
        wl = w % 4
        first = wa * 576 + 2 * wl + 1
        second = wa * 576 + lax.rem(2 * wl + 2, 8)

        def window_of(ref):
            parts = []
            for half in range(2):
                rows = jnp.concatenate(
                    [ref[half, pl.ds(first, 72, stride=8), :], ref[half, pl.ds(second, 72, stride=8), :]],
                    axis=0,
                )
                parts.append(rows)
            return jnp.concatenate(parts, axis=1)[:, 0:WIDTH]

        x = window_of(xs)
        up = window_of(us)
        up_low = up.astype(bf16)
        cell = idc[pl.ds(pl.multiple_of(wa * 72, 8), 72), :]
        cell = jnp.concatenate([cell, cell], axis=0)
        embedded = jnp.where(
            cell < 1.5,
            jnp.where(cell < 0.5, ct_ref[0:1, :], ct_ref[1:2, :]),
            jnp.where(cell < 2.5, ct_ref[2:3, :], ct_ref[3:4, :]),
        )
        hidden = x + embedded
        centred = hidden - jnp.mean(hidden, axis=1, keepdims=True)
        inv_std = lax.rsqrt(jnp.mean(centred * centred, axis=1, keepdims=True) + NORM_EPS)
        normal_hat = centred * inv_std
        normed = (normal_hat * gain_ref[...] + nb_ref[...]).astype(bf16)

        query = (dot(normed, w3[0]) + bq_ref[:, 0:192]).astype(bf16)
        key = dot(normed, w3[1]) + bq_ref[:, 192:384]
        value = dot(normed, w3[2]) + bq_ref[:, 384:576]
        key_turned, value_turned = key.T.astype(bf16), value.T.astype(bf16)
        key_heads = jnp.concatenate([key.astype(bf16)] * HEADS, axis=0) * mask[...]
        value_heads = jnp.concatenate([value.astype(bf16)] * HEADS, axis=0) * mask[...]
        grad_mixed = dot_nt(up_low, wo_ref[...]).astype(bf16)

        def heads_of(a):
            return a.reshape(HEADS, WIN_TOKENS, WIN_TOKENS)

        def by_head(turned, pairs):
            parts = [
                dot(turned[h * 32 : h * 32 + 32], pairs[h * WIN_TOKENS : (h + 1) * WIN_TOKENS])
                for h in range(HEADS)
            ]
            return jnp.concatenate(parts, axis=0)

        def own_head(wide):
            lane = iota((WIN_TOKENS, WIDTH), 1)
            picked = wide[0:WIN_TOKENS]
            for h in range(1, HEADS):
                picked = jnp.where(lane >= 32 * h, wide[h * WIN_TOKENS : (h + 1) * WIN_TOKENS], picked)
            return picked

        scores = heads_of(dot_nt(key_heads, query) * (SCALE * LOG2E) + b_ref[sub])
        powers = jnp.exp2(scores - jnp.max(scores, axis=1, keepdims=True))
        attention = powers * (1.0 / jnp.sum(powers, axis=1, keepdims=True))
        attention_low = attention.astype(bf16).reshape(PAIRS, WIN_TOKENS)
        mixed = by_head(value_turned, attention_low).astype(bf16)
        gwo[...] += dot(mixed, up_low)
        grad_attention = heads_of(dot_nt(value_heads, grad_mixed))
        grad_value = own_head(dot(attention_low, grad_mixed))
        row_sum = jnp.sum(grad_attention * attention, axis=1, keepdims=True)
        grad_scores = attention * (grad_attention - row_sum)
        grad_scores_low = grad_scores.astype(bf16).reshape(PAIRS, WIN_TOKENS)
        grad_key = own_head(dot(grad_scores_low, query)) * SCALE
        grad_query = (by_head(key_turned, grad_scores_low) * SCALE).T
        for h in range(HEADS):
            at = pl.multiple_of((w * HEADS + h) * WIN_TOKENS, WIN_TOKENS)
            for lu in range(2):
                fold[lu, pl.ds(at, WIN_TOKENS), :] = grad_scores[h, lu * 16 : lu * 16 + 128, :].T

        normed_turned = normed.T
        grad_normed = jnp.zeros((WIN_TOKENS, WIDTH), f32)
        for part, grad in enumerate((grad_query, grad_key, grad_value)):
            sm[6 + part : 7 + part, :] += jnp.sum(grad, axis=0, keepdims=True)
            grad_low = grad.astype(bf16)
            gw[part] += dot(normed_turned, grad_low)
            grad_normed = grad_normed + dot_nt(grad_low, w3[part])

        scaled = grad_normed * gain_ref[...]
        scaled_mean = jnp.mean(scaled, axis=1, keepdims=True)
        hat_mean = jnp.mean(scaled * normal_hat, axis=1, keepdims=True)
        grad_hidden = up + inv_std * (scaled - scaled_mean - normal_hat * hat_mean)
        for k in range(CLASSES):
            picked = jnp.where(cell == float(k), grad_hidden, 0.0)
            sm[k : k + 1, :] += jnp.sum(picked, axis=0, keepdims=True)
        sm[4:5, :] += jnp.sum(grad_normed * normal_hat, axis=0, keepdims=True)
        sm[5:6, :] += jnp.sum(grad_normed, axis=0, keepdims=True)
        sm[9:10, :] += jnp.sum(up, axis=0, keepdims=True)
        for half in range(2):
            if half == 0:
                part = grad_hidden[:, 0:128]
            else:
                part = jnp.concatenate([grad_hidden[:, 128:192], jnp.zeros((WIN_TOKENS, 64), f32)], axis=1)
            os[half, pl.ds(first, 72, stride=8), :] = part[0:72]
            os[half, pl.ds(second, 72, stride=8), :] = part[72:144]

    @pl.when(step == 8 // PER_STEP - 1)
    def _():
        for half in range(2):
            lanes = slice(0, 128) if half == 0 else slice(128, 192)
            width = 128 if half == 0 else 64
            for lat in range(12):
                at = lat * 96
                west, east = (own_ref, eo_ref) if lat < 9 else (so_ref, do_ref)
                to = (lat if lat < 9 else lat - 9) * 48
                west[to : to + 48, lanes] = os[half, at : at + 48, 0:width].astype(bf16)
                east[to : to + 48, lanes] = os[half, at + 48 : at + 96, 0:width].astype(bf16)
        srow = iota((256, 256), 0)
        scol = iota((256, 256), 1)
        row_hi = (srow >= 128).astype(jnp.int32)
        pos = srow - 128 * row_hi
        tail = scol - 128
        tail = tail - 10 * quotient(tail, 10) + 128
        wanted = jnp.where(scol < 128, scol, jnp.where(scol < 218, tail, -1))
        for lu in range(2):
            key_at = pos - 56 * lu
            a_u = quotient(key_at, 12)
            target = a_u * SPREAD - (key_at - 12 * a_u) + 11 + row_hi
            target = jnp.where((key_at >= 0) & (key_at < 72), target, -1000)
            acc = jnp.zeros((576, 256), f32)
            for ip in range(6):
                sums = jnp.where(target + 2 * ip == wanted, 1.0, 0.0).astype(bf16)
                both = jnp.concatenate(
                    [fold[lu, pl.ds(2 * ip + i, 576, stride=12), :] for i in range(2)], axis=1
                ).astype(bf16)
                acc = acc + dot(both, sums)
            for at in range(8):
                rows = acc[at * 72 : (at + 1) * 72]
                folded[0, pl.ds(lu * 576 + at, 72, stride=8), :] = rows[:, 0:128]
                folded[1, pl.ds(lu * 576 + at, 72, stride=8), :] = rows[:, 128:256]

        def put(k, plane):
            for core in range(2):
                rows = pl.ds(core * SEND_ROWS + k, 64, stride=2 * SEND_ROWS)
                snd[rows, :] = plane[core * 64 : (core + 1) * 64]

        for k in range(9):
            put(k, folded[0, k * 128 : (k + 1) * 128])
        lane = iota((128, 128), 1)
        slot = quotient(lane, 10)
        plane = jnp.zeros((128, 128), f32)
        for k in range(9):
            plane = jnp.where(slot == k, folded[1, k * 128 : (k + 1) * 128], plane)
        small = sm[...]
        small = jnp.concatenate(
            [
                jnp.zeros((96, 128), f32),
                small[0:10, 0:128],
                jnp.concatenate([small[0:10, 128:192], jnp.zeros((10, 64), f32)], axis=1),
                jnp.zeros((12, 128), f32),
            ],
            axis=0,
        )
        put(9, jnp.where(lane < 96, plane, small.T))
        weights = jnp.concatenate([gw[0], gw[1], gw[2], gwo[...]], axis=1)
        weights = jnp.concatenate([weights[:, b * 128 : (b + 1) * 128] for b in range(6)], axis=0)
        for k in range(9):
            put(10 + k, weights[k * 128 : (k + 1) * 128])
        for k in range(19, SEND_ROWS):
            put(k, jnp.zeros((128, 128), f32))
        send_ref[...] = snd[...].astype(bf16)


def attend(x, u, east, south, diag, ids, ct, gain, nb, w3, bq, wo, bias):
    def whole(shape):
        return pl.BlockSpec(shape, lambda w: (0,) * len(shape))

    ins = [x, u, east, south, diag, ids, ct, gain, nb, w3, bq, wo]
    outs = [(432, WIDTH), (432, WIDTH), (144, WIDTH), (144, WIDTH), (128 * SEND_ROWS, 128)]
    return pl.pallas_call(
        window_kernel,
        grid=(8 // PER_STEP,),
        out_shape=[jax.ShapeDtypeStruct(o, bf16) for o in outs],
        in_specs=[whole(a.shape) for a in ins]
        + [pl.BlockSpec((PER_STEP, PAIRS, WIN_TOKENS), lambda w: (w, 0, 0))],
        out_specs=[whole(o) for o in outs],
        scratch_shapes=[
            pltpu.VMEM((2, 1152, 128), f32),
            pltpu.VMEM((2, 1152, 128), f32),
            pltpu.VMEM((2, 1152, 128), f32),
            pltpu.VMEM((WIN_TOKENS, WIDTH), f32),
            pltpu.VMEM((3, WIDTH, WIDTH), bf16),
            pltpu.VMEM((PAIRS, WIDTH), bf16),
            pltpu.VMEM((2, 8 * PAIRS, 128), f32),
            pltpu.VMEM((3, WIDTH, WIDTH), f32),
            pltpu.VMEM((WIDTH, WIDTH), f32),
            pltpu.VMEM((16, WIDTH), f32),
            pltpu.VMEM((2, 1152, 128), f32),
            pltpu.VMEM((128 * SEND_ROWS, 128), f32),
        ],
        compiler_params=pltpu.CompilerParams(
            vmem_limit_bytes=VMEM, dimension_semantics=("arbitrary",)
        ),
        cost_estimate=pl.CostEstimate(flops=4 * 10**9, bytes_accessed=8 * 10**6, transcendentals=10**6),
        name="windows",
    )(*ins, bias)


def sum_kernel(root, in_ref, out_ref):
    total = jnp.sum(in_ref[...].astype(f32).reshape(32, 4 * SEND_ROWS, 128), axis=0) * (1.0 / root)
    parts = [total[lat * SEND_ROWS : (lat + 1) * SEND_ROWS] for lat in range(4)]
    shared = (parts[0] + parts[1]) + (parts[2] + parts[3])
    tails = [
        jnp.concatenate(
            [
                parts[j][9:10, 0:90],
                parts[3][9:10, 30 * j : 30 * j + 30],
                shared[9:10, 96 + 7 * j : 103 + 7 * j],
                jnp.zeros((1, 1), f32),
            ],
            axis=1,
        )
        for j in range(3)
    ]
    rows = [p[0:9] for p in parts] + [shared[10:19]] + tails
    rows = jnp.concatenate(rows, axis=0).astype(bf16)
    for peer in range(64):
        out_ref[peer * GATHER_ROWS : (peer + 1) * GATHER_ROWS, :] = rows


def summed(received, root):
    def body(in_ref, out_ref):
        sum_kernel(root, in_ref, out_ref)

    return pl.pallas_call(
        body,
        out_shape=jax.ShapeDtypeStruct((64 * GATHER_ROWS, 128), bf16),
        in_specs=[pl.BlockSpec(memory_space=pltpu.VMEM)],
        out_specs=pl.BlockSpec(memory_space=pltpu.VMEM),
        compiler_params=pltpu.CompilerParams(vmem_limit_bytes=VMEM),
        name="sums",
    )(received)


def spread_kernel(
    scal_ref,
    own_ref,
    other_ref,
    tab_ref,
    class_ref,
    gain_ref,
    nb_ref,
    wqkv_ref,
    bqkv_ref,
    wo_ref,
    bo_ref,
    g,
    tails,
    p,
):
    core = scal_ref[32]
    half = 64 * GATHER_ROWS
    g[pl.ds(pl.multiple_of(core * half, half), half), :] = own_ref[...].astype(f32)
    g[pl.ds(pl.multiple_of((1 - core) * half, half), half), :] = other_ref[...].astype(f32)
    extra = [g[pl.ds(45 + j, 128, stride=GATHER_ROWS), :] for j in range(3)]
    for lat in range(3):
        tails[lat] = extra[lat]
    tails[3] = jnp.concatenate([e[:, 90:120] for e in extra] + [jnp.zeros((128, 38), f32)], axis=1)
    for lat in range(4):
        for w in range(8):
            kind = scal_ref[lat * 8 + w]
            for q in range(16):
                e = q * 8 + w
                src = e * GATHER_ROWS + lat * 9
                to = pl.multiple_of((q * 32 + kind) * 16, 16)
                p[pl.ds(to, 9), :] = g[src : src + 9, :]
                p[pl.ds(to + 9, 1), :] = tails[lat, e : e + 1, :]
    for m in range(144):
        k, q = m // 16, m % 16
        lu, c = m // 72, m % 72
        h, la = c // 12, c % 12
        at = (((la // 6) * 2 + lu) * 6 + la % 6) * GROUP
        tab_ref[h, :, at : at + 128] = p[pl.ds(q * 512 + k, 32, stride=16), :]
        tail = p[pl.ds(q * 512 + 9, 32, stride=16), :]
        tab_ref[h, :, at + 128 : at + GROUP] = tail[:, k * 10 : k * 10 + 10]
    weights = jnp.concatenate(
        [g[pl.ds(36 + k, 128, stride=GATHER_ROWS), :] for k in range(9)], axis=0
    )
    weights = jnp.concatenate([weights[b * 192 : (b + 1) * 192] for b in range(6)], axis=1)
    wqkv_ref[...] = weights[:, 0:576]
    wo_ref[...] = weights[:, 576:768]
    small = jnp.concatenate([e[:, 120:127] for e in extra] + [jnp.zeros((128, 107), f32)], axis=1).T
    small = jnp.concatenate([small[0:10], small[10:20]], axis=1)[:, 0:WIDTH]
    class_ref[...] = small[0:4]
    gain_ref[...] = small[4:5]
    nb_ref[...] = small[5:6]
    bqkv_ref[...] = jnp.concatenate([small[6:7], small[7:8], small[8:9]], axis=1)
    bo_ref[...] = small[9:10]


def spread(own, other, scal):
    outs = [
        (HEADS, 32, POSITIONS),
        (CLASSES, WIDTH),
        (1, WIDTH),
        (1, WIDTH),
        (WIDTH, 3 * WIDTH),
        (1, 3 * WIDTH),
        (WIDTH, WIDTH),
        (1, WIDTH),
    ]
    return pl.pallas_call(
        spread_kernel,
        out_shape=[jax.ShapeDtypeStruct(o, f32) for o in outs],
        in_specs=[
            pl.BlockSpec(memory_space=pltpu.SMEM),
            pl.BlockSpec(memory_space=pltpu.VMEM),
            pl.BlockSpec(memory_space=pltpu.VMEM),
        ],
        out_specs=[pl.BlockSpec(memory_space=pltpu.VMEM)] * len(outs),
        scratch_shapes=[
            pltpu.VMEM((128 * GATHER_ROWS, 128), f32),
            pltpu.VMEM((4, 128, 128), f32),
            pltpu.VMEM((16 * 32 * 16, 128), f32),
        ],
        compiler_params=pltpu.CompilerParams(vmem_limit_bytes=VMEM),
        name="spread",
    )(scal, own, other)


def moved(array, lon_by, lat_by):
    lon, lat = lax.axis_size("lon"), lax.axis_size("lat")
    pairs = [
        (i * lat + j, ((i + lon_by) % lon) * lat + (j + lat_by) % lat)
        for i in range(lon)
        for j in range(lat)
    ]
    return lax.ppermute(array, BOTH, pairs)


def shards(
    inputs,
    upstream,
    land_ids,
    window_kinds,
    class_table,
    norm_gain,
    norm_bias,
    qkv_weight,
    qkv_bias,
    out_weight,
    bias_table,
):
    x = inputs[0].transpose(1, 2, 0, 3)
    u = upstream[0].transpose(1, 2, 0, 3)
    both = jnp.concatenate([x, u], axis=-1)
    ids = land_ids.astype(bf16)

    def frame_row(piece, before, after):
        row = jnp.pad(piece, (before, after)).reshape(1, WIN_TOKENS)
        return jnp.pad(row, ((0, 7), (0, 2 * WIDTH - WIN_TOKENS)))

    def packet(rows, row):
        return jnp.concatenate([rows.reshape(-1, 2 * WIDTH), row], axis=0)

    east = packet(both[3:12, 0:6], frame_row(ids[3:12, 0:6], (0, 3), (6, 0)))
    south = packet(both[0:3, 6:12], frame_row(ids[0:3, 6:12], (9, 0), (0, 6)))
    diag = packet(both[0:3, 0:6], frame_row(ids[0:3, 0:6], (9, 0), (6, 0)))
    east = moved(east, -1, 0)
    south = moved(south, 0, -1)
    diag = moved(diag, -1, -1)
    own_ids = frame_row(ids[3:12, 6:12], (0, 3), (0, 6)).astype(f32)

    lats = lax.axis_size("lat")
    mine_at = lax.axis_index("lat")
    kinds = jnp.zeros((lats, 8), jnp.int32)
    for by in range(lats):
        theirs = window_kinds if by == 0 else moved(window_kinds, 0, -by)
        owner = lax.rem(mine_at + by, lats)
        kinds = jnp.where((jnp.arange(lats) == owner)[:, None], theirs[None], kinds)
    kinds = kinds.reshape(32)

    last_lat = (lax.axis_index("lat") == lax.axis_size("lat") - 1).astype(jnp.int32)
    scal = jnp.concatenate([window_kinds, last_lat.reshape(1)])
    bias = expand_bias(bias_table.transpose(1, 0, 2), scal)

    own, east_out, south_out, diag_out, send = attend(
        x.reshape(1152, WIDTH),
        u.reshape(1152, WIDTH),
        east,
        south,
        diag,
        own_ids,
        class_table,
        norm_gain.reshape(1, WIDTH),
        norm_bias.reshape(1, WIDTH),
        qkv_weight,
        qkv_bias.reshape(1, 3 * WIDTH),
        out_weight,
        bias,
    )
    east_back = moved(east_out, 1, 0).reshape(9, 6, 8, WIDTH)
    south_back = moved(south_out, 0, 1).reshape(3, 6, 8, WIDTH)
    diag_back = moved(diag_out, 1, 1).reshape(3, 6, 8, WIDTH)
    own = own.reshape(9, 6, 8, WIDTH)

    root = math.sqrt(inputs.size // WIDTH * lax.axis_size("lon") * lax.axis_size("lat"))
    received = lax.all_to_all(send.reshape(128, SEND_ROWS, 128), BOTH, 0, 0)
    received, east_back, south_back, diag_back = lax.optimization_barrier(
        (received, east_back, south_back, diag_back)
    )
    part = summed(received.reshape(128 * SEND_ROWS, 128), root)
    same_core = [[d for d in range(128) if d % 2 == core] for core in range(2)]
    mine = lax.all_to_all(
        part.reshape(64, GATHER_ROWS, 128), BOTH, 0, 0, axis_index_groups=same_core
    )
    other = lax.ppermute(mine, BOTH, [(d, d ^ 1) for d in range(128)])
    flat = (64 * GATHER_ROWS, 128)
    scal = jnp.concatenate([kinds, (lax.axis_index("lat") % 2).reshape(1)])
    table, grad_class, grad_gain, grad_nb, grad_wqkv, grad_bqkv, grad_wout, grad_bout = spread(
        mine.reshape(flat), other.reshape(flat), scal
    )

    grad_x = jnp.concatenate(
        [
            jnp.concatenate([diag_back, south_back], axis=1),
            jnp.concatenate([east_back, own], axis=1),
        ],
        axis=0,
    )
    return (
        grad_x.transpose(2, 0, 1, 3)[None],
        grad_class,
        grad_gain.reshape(WIDTH),
        grad_nb.reshape(WIDTH),
        grad_wqkv,
        grad_bqkv.reshape(3 * WIDTH),
        grad_wout,
        grad_bout.reshape(WIDTH),
        table.transpose(1, 0, 2),
    )


def solution(mesh):
    placed = (
        P(None, None, "lat", "lon", None),
        P(None, None, "lat", "lon", None),
        P("lat", "lon"),
        P("lat"),
        P(),
        P(),
        P(),
        P(),
        P(),
        P(),
        P(),
    )
    return jax.shard_map(
        shards,
        mesh=mesh,
        in_specs=placed,
        out_specs=(P(None, None, "lat", "lon", None), P(), P(), P(), P(), P(), P(), P(), P()),
        check_vma=False,
    )
```

time: 134 us -> 118 us (0.88)
  waiting for transfers between devices: 44.3 us -> 22.6 us
  blocking collectives: 0 us -> 20.3 us
  local copies, waits for them, and re-layouts: 12.1 us -> 3.93 us
  Pallas kernels: 43.9 us -> 38 us
  starting transfers between devices: 27.3 us -> 25.2 us
  other arithmetic: 5.21 us -> 7.13 us
    all_to_all x0 -> x1, blocking collectives: none -> 20.3 us  [shards(): lax.all_to_all(part.reshape(64, GATHER_ROWS, 128), BOTH, 0, 0, axis_index...]
    all_to_all x1, waiting for transfers between devices: 15.7 us -> 0.01 us  [shards(): received = lax.all_to_all(send.reshape(128, SEND_ROWS, 128), BOTH, 0, 0)]
    ppermute x6 -> x9, waiting for transfers between devices: 28.6 us -> 22.6 us  [moved(): return lax.ppermute(array, BOTH, pairs)]
    pallas_call x4, Pallas kernels: 43.9 us -> 38 us  [the longest x1 20.7 us: attend(): pl.pallas_call(window_kernel, grid=(8 // PER_STEP,), out_shape=[jax.Shape...]
    all_to_all x1 -> x0, starting transfers between devices: 4.53 us -> none  [shards(): lax.all_to_all(jnp.broadcast_to(part, (128, GATHER_ROWS, 128)), BOTH, 0, 0)]
    slice x3 -> x0, local copies, waits for them, and re-layouts: 3.35 us -> none  [the longest x1 1.35 us: shards(): small[9]]
    broadcast_in_dim x1 -> x0, local copies, waits for them, and re-layouts: 2.24 us -> none  [shards(): jnp.broadcast_to(part, (128, GATHER_ROWS, 128))]
    reshape x3 -> x1, local copies, waits for them, and re-layouts: 2.21 us -> 0.58 us  [shards(): qkv_bias.reshape(1, 3 * WIDTH)]
  transfers between devices with their start and end apart: 8 -> 11, of which waited for: 2 -> 4; matrix products, arithmetic and copies ran while one was open for 5% -> 4% of each run, Pallas kernels for 6% -> 8%
where the time goes in v2:
time: 118 us
  Pallas kernels  38 us (32%)
  starting transfers between devices  25.2 us (21%)
  waiting for transfers between devices  22.6 us (19%)
  blocking collectives  20.3 us (17%)
  other arithmetic  7.13 us (6%)
  local copies, waits for them, and re-layouts  3.93 us (3%)
    ppermute x9, waiting for transfers between devices, moved(): return lax.ppermute(array, BOTH, pairs)  22.6 us
    pallas_call x1, Pallas kernels, attend(): pl.pallas_call(window_kernel, grid=(8 // PER_STEP,), out_shape=[jax.Shape...  20.7 us
    all_to_all x1, blocking collectives, shards(): lax.all_to_all(part.reshape(64, GATHER_ROWS, 128), BOTH, 0, 0, axis_index...  20.3 us
    ppermute x9, starting transfers between devices, moved(): return lax.ppermute(array, BOTH, pairs)  17.9 us
    pallas_call x1, Pallas kernels, expand_bias(): pl.pallas_call(bias_kernel, out_shape=jax.ShapeDtypeStruct((8, PAIRS, WIN...  9.42 us
    all_to_all x1, starting transfers between devices, shards(): received = lax.all_to_all(send.reshape(128, SEND_ROWS, 128), BOTH, 0, 0)  5.68 us
    pallas_call x1, Pallas kernels, spread(): pl.pallas_call(spread_kernel, out_shape=[jax.ShapeDtypeStruct(o, f32) for...  5.63 us
    unnamed x18, local copies, waits for them, and re-layouts  2.59 us
  transfers between devices with their start and end apart: 11, of which 4 were waited for; matrix products, arithmetic and copies ran while one was open for 4% of the time, Pallas kernels for 8%

profile of v2, /device:TPU:1, one launch (start us, length us, event | category | flops | bytes accessed | tf_op | source)
XLA Modules:
  0.0 117.9 jit_solution(10465946937736109709)
XLA Ops:
  0.7 0.7 convert_element_type.20
  1.6 1.1 pad_maximum_fusion
  2.7 8.6 %collective-permute-start.2 = (bf16[152,384]{1,0:T(8,128)(2,1)S(1)}, bf16[152,384]{1,0:T(8,128)(2,1)S(1)}, u32[]{:S(2)}, u32[]{:S(2)}) collective-permute-start(bf16[152,384]{1,0:T(8,128)(2,1)S(1)} %fusion.6), channel_id=1, source_target_pairs={{0,127},{1,124},{2,125},{3,126},{4,3},{5,0},{6,1},{7,2},{8,7},{9,4... | collective-permute-start | bytes 350216 | tf_op jit(solution)/shard_map/ppermute | solution.py:530
  11.5 1.2 collective-permute-start.1
  12.7 1.2 fusion.2
  14.0 0.1 reshape.139
  14.2 0.6 pad_add_fusion.scal_ref
  14.8 9.4 %bias.1.b_ref = f32[8,864,144]{2,1,0:T(8,128)} custom-call(s32[9]{0:T(128)} %pad_add_fusion.scal_ref, f32[6,32,3312]{2,1,0:T(8,128)} %bitcast.38), custom_call_target="tpu_custom_call" | custom-call | flops 2000000000 | bytes 7000000 | tf_op jit(solution)/shard_map/bias/pallas_call | solution.py:107
  24.2 0.6 reshape.147.bq_ref
  24.9 0.6 pad_convert_fusion.ids_ref
  25.6 0.6 copy-done.7
  26.2 0.1 copy-done.6
  26.3 20.7 %windows.1 = (bf16[432,192]{1,0:T(8,128)(2,1)}, bf16[432,192]{1,0:T(8,128)(2,1)}, bf16[144,192]{1,0:T(8,128)(2,1)}, bf16[144,192]{1,0:T(8,128)(2,1)}, bf16[3072,128]{1,0:T(8,128)(2,1)}) custom-call(bf16[1152,192]{1,0:T(8,128)(2,1)} %bitcast.41, bf16[1152,192]{1,0:T(8,128)(2,1)} %bitcast.44, bf16[440,384]{1,0:T(8,128)(2,1)} %copy-done.6, ...), custom_call_target="tpu_custom_call" | custom-call | flops 4000000000 | bytes 8000000 | tf_op jit(solution)/shard_map/windows/pallas_call | solution.py:372
  47.0 5.7 %all-to-all-start = ((bf16[128,24,128]{2,1,0:T(8,128)(2,1)}), bf16[128,24,128]{2,1,0:T(8,128)(2,1)S(1)}, u32[]{:S(2)}, u32[]{:S(2)}) async-start(bf16[128,24,128]{2,1,0:T(8,128)(2,1)} %bitcast.47), calls=%async_computation | async-start | bytes 1572864 | tf_op jit(solution)/shard_map/all_to_all | solution.py:600
  52.7 1.5 %collective-permute-start.3 = (bf16[432,192]{1,0:T(8,128)(2,1)}, bf16[432,192]{1,0:T(8,128)(2,1)S(1)}, u32[]{:S(2)}, u32[]{:S(2)}) collective-permute-start(bf16[432,192]{1,0:T(8,128)(2,1)} %get-tuple-element.27), channel_id=1, source_target_pairs={{0,4},{1,5},{2,6},{3,7},{4,8},{5,9},{6,10},{7,11},{8,12},{9,13},{1... | collective-permute-start | bytes 497672 | tf_op jit(solution)/shard_map/ppermute | solution.py:530
  54.2 3.0 %collective-permute-start.4 = (bf16[144,192]{1,0:T(8,128)(2,1)}, bf16[144,192]{1,0:T(8,128)(2,1)S(1)}, u32[]{:S(2)}, u32[]{:S(2)}) collective-permute-start(bf16[144,192]{1,0:T(8,128)(2,1)} %get-tuple-element.28), channel_id=1, source_target_pairs={{0,1},{1,2},{2,3},{3,0},{4,5},{5,6},{6,7},{7,4},{8,9},{9,10},{10,1... | collective-permute-start | bytes 165896 | tf_op jit(solution)/shard_map/ppermute | solution.py:530
  57.1 0.5 collective-permute-start.5
  57.7 8.4 %collective-permute-done.4 = bf16[144,192]{1,0:T(8,128)(2,1)S(1)} collective-permute-done((bf16[144,192]{1,0:T(8,128)(2,1)}, bf16[144,192]{1,0:T(8,128)(2,1)S(1)}, u32[]{:S(2)}, u32[]{:S(2)}) %collective-permute-start.4) | collective-permute-done | bytes 55328 | tf_op jit(solution)/shard_map/ppermute | solution.py:530
  66.1 9.7 %collective-permute-done.5 = bf16[144,192]{1,0:T(8,128)(2,1)S(1)} collective-permute-done((bf16[144,192]{1,0:T(8,128)(2,1)}, bf16[144,192]{1,0:T(8,128)(2,1)S(1)}, u32[]{:S(2)}, u32[]{:S(2)}) %collective-permute-start.5) | collective-permute-done | bytes 55328 | tf_op jit(solution)/shard_map/ppermute | solution.py:530
  75.8 0.9 copy-done.1
  76.7 2.2 %sums.1 = bf16[3072,128]{1,0:T(8,128)(2,1)} custom-call(bf16[3072,128]{1,0:T(8,128)(2,1)} %bitcast.36), custom_call_target="tpu_custom_call" | custom-call | tf_op jit(solution)/shard_map/sums/pallas_call | solution.py:427
  78.9 20.3 %all_to_all.10 = bf16[64,48,128]{2,1,0:T(8,128)(2,1)S(1)} all-to-all(bf16[64,48,128]{2,1,0:T(8,128)(2,1)} %bitcast.37), channel_id=1, replica_groups={{0,2,4,6,8,10,12,14,16,18,20,22,24,26,28,30,32,34,36,38,40,42,44,46,48,..., dimensions={0} | all-to-all | bytes 1572864 | tf_op jit(solution)/shard_map/all_to_all | solution.py:606
  99.2 1.5 %collective-permute-start.9 = (bf16[64,48,128]{2,1,0:T(8,128)(2,1)S(1)}, bf16[64,48,128]{2,1,0:T(8,128)(2,1)S(1)}, u32[]{:S(2)}, u32[]{:S(2)}) collective-permute-start(bf16[64,48,128]{2,1,0:T(8,128)(2,1)S(1)} %all_to_all.10), channel_id=1, source_target_pairs={{0,1},{1,0},{2,3},{3,2},{4,5},{5,4},{6,7},{7,6},{8,9},{9,8},{10,11... | collective-permute-start | bytes 2359304 | tf_op jit(solution)/shard_map/ppermute | solution.py:609
  100.7 0.9 collective-permute-start.7
  101.6 2.3 %collective-permute-start.6 = (s32[8]{0:T(128)S(1)}, s32[8]{0:T(128)S(1)}, u32[]{:S(2)}, u32[]{:S(2)}) collective-permute-start(s32[8]{0:T(128)S(1)} %copy-done.5), channel_id=1, source_target_pairs={{0,1},{1,2},{2,3},{3,0},{4,5},{5,6},{6,7},{7,4},{8,9},{9,10},{10,1... | collective-permute-start | bytes 104 | tf_op jit(solution)/shard_map/ppermute | solution.py:530
  103.9 0.7 collective-permute-done.7
  104.6 3.7 %collective-permute-done.8 = s32[8]{0:T(128)S(1)} collective-permute-done((s32[8]{0:T(128)S(1)}, s32[8]{0:T(128)S(1)}, u32[]{:S(2)}, u32[]{:S(2)}) %collective-permute-start.8) | collective-permute-done | bytes 64 | tf_op jit(solution)/shard_map/ppermute | solution.py:530
  108.5 0.6 pad_add_fusion.1.scal_ref
  109.1 0.9 maximum_bitcast_fusion
  110.0 0.9 copy-done.2
  110.9 5.6 %spread.1 = (f32[6,32,3312]{2,1,0:T(8,128)}, f32[4,192]{1,0:T(4,128)}, f32[1,192]{1,0:T(1,128)}, f32[1,192]{1,0:T(1,128)}, f32[192,576]{1,0:T(8,128)}, /*index=5...) custom-call(s32[33]{0:T(128)} %pad_add_fusion.1.scal_ref, bf16[3072,128]{1,0:T(8,128)(2,1)} %bitcast.35, ...), custom_call_target="tpu_custom_call" | custom-call | tf_op jit(solution)/shard_map/spread/pallas_call | solution.py:504
  116.6 1.3 %reduce = f32[576]{0:T(1024)} reduce(f32[1,576]{1,0:T(1,128)} %get-tuple-element.39, f32[]{:T(128)} %constant.52), dimensions={0}, to_apply=%get-tuple-element.39.reduce_sub_computation | reduce | bytes 4612 | tf_op jit(solution)/shard_map/spread/pallas_call | solution.py:504
  (39 shorter events, 1.0 us)
Async XLA Ops:
  0.6 13.6 %copy-start.5 = (s32[8]{0:T(128)S(1)}, s32[8]{0:T(128)}, u32[]{:S(2)}) copy-start(s32[8]{0:T(128)} %param.14) | copy-start | bytes 100
  2.7 22.8 %collective-permute-start.2 = (bf16[152,384]{1,0:T(8,128)(2,1)S(1)}, bf16[152,384]{1,0:T(8,128)(2,1)S(1)}, u32[]{:S(2)}, u32[]{:S(2)}) collective-permute-start(bf16[152,384]{1,0:T(8,128)(2,1)S(1)} %fusion.6), channel_id=1, source_target_pairs={{0,127},{1,124},{2,125},{3,126},{4,3},{5,0},{6,1},{7,2},{8,7},{9,4... | collective-permute-start | bytes 350216 | tf_op jit(solution)/shard_map/ppermute | solution.py:530
  11.5 14.1 %collective-permute-start.1 = (bf16[152,384]{1,0:T(8,128)(2,1)S(1)}, bf16[152,384]{1,0:T(8,128)(2,1)S(1)}, u32[]{:S(2)}, u32[]{:S(2)}) collective-permute-start(bf16[152,384]{1,0:T(8,128)(2,1)S(1)} %fusion.5), channel_id=1, source_target_pairs={{0,3},{1,0},{2,1},{3,2},{4,7},{5,4},{6,5},{7,6},{8,11},{9,8},{10,9... | collective-permute-start | bytes 350216 | tf_op jit(solution)/shard_map/ppermute | solution.py:530
  14.1 11.4 %collective-permute-start = (bf16[440,384]{1,0:T(8,128)(2,1)S(1)}, bf16[440,384]{1,0:T(8,128)(2,1)S(1)}, u32[]{:S(2)}, u32[]{:S(2)}) collective-permute-start(bf16[440,384]{1,0:T(8,128)(2,1)S(1)} %fusion.1), channel_id=1, source_target_pairs={{0,124},{1,125},{2,126},{3,127},{4,0},{5,1},{6,2},{7,3},{8,4},{9,5... | collective-permute-start | bytes 1013768 | tf_op jit(solution)/shard_map/ppermute | solution.py:530
  14.8 9.4 %copy-start.4 = (f32[576]{0:T(1024)S(1)}, f32[576]{0:T(1024)}, u32[]{:S(2)}) copy-start(f32[576]{0:T(1024)} %param.19) | copy-start | bytes 6916
  25.5 0.6 copy-start.7
  25.5 0.7 copy-start.8
  25.5 0.8 copy-start.6
  47.0 62.1 %copy-start.3 = (bf16[432,192]{1,0:T(8,128)(2,1)S(1)}, bf16[432,192]{1,0:T(8,128)(2,1)}, u32[]{:S(2)}) copy-start(bf16[432,192]{1,0:T(8,128)(2,1)} %get-tuple-element.33) | copy-start | bytes 497668
  47.0 28.8 %all-to-all-start = ((bf16[128,24,128]{2,1,0:T(8,128)(2,1)}), bf16[128,24,128]{2,1,0:T(8,128)(2,1)S(1)}, u32[]{:S(2)}, u32[]{:S(2)}) async-start(bf16[128,24,128]{2,1,0:T(8,128)(2,1)} %bitcast.47), calls=%async_computation | async-start | bytes 1572864 | tf_op jit(solution)/shard_map/all_to_all | solution.py:600
  52.7 23.1 %collective-permute-start.3 = (bf16[432,192]{1,0:T(8,128)(2,1)}, bf16[432,192]{1,0:T(8,128)(2,1)S(1)}, u32[]{:S(2)}, u32[]{:S(2)}) collective-permute-start(bf16[432,192]{1,0:T(8,128)(2,1)} %get-tuple-element.27), channel_id=1, source_target_pairs={{0,4},{1,5},{2,6},{3,7},{4,8},{5,9},{6,10},{7,11},{8,12},{9,13},{1... | collective-permute-start | bytes 497672 | tf_op jit(solution)/shard_map/ppermute | solution.py:530
  54.2 11.9 %collective-permute-start.4 = (bf16[144,192]{1,0:T(8,128)(2,1)}, bf16[144,192]{1,0:T(8,128)(2,1)S(1)}, u32[]{:S(2)}, u32[]{:S(2)}) collective-permute-start(bf16[144,192]{1,0:T(8,128)(2,1)} %get-tuple-element.28), channel_id=1, source_target_pairs={{0,1},{1,2},{2,3},{3,0},{4,5},{5,6},{6,7},{7,4},{8,9},{9,10},{10,1... | collective-permute-start | bytes 165896 | tf_op jit(solution)/shard_map/ppermute | solution.py:530
  57.1 18.7 %collective-permute-start.5 = (bf16[144,192]{1,0:T(8,128)(2,1)}, bf16[144,192]{1,0:T(8,128)(2,1)S(1)}, u32[]{:S(2)}, u32[]{:S(2)}) collective-permute-start(bf16[144,192]{1,0:T(8,128)(2,1)} %get-tuple-element.29), channel_id=1, source_target_pairs={{0,5},{1,6},{2,7},{3,4},{4,9},{5,10},{6,11},{7,8},{8,13},{9,14},{1... | collective-permute-start | bytes 165896 | tf_op jit(solution)/shard_map/ppermute | solution.py:530
  75.8 0.9 copy-start.1
  99.2 10.8 %copy-start = (bf16[64,48,128]{2,1,0:T(8,128)(2,1)}, bf16[64,48,128]{2,1,0:T(8,128)(2,1)S(1)}, u32[]{:S(2)}) copy-start(bf16[64,48,128]{2,1,0:T(8,128)(2,1)S(1)} %all_to_all.10) | copy-start | bytes 2359300
  99.2 10.8 %collective-permute-start.9 = (bf16[64,48,128]{2,1,0:T(8,128)(2,1)S(1)}, bf16[64,48,128]{2,1,0:T(8,128)(2,1)S(1)}, u32[]{:S(2)}, u32[]{:S(2)}) collective-permute-start(bf16[64,48,128]{2,1,0:T(8,128)(2,1)S(1)} %all_to_all.10), channel_id=1, source_target_pairs={{0,1},{1,0},{2,3},{3,2},{4,5},{5,4},{6,7},{7,6},{8,9},{9,8},{10,11... | collective-permute-start | bytes 2359304 | tf_op jit(solution)/shard_map/ppermute | solution.py:609
  100.7 3.9 %collective-permute-start.7 = (s32[8]{0:T(128)S(1)}, s32[8]{0:T(128)S(1)}, u32[]{:S(2)}, u32[]{:S(2)}) collective-permute-start(s32[8]{0:T(128)S(1)} %copy-done.5), channel_id=1, source_target_pairs={{0,2},{1,3},{2,0},{3,1},{4,6},{5,7},{6,4},{7,5},{8,10},{9,11},{10,... | collective-permute-start | bytes 104 | tf_op jit(solution)/shard_map/ppermute | solution.py:530
  101.6 3.0 %collective-permute-start.6 = (s32[8]{0:T(128)S(1)}, s32[8]{0:T(128)S(1)}, u32[]{:S(2)}, u32[]{:S(2)}) collective-permute-start(s32[8]{0:T(128)S(1)} %copy-done.5), channel_id=1, source_target_pairs={{0,1},{1,2},{2,3},{3,0},{4,5},{5,6},{6,7},{7,4},{8,9},{9,10},{10,1... | collective-permute-start | bytes 104 | tf_op jit(solution)/shard_map/ppermute | solution.py:530
  103.9 4.5 %collective-permute-start.8 = (s32[8]{0:T(128)S(1)}, s32[8]{0:T(128)S(1)}, u32[]{:S(2)}, u32[]{:S(2)}) collective-permute-start(s32[8]{0:T(128)S(1)} %copy-done.5), channel_id=1, source_target_pairs={{0,3},{1,0},{2,1},{3,2},{4,7},{5,4},{6,5},{7,6},{8,11},{9,8},{10,9... | collective-permute-start | bytes 104 | tf_op jit(solution)/shard_map/ppermute | solution.py:530
  110.0 0.9 copy-start.2

commit v3 on v2

--- a/solution.py
+++ b/solution.py
@@ -51,7 +51,7 @@
     return jnp.floor((a.astype(f32) + 0.5) * (1.0 / b)).astype(jnp.int32)
 
 
-def bias_kernel(scal_ref, tab_ref, out_ref, sel_ref, t_ref, e_ref):
+def bias_kernel(scal_ref, tab_ref, out_ref, sel_ref, t_ref, e_ref, stage, sems):
     for w in range(8):
         kind = scal_ref[w]
         for h in range(HEADS):
@@ -93,14 +93,20 @@
         for ip in range(6):
             spread = jnp.where(srow == base + 2 * ip, 1.0, 0.0).astype(bf16)
             acc = dot(hi, spread) + dot(mid, spread) + dot(low, spread)
-            e_ref[pl.ds(2 * ip, 576, stride=12), :] = acc[:, 0:128]
-            e_ref[pl.ds(2 * ip + 1, 576, stride=12), :] = acc[:, 128:256]
-        for w in range(8):
+            e_ref[lu, pl.ds(2 * ip, 576, stride=12), :] = acc[:, 0:128]
+            e_ref[lu, pl.ds(2 * ip + 1, 576, stride=12), :] = acc[:, 128:256]
+    copies = []
+    for w in range(8):
+        for lu in range(2):
             for h in range(HEADS):
                 at = (w * HEADS + h) * WIN_TOKENS
-                turned = e_ref[at : at + WIN_TOKENS, :].T
+                turned = e_ref[lu, at : at + WIN_TOKENS, :].T
                 to = h * WIN_TOKENS + lu * 72
-                out_ref[w, to : to + 72, :] = turned[0:72, :]
+                stage[w, to : to + 72, :] = turned[0:72, :]
+        copies.append(pltpu.make_async_copy(stage.at[w], out_ref.at[w], sems.at[w]))
+        copies[-1].start()
+    for copy in copies:
+        copy.wait()
 
 
 def expand_bias(table, scal):
@@ -111,11 +117,13 @@
             pl.BlockSpec(memory_space=pltpu.SMEM),
             pl.BlockSpec(memory_space=pltpu.VMEM),
         ],
-        out_specs=pl.BlockSpec(memory_space=pltpu.VMEM),
+        out_specs=pl.BlockSpec(memory_space=pl.ANY),
         scratch_shapes=[
             pltpu.VMEM((HEADS, 8, 3456), f32),
             pltpu.VMEM((2, 2, 576, 128), f32),
-            pltpu.VMEM((8 * PAIRS, 128), f32),
+            pltpu.VMEM((2, 8 * PAIRS, 128), f32),
+            pltpu.VMEM((8, PAIRS, WIN_TOKENS), f32),
+            pltpu.SemaphoreType.DMA((8,)),
         ],
         compiler_params=pltpu.CompilerParams(vmem_limit_bytes=VMEM),
         cost_estimate=pl.CostEstimate(flops=2 * 10**9, bytes_accessed=7 * 10**6, transcendentals=0),
@@ -227,9 +235,10 @@
         normal_hat = centred * inv_std
         normed = (normal_hat * gain_ref[...] + nb_ref[...]).astype(bf16)
 
-        query = (dot(normed, w3[0]) + bq_ref[:, 0:192]).astype(bf16)
-        key = dot(normed, w3[1]) + bq_ref[:, 192:384]
-        value = dot(normed, w3[2]) + bq_ref[:, 384:576]
+        bq = bq_ref[...].reshape(1, 3 * WIDTH)
+        query = (dot(normed, w3[0]) + bq[:, 0:192]).astype(bf16)
+        key = dot(normed, w3[1]) + bq[:, 192:384]
+        value = dot(normed, w3[2]) + bq[:, 384:576]
         key_turned, value_turned = key.T.astype(bf16), value.T.astype(bf16)
         key_heads = jnp.concatenate([key.astype(bf16)] * HEADS, axis=0) * mask[...]
         value_heads = jnp.concatenate([value.astype(bf16)] * HEADS, axis=0) * mask[...]
@@ -484,22 +493,23 @@
     small = jnp.concatenate([e[:, 120:127] for e in extra] + [jnp.zeros((128, 107), f32)], axis=1).T
     small = jnp.concatenate([small[0:10], small[10:20]], axis=1)[:, 0:WIDTH]
     class_ref[...] = small[0:4]
-    gain_ref[...] = small[4:5]
-    nb_ref[...] = small[5:6]
-    bqkv_ref[...] = jnp.concatenate([small[6:7], small[7:8], small[8:9]], axis=1)
-    bo_ref[...] = small[9:10]
+    gain_ref[...] = small[4:5].reshape(WIDTH)
+    nb_ref[...] = small[5:6].reshape(WIDTH)
+    grad_bqkv = jnp.concatenate([small[6:7], small[7:8], small[8:9]], axis=1)
+    bqkv_ref[...] = grad_bqkv.reshape(3 * WIDTH)
+    bo_ref[...] = small[9:10].reshape(WIDTH)
 
 
 def spread(own, other, scal):
     outs = [
         (HEADS, 32, POSITIONS),
         (CLASSES, WIDTH),
-        (1, WIDTH),
-        (1, WIDTH),
+        (WIDTH,),
+        (WIDTH,),
         (WIDTH, 3 * WIDTH),
-        (1, 3 * WIDTH),
+        (3 * WIDTH,),
         (WIDTH, WIDTH),
-        (1, WIDTH),
+        (WIDTH,),
     ]
     return pl.pallas_call(
         spread_kernel,
@@ -520,6 +530,52 @@
     )(scal, own, other)
 
 
+def pack_kernel(x_ref, u_ref, ids_ref, east_ref, south_ref, diag_ref, ids_out):
+    lane = iota((1, WIN_TOKENS), 1)
+    lat = quotient(lane, 12)
+    lon = lane - 12 * lat
+    ids = ids_ref[...].astype(f32)
+    row = jnp.concatenate([ids[a : a + 1, :] for a in range(12)], axis=1)
+
+    def moved_row(keep, by):
+        kept = jnp.where(keep, row, 0.0)
+        if by < 0:
+            kept = jnp.concatenate([kept[:, -by:], jnp.zeros((1, 2 * WIDTH - WIN_TOKENS - by), f32)], axis=1)
+        else:
+            tail = jnp.zeros((1, 2 * WIDTH - WIN_TOKENS), f32)
+            kept = jnp.concatenate([jnp.zeros((1, by), f32), kept[:, : WIN_TOKENS - by], tail], axis=1)
+        return jnp.concatenate([kept, jnp.zeros((7, 2 * WIDTH), f32)], axis=0)
+
+    def fill(out, lats, lon_at, id_rows):
+        rows = []
+        for a in lats:
+            at = a * 96 + lon_at * 8
+            rows.append(
+                jnp.concatenate(
+                    [x_ref[at : at + 48, :].astype(f32), u_ref[at : at + 48, :].astype(f32)], axis=1
+                )
+            )
+        out[...] = jnp.concatenate(rows + [id_rows], axis=0).astype(bf16)
+
+    fill(east_ref, range(3, 12), 0, moved_row((lat >= 3) & (lon < 6), -30))
+    fill(south_ref, range(0, 3), 6, moved_row((lat < 3) & (lon >= 6), 102))
+    fill(diag_ref, range(0, 3), 0, moved_row((lat < 3) & (lon < 6), 114))
+    ids_out[...] = moved_row((lat >= 3) & (lon >= 6), -42)
+
+
+def pack(x, u, ids):
+    shapes = [((440, 2 * WIDTH), bf16), ((152, 2 * WIDTH), bf16), ((152, 2 * WIDTH), bf16)]
+    shapes.append(((8, 2 * WIDTH), f32))
+    return pl.pallas_call(
+        pack_kernel,
+        out_shape=[jax.ShapeDtypeStruct(*o) for o in shapes],
+        in_specs=[pl.BlockSpec(memory_space=pltpu.VMEM)] * 3,
+        out_specs=[pl.BlockSpec(memory_space=pltpu.VMEM)] * 4,
+        compiler_params=pltpu.CompilerParams(vmem_limit_bytes=VMEM // 4),
+        name="pack",
+    )(x, u, ids)
+
+
 def moved(array, lon_by, lat_by):
     lon, lat = lax.axis_size("lon"), lax.axis_size("lat")
     pairs = [
@@ -545,23 +601,12 @@
 ):
     x = inputs[0].transpose(1, 2, 0, 3)
     u = upstream[0].transpose(1, 2, 0, 3)
-    both = jnp.concatenate([x, u], axis=-1)
-    ids = land_ids.astype(bf16)
-
-    def frame_row(piece, before, after):
-        row = jnp.pad(piece, (before, after)).reshape(1, WIN_TOKENS)
-        return jnp.pad(row, ((0, 7), (0, 2 * WIDTH - WIN_TOKENS)))
-
-    def packet(rows, row):
-        return jnp.concatenate([rows.reshape(-1, 2 * WIDTH), row], axis=0)
-
-    east = packet(both[3:12, 0:6], frame_row(ids[3:12, 0:6], (0, 3), (6, 0)))
-    south = packet(both[0:3, 6:12], frame_row(ids[0:3, 6:12], (9, 0), (0, 6)))
-    diag = packet(both[0:3, 0:6], frame_row(ids[0:3, 0:6], (9, 0), (6, 0)))
+    x = x.reshape(1152, WIDTH)
+    u = u.reshape(1152, WIDTH)
+    east, south, diag, own_ids = pack(x, u, land_ids)
     east = moved(east, -1, 0)
     south = moved(south, 0, -1)
     diag = moved(diag, -1, -1)
-    own_ids = frame_row(ids[3:12, 6:12], (0, 3), (0, 6)).astype(f32)
 
     lats = lax.axis_size("lat")
     mine_at = lax.axis_index("lat")
@@ -576,9 +621,10 @@
     scal = jnp.concatenate([window_kinds, last_lat.reshape(1)])
     bias = expand_bias(bias_table.transpose(1, 0, 2), scal)
 
+    bias, kinds = lax.optimization_barrier((bias, kinds))
     own, east_out, south_out, diag_out, send = attend(
-        x.reshape(1152, WIDTH),
-        u.reshape(1152, WIDTH),
+        x,
+        u,
         east,
         south,
         diag,
@@ -587,7 +633,7 @@
         norm_gain.reshape(1, WIDTH),
         norm_bias.reshape(1, WIDTH),
         qkv_weight,
-        qkv_bias.reshape(1, 3 * WIDTH),
+        qkv_bias,
         out_weight,
         bias,
     )
@@ -598,9 +644,14 @@
 
     root = math.sqrt(inputs.size // WIDTH * lax.axis_size("lon") * lax.axis_size("lat"))
     received = lax.all_to_all(send.reshape(128, SEND_ROWS, 128), BOTH, 0, 0)
-    received, east_back, south_back, diag_back = lax.optimization_barrier(
-        (received, east_back, south_back, diag_back)
+    grad_x = jnp.concatenate(
+        [
+            jnp.concatenate([diag_back, south_back], axis=1),
+            jnp.concatenate([east_back, own], axis=1),
+        ],
+        axis=0,
     )
+    received, grad_x = lax.optimization_barrier((received, grad_x))
     part = summed(received.reshape(128 * SEND_ROWS, 128), root)
     same_core = [[d for d in range(128) if d % 2 == core] for core in range(2)]
     mine = lax.all_to_all(
@@ -613,22 +664,15 @@
         mine.reshape(flat), other.reshape(flat), scal
     )
 
-    grad_x = jnp.concatenate(
-        [
-            jnp.concatenate([diag_back, south_back], axis=1),
-            jnp.concatenate([east_back, own], axis=1),
-        ],
-        axis=0,
-    )
     return (
         grad_x.transpose(2, 0, 1, 3)[None],
         grad_class,
-        grad_gain.reshape(WIDTH),
-        grad_nb.reshape(WIDTH),
+        grad_gain,
+        grad_nb,
         grad_wqkv,
-        grad_bqkv.reshape(3 * WIDTH),
+        grad_bqkv,
         grad_wout,
-        grad_bout.reshape(WIDTH),
+        grad_bout,
         table.transpose(1, 0, 2),
     )
 

time: 118 us -> 120 us (1.017)
  starting transfers between devices: 25.2 us -> 29.4 us
  other arithmetic: 7.13 us -> 3.84 us
  local copies, waits for them, and re-layouts: 3.93 us -> 6.07 us
    ppermute x9, starting transfers between devices: 17.9 us -> 21.4 us  [moved(): return lax.ppermute(array, BOTH, pairs)]
    unnamed x18 -> x22, local copies, waits for them, and re-layouts: 2.59 us -> 5.98 us
    ppermute x9, waiting for transfers between devices: 22.6 us -> 21.1 us  [moved(): return lax.ppermute(array, BOTH, pairs)]
    convert_element_type x2 -> x0, other arithmetic: 1.31 us -> none  [the longest x1 0.71 us: shards(): ids = land_ids.astype(bf16)]
    pallas_call x1 -> x0, other arithmetic: 1.27 us -> none  [spread(): pl.pallas_call(spread_kernel, out_shape=[jax.ShapeDtypeStruct(o, f32) for...]
    ppermute x1, waiting for transfers between devices: 0.01 us -> 1.27 us  [shards(): other = lax.ppermute(mine, BOTH, [(d, d ^ 1) for d in range(128)])]
  transfers between devices with their start and end apart: 11 -> 11, of which waited for: 4 -> 3; matrix products, arithmetic and copies ran while one was open for 4% -> 3% of each run, Pallas kernels for 8% -> 7%
where the time goes in v3:
time: 120 us
  Pallas kernels  37.2 us (31%)
  starting transfers between devices  29.4 us (24%)
  waiting for transfers between devices  22.4 us (19%)
  blocking collectives  20.3 us (17%)
  local copies, waits for them, and re-layouts  6.07 us (5%)
  other arithmetic  3.84 us (3%)
    ppermute x9, starting transfers between devices, moved(): return lax.ppermute(array, BOTH, pairs)  21.4 us
    ppermute x9, waiting for transfers between devices, moved(): return lax.ppermute(array, BOTH, pairs)  21.1 us
    pallas_call x1, Pallas kernels, attend(): pl.pallas_call(window_kernel, grid=(8 // PER_STEP,), out_shape=[jax.Shape...  20.7 us
    all_to_all x1, blocking collectives, shards(): lax.all_to_all(part.reshape(64, GATHER_ROWS, 128), BOTH, 0, 0, axis_index...  20.3 us
    pallas_call x1, Pallas kernels, expand_bias(): pl.pallas_call(bias_kernel, out_shape=jax.ShapeDtypeStruct((8, PAIRS, WIN...  8.39 us
    all_to_all x1, starting transfers between devices, shards(): received = lax.all_to_all(send.reshape(128, SEND_ROWS, 128), BOTH, 0, 0)  6.44 us
    unnamed x22, local copies, waits for them, and re-layouts  5.98 us
    pallas_call x1, Pallas kernels, spread(): pl.pallas_call(spread_kernel, out_shape=[jax.ShapeDtypeStruct(o, f32) for...  5.64 us
  transfers between devices with their start and end apart: 11, of which 3 were waited for; matrix products, arithmetic and copies ran while one was open for 3% of the time, Pallas kernels for 7%

profile of v3, /device:TPU:1, one launch (start us, length us, event | category | flops | bytes accessed | tf_op | source)
XLA Modules:
  0.0 119.9 jit_solution(5339373579714675124)
XLA Ops:
  0.6 3.7 %collective-permute-start.4 = (s32[8]{0:T(128)}, s32[8]{0:T(128)S(1)}, u32[]{:S(2)}, u32[]{:S(2)}) collective-permute-start(s32[8]{0:T(128)} %param.14), channel_id=1, source_target_pairs={{0,2},{1,3},{2,0},{3,1},{4,6},{5,7},{6,4},{7,5},{8,10},{9,11},{10,... | collective-permute-start | bytes 104 | tf_op jit(solution)/shard_map/ppermute | solution.py:586
  4.3 1.0 collective-permute-start.3
  5.3 1.1 copy-done
  6.3 1.1 copy-done.1
  7.4 0.7 copy-done.2
  8.1 0.2 pack.1
  8.3 0.6 copy-done.3
  8.9 3.2 %collective-permute-start.1 = (bf16[152,384]{1,0:T(8,128)(2,1)S(1)}, bf16[152,384]{1,0:T(8,128)(2,1)S(1)}, u32[]{:S(2)}, u32[]{:S(2)}) collective-permute-start(bf16[152,384]{1,0:T(8,128)(2,1)S(1)} %get-tuple-element.31), channel_id=1, source_target_pairs={{0,3},{1,0},{2,1},{3,2},{4,7},{5,4},{6,5},{7,6},{8,11},{9,8},{10,9... | collective-permute-start | bytes 350216 | tf_op jit(solution)/shard_map/ppermute | solution.py:586
  12.1 6.2 %collective-permute-start = (bf16[440,384]{1,0:T(8,128)(2,1)S(1)}, bf16[440,384]{1,0:T(8,128)(2,1)S(1)}, u32[]{:S(2)}, u32[]{:S(2)}) collective-permute-start(bf16[440,384]{1,0:T(8,128)(2,1)S(1)} %get-tuple-element.30), channel_id=1, source_target_pairs={{0,124},{1,125},{2,126},{3,127},{4,0},{5,1},{6,2},{7,3},{8,4},{9,5... | collective-permute-start | bytes 1013768 | tf_op jit(solution)/shard_map/ppermute | solution.py:586
  18.4 1.2 %pad_add_fusion.scal_ref = s32[9]{0:T(128)} fusion(s32[1]{0:T(128)} %bitcast.12, s32[8]{0:T(128)} %param.14), kind=kLoop, calls=%fused_computation.2 | loop fusion | flops 9 | bytes 72 | tf_op jit(solution)/shard_map/concatenate | solution.py:621
  19.6 8.4 %bias.1.b_ref = f32[8,864,144]{2,1,0:T(8,128)} custom-call(s32[9]{0:T(128)} %pad_add_fusion.scal_ref, f32[6,32,3312]{2,1,0:T(8,128)} %bitcast.35), custom_call_target="tpu_custom_call" | custom-call | flops 2000000000 | bytes 7000000 | tf_op jit(solution)/shard_map/bias/pallas_call | solution.py:113
  28.0 1.6 %collective-permute-start.2 = (bf16[152,384]{1,0:T(8,128)(2,1)S(1)}, bf16[152,384]{1,0:T(8,128)(2,1)S(1)}, u32[]{:S(2)}, u32[]{:S(2)}) collective-permute-start(bf16[152,384]{1,0:T(8,128)(2,1)S(1)} %get-tuple-element.32), channel_id=1, source_target_pairs={{0,127},{1,124},{2,125},{3,126},{4,3},{5,0},{6,1},{7,2},{8,7},{9,4... | collective-permute-start | bytes 350216 | tf_op jit(solution)/shard_map/ppermute | solution.py:586
  29.6 0.1 select_select_fusion
  29.7 0.1 select_n.34
  29.8 3.9 %collective-permute-done.2.d_ref = bf16[152,384]{1,0:T(8,128)(2,1)S(1)} collective-permute-done((bf16[152,384]{1,0:T(8,128)(2,1)S(1)}, bf16[152,384]{1,0:T(8,128)(2,1)S(1)}, u32[]{:S(2)}, u32[]{:S(2)}) %collective-permute-start.2) | collective-permute-done | bytes 116768 | tf_op jit(solution)/shard_map/ppermute | solution.py:586
  33.7 0.6 copy-done.10
  34.4 0.1 copy-done.8
  34.5 20.7 %windows.1 = (bf16[432,192]{1,0:T(8,128)(2,1)}, bf16[432,192]{1,0:T(8,128)(2,1)}, bf16[144,192]{1,0:T(8,128)(2,1)}, bf16[144,192]{1,0:T(8,128)(2,1)}, bf16[3072,128]{1,0:T(8,128)(2,1)}) custom-call(bf16[1152,192]{1,0:T(8,128)(2,1)} %bitcast.28, bf16[1152,192]{1,0:T(8,128)(2,1)} %bitcast.30, bf16[440,384]{1,0:T(8,128)(2,1)} %copy-done.8, ...), custom_call_target="tpu_custom_call" | custom-call | flops 4000000000 | bytes 8000000 | tf_op jit(solution)/shard_map/windows/pallas_call | solution.py:381
  55.2 6.4 %all-to-all-start = ((bf16[128,24,128]{2,1,0:T(8,128)(2,1)}), bf16[128,24,128]{2,1,0:T(8,128)(2,1)S(1)}, u32[]{:S(2)}, u32[]{:S(2)}) async-start(bf16[128,24,128]{2,1,0:T(8,128)(2,1)} %bitcast.36), calls=%async_computation | async-start | bytes 1572864 | tf_op jit(solution)/shard_map/all_to_all | solution.py:646
  61.7 1.5 %collective-permute-start.8 = (bf16[432,192]{1,0:T(8,128)(2,1)}, bf16[432,192]{1,0:T(8,128)(2,1)S(1)}, u32[]{:S(2)}, u32[]{:S(2)}) collective-permute-start(bf16[432,192]{1,0:T(8,128)(2,1)} %get-tuple-element.38), channel_id=1, source_target_pairs={{0,4},{1,5},{2,6},{3,7},{4,8},{5,9},{6,10},{7,11},{8,12},{9,13},{1... | collective-permute-start | bytes 497672 | tf_op jit(solution)/shard_map/ppermute | solution.py:586
  63.1 3.4 %collective-permute-start.6 = (bf16[144,192]{1,0:T(8,128)(2,1)}, bf16[144,192]{1,0:T(8,128)(2,1)S(1)}, u32[]{:S(2)}, u32[]{:S(2)}) collective-permute-start(bf16[144,192]{1,0:T(8,128)(2,1)} %get-tuple-element.36), channel_id=1, source_target_pairs={{0,5},{1,6},{2,7},{3,4},{4,9},{5,10},{6,11},{7,8},{8,13},{9,14},{1... | collective-permute-start | bytes 165896 | tf_op jit(solution)/shard_map/ppermute | solution.py:586
  66.5 0.9 collective-permute-start.7
  67.4 17.2 %collective-permute-done.6 = bf16[144,192]{1,0:T(8,128)(2,1)S(1)} collective-permute-done((bf16[144,192]{1,0:T(8,128)(2,1)}, bf16[144,192]{1,0:T(8,128)(2,1)S(1)}, u32[]{:S(2)}, u32[]{:S(2)}) %collective-permute-start.6) | collective-permute-done | bytes 55328 | tf_op jit(solution)/shard_map/ppermute | solution.py:586
  84.6 1.9 %maximum_maximum_fusion = bf16[12,12,8,192]{3,2,1,0:T(8,128)(2,1)} fusion(bf16[9,6,8,192]{3,2,1,0:T(8,128)(2,1)} %bitcast.39, bf16[9,6,8,192]{3,2,1,0:T(8,128)(2,1)S(1)} %bitcast.40, bf16[3,6,8,192]{3,2,1,0:T(8,128)(2,1)S(1)} %bitcast.42, bf16[3,6,8,192]{3,2,1,0:T(8,128)(2,1)S(1)} %bitcast.41), kind=kLoop, calls=%fused_computation | loop fusion | flops 663552 | bytes 884736 | tf_op jit(solution)/shard_map/concatenate | solution.py:647
  86.5 0.9 copy-done.4
  87.4 2.2 %sums.1 = bf16[3072,128]{1,0:T(8,128)(2,1)} custom-call(bf16[3072,128]{1,0:T(8,128)(2,1)} %bitcast.32), custom_call_target="tpu_custom_call" | custom-call | tf_op jit(solution)/shard_map/sums/pallas_call | solution.py:436
  89.6 20.3 %all_to_all.10 = bf16[64,48,128]{2,1,0:T(8,128)(2,1)S(1)} all-to-all(bf16[64,48,128]{2,1,0:T(8,128)(2,1)} %bitcast.34), channel_id=1, replica_groups={{0,2,4,6,8,10,12,14,16,18,20,22,24,26,28,30,32,34,36,38,40,42,44,46,48,..., dimensions={0} | all-to-all | bytes 1572864 | tf_op jit(solution)/shard_map/all_to_all | solution.py:657
  109.9 1.5 %collective-permute-start.9 = (bf16[64,48,128]{2,1,0:T(8,128)(2,1)S(1)}, bf16[64,48,128]{2,1,0:T(8,128)(2,1)S(1)}, u32[]{:S(2)}, u32[]{:S(2)}) collective-permute-start(bf16[64,48,128]{2,1,0:T(8,128)(2,1)S(1)} %all_to_all.10), channel_id=1, source_target_pairs={{0,1},{1,0},{2,3},{3,2},{4,5},{5,4},{6,7},{7,6},{8,9},{9,8},{10,11... | collective-permute-start | bytes 2359304 | tf_op jit(solution)/shard_map/ppermute | solution.py:660
  111.4 0.6 pad_add_fusion.1.scal_ref
  112.1 1.3 %collective-permute-done.9 = bf16[64,48,128]{2,1,0:T(8,128)(2,1)S(1)} collective-permute-done((bf16[64,48,128]{2,1,0:T(8,128)(2,1)S(1)}, bf16[64,48,128]{2,1,0:T(8,128)(2,1)S(1)}, u32[]{:S(2)}, u32[]{:S(2)}) %collective-permute-start.9) | collective-permute-done | bytes 786464 | tf_op jit(solution)/shard_map/ppermute | solution.py:660
  113.4 0.9 copy-done.6
  114.3 5.6 %spread.1 = (f32[6,32,3312]{2,1,0:T(8,128)}, f32[4,192]{1,0:T(4,128)}, f32[192]{0:T(256)}, f32[192]{0:T(256)}, f32[192,576]{1,0:T(8,128)}, /*index=5*/f32[576]{0:T(1024)}, f32[192,192]{1,0:T(8,128)}, f32[192]{0:T(256)}) custom-call(s32[33]{0:T(128)} %pad_add_fusion.1.scal_ref, bf16[3072,128]{1,0:T(8,128)(2,1)} %bitcast.33, bf16[3072,128]{1,0:T(8,128)(2,1)} %bitcast.37), custom_call_target="tpu_custom_call" | custom-call | tf_op jit(solution)/shard_map/spread/pallas_call | solution.py:514
  (25 shorter events, 0.1 us)
Async XLA Ops:
  0.6 27.4 %collective-permute-start.4 = (s32[8]{0:T(128)}, s32[8]{0:T(128)S(1)}, u32[]{:S(2)}, u32[]{:S(2)}) collective-permute-start(s32[8]{0:T(128)} %param.14), channel_id=1, source_target_pairs={{0,2},{1,3},{2,0},{3,1},{4,6},{5,7},{6,4},{7,5},{8,10},{9,11},{10,... | collective-permute-start | bytes 104 | tf_op jit(solution)/shard_map/ppermute | solution.py:586
  4.3 25.3 %collective-permute-start.3 = (s32[8]{0:T(128)}, s32[8]{0:T(128)S(1)}, u32[]{:S(2)}, u32[]{:S(2)}) collective-permute-start(s32[8]{0:T(128)} %param.14), channel_id=1, source_target_pairs={{0,1},{1,2},{2,3},{3,0},{4,5},{5,6},{6,7},{7,4},{8,9},{9,10},{10,1... | collective-permute-start | bytes 104 | tf_op jit(solution)/shard_map/ppermute | solution.py:586
  5.3 24.3 %collective-permute-start.5 = (s32[8]{0:T(128)}, s32[8]{0:T(128)S(1)}, u32[]{:S(2)}, u32[]{:S(2)}) collective-permute-start(s32[8]{0:T(128)} %param.14), channel_id=1, source_target_pairs={{0,3},{1,0},{2,1},{3,2},{4,7},{5,4},{6,5},{7,6},{8,11},{9,8},{10,9... | collective-permute-start | bytes 104 | tf_op jit(solution)/shard_map/ppermute | solution.py:586
  5.3 1.1 copy-start
  6.3 1.1 copy-start.1
  7.4 0.7 copy-start.2
  8.3 0.6 copy-start.3
  8.9 20.9 %collective-permute-start.1 = (bf16[152,384]{1,0:T(8,128)(2,1)S(1)}, bf16[152,384]{1,0:T(8,128)(2,1)S(1)}, u32[]{:S(2)}, u32[]{:S(2)}) collective-permute-start(bf16[152,384]{1,0:T(8,128)(2,1)S(1)} %get-tuple-element.31), channel_id=1, source_target_pairs={{0,3},{1,0},{2,1},{3,2},{4,7},{5,4},{6,5},{7,6},{8,11},{9,8},{10,9... | collective-permute-start | bytes 350216 | tf_op jit(solution)/shard_map/ppermute | solution.py:586
  12.1 21.6 %collective-permute-start = (bf16[440,384]{1,0:T(8,128)(2,1)S(1)}, bf16[440,384]{1,0:T(8,128)(2,1)S(1)}, u32[]{:S(2)}, u32[]{:S(2)}) collective-permute-start(bf16[440,384]{1,0:T(8,128)(2,1)S(1)} %get-tuple-element.30), channel_id=1, source_target_pairs={{0,124},{1,125},{2,126},{3,127},{4,0},{5,1},{6,2},{7,3},{8,4},{9,5... | collective-permute-start | bytes 1013768 | tf_op jit(solution)/shard_map/ppermute | solution.py:586
  19.6 10.0 %copy-start.7 = (s32[8]{0:T(128)S(1)}, s32[8]{0:T(128)}, u32[]{:S(2)}) copy-start(s32[8]{0:T(128)} %param.14) | copy-start | bytes 100
  28.0 5.7 %collective-permute-start.2 = (bf16[152,384]{1,0:T(8,128)(2,1)S(1)}, bf16[152,384]{1,0:T(8,128)(2,1)S(1)}, u32[]{:S(2)}, u32[]{:S(2)}) collective-permute-start(bf16[152,384]{1,0:T(8,128)(2,1)S(1)} %get-tuple-element.32), channel_id=1, source_target_pairs={{0,127},{1,124},{2,125},{3,126},{4,3},{5,0},{6,1},{7,2},{8,7},{9,4... | collective-permute-start | bytes 350216 | tf_op jit(solution)/shard_map/ppermute | solution.py:586
  29.8 4.0 %copy-start.9 = (bf16[152,384]{1,0:T(8,128)(2,1)}, bf16[152,384]{1,0:T(8,128)(2,1)S(1)}, u32[]{:S(2)}) copy-start(bf16[152,384]{1,0:T(8,128)(2,1)S(1)} %collective-permute-done.1.s_ref) | copy-start | bytes 350212
  33.7 0.6 copy-start.10
  33.7 0.8 copy-start.8
  55.2 31.3 %all-to-all-start = ((bf16[128,24,128]{2,1,0:T(8,128)(2,1)}), bf16[128,24,128]{2,1,0:T(8,128)(2,1)S(1)}, u32[]{:S(2)}, u32[]{:S(2)}) async-start(bf16[128,24,128]{2,1,0:T(8,128)(2,1)} %bitcast.36), calls=%async_computation | async-start | bytes 1572864 | tf_op jit(solution)/shard_map/all_to_all | solution.py:646
  61.7 23.0 %collective-permute-start.8 = (bf16[432,192]{1,0:T(8,128)(2,1)}, bf16[432,192]{1,0:T(8,128)(2,1)S(1)}, u32[]{:S(2)}, u32[]{:S(2)}) collective-permute-start(bf16[432,192]{1,0:T(8,128)(2,1)} %get-tuple-element.38), channel_id=1, source_target_pairs={{0,4},{1,5},{2,6},{3,7},{4,8},{5,9},{6,10},{7,11},{8,12},{9,13},{1... | collective-permute-start | bytes 497672 | tf_op jit(solution)/shard_map/ppermute | solution.py:586
  63.1 21.5 %collective-permute-start.6 = (bf16[144,192]{1,0:T(8,128)(2,1)}, bf16[144,192]{1,0:T(8,128)(2,1)S(1)}, u32[]{:S(2)}, u32[]{:S(2)}) collective-permute-start(bf16[144,192]{1,0:T(8,128)(2,1)} %get-tuple-element.36), channel_id=1, source_target_pairs={{0,5},{1,6},{2,7},{3,4},{4,9},{5,10},{6,11},{7,8},{8,13},{9,14},{1... | collective-permute-start | bytes 165896 | tf_op jit(solution)/shard_map/ppermute | solution.py:586
  66.5 18.1 %collective-permute-start.7 = (bf16[144,192]{1,0:T(8,128)(2,1)}, bf16[144,192]{1,0:T(8,128)(2,1)S(1)}, u32[]{:S(2)}, u32[]{:S(2)}) collective-permute-start(bf16[144,192]{1,0:T(8,128)(2,1)} %get-tuple-element.37), channel_id=1, source_target_pairs={{0,1},{1,2},{2,3},{3,0},{4,5},{5,6},{6,7},{7,4},{8,9},{9,10},{10,1... | collective-permute-start | bytes 165896 | tf_op jit(solution)/shard_map/ppermute | solution.py:586
  86.5 0.9 copy-start.4
  109.9 3.5 %copy-start.5 = (bf16[64,48,128]{2,1,0:T(8,128)(2,1)}, bf16[64,48,128]{2,1,0:T(8,128)(2,1)S(1)}, u32[]{:S(2)}) copy-start(bf16[64,48,128]{2,1,0:T(8,128)(2,1)S(1)} %all_to_all.10) | copy-start | bytes 2359300
  109.9 3.4 %collective-permute-start.9 = (bf16[64,48,128]{2,1,0:T(8,128)(2,1)S(1)}, bf16[64,48,128]{2,1,0:T(8,128)(2,1)S(1)}, u32[]{:S(2)}, u32[]{:S(2)}) collective-permute-start(bf16[64,48,128]{2,1,0:T(8,128)(2,1)S(1)} %all_to_all.10), channel_id=1, source_target_pairs={{0,1},{1,0},{2,3},{3,2},{4,5},{5,4},{6,7},{7,6},{8,9},{9,8},{10,11... | collective-permute-start | bytes 2359304 | tf_op jit(solution)/shard_map/ppermute | solution.py:660
  113.3 0.9 copy-start.6

commit v4 on v3

--- a/solution.py
+++ b/solution.py
@@ -132,6 +132,7 @@
 
 
 def window_kernel(
+    scal_ref,
     x_ref,
     u_ref,
     e_ref,
@@ -367,12 +368,16 @@
         weights = jnp.concatenate([weights[:, b * 128 : (b + 1) * 128] for b in range(6)], axis=0)
         for k in range(9):
             put(10 + k, weights[k * 128 : (k + 1) * 128])
-        for k in range(19, SEND_ROWS):
+        kinds = jnp.zeros((128, 128), f32)
+        for win in range(8):
+            kinds = jnp.where(lane == win, scal_ref[win].astype(f32), kinds)
+        put(19, kinds)
+        for k in range(20, SEND_ROWS):
             put(k, jnp.zeros((128, 128), f32))
         send_ref[...] = snd[...].astype(bf16)
 
 
-def attend(x, u, east, south, diag, ids, ct, gain, nb, w3, bq, wo, bias):
+def attend(scal, x, u, east, south, diag, ids, ct, gain, nb, w3, bq, wo, bias):
     def whole(shape):
         return pl.BlockSpec(shape, lambda w: (0,) * len(shape))
 
@@ -382,7 +387,8 @@
         window_kernel,
         grid=(8 // PER_STEP,),
         out_shape=[jax.ShapeDtypeStruct(o, bf16) for o in outs],
-        in_specs=[whole(a.shape) for a in ins]
+        in_specs=[pl.BlockSpec(memory_space=pltpu.SMEM)]
+        + [whole(a.shape) for a in ins]
         + [pl.BlockSpec((PER_STEP, PAIRS, WIN_TOKENS), lambda w: (w, 0, 0))],
         out_specs=[whole(o) for o in outs],
         scratch_shapes=[
@@ -404,10 +410,14 @@
         ),
         cost_estimate=pl.CostEstimate(flops=4 * 10**9, bytes_accessed=8 * 10**6, transcendentals=10**6),
         name="windows",
-    )(*ins, bias)
-
-
-def sum_kernel(root, in_ref, out_ref):
+    )(scal, *ins, bias)
+
+
+def sum_kernel(root, core_ref, in_ref, out_ref, kinds_ref):
+    first = in_ref[0 : 4 * SEND_ROWS, :].astype(f32)
+    kinds = [first[lat * SEND_ROWS + 19 : lat * SEND_ROWS + 20] for lat in range(4)]
+    kinds = jnp.concatenate(kinds + [jnp.zeros((4, 128), f32)], axis=0).astype(jnp.int32)
+    kinds_ref[...] = jnp.where(iota((8, 128), 1) == 8, core_ref[0], kinds)
     total = jnp.sum(in_ref[...].astype(f32).reshape(32, 4 * SEND_ROWS, 128), axis=0) * (1.0 / root)
     parts = [total[lat * SEND_ROWS : (lat + 1) * SEND_ROWS] for lat in range(4)]
     shared = (parts[0] + parts[1]) + (parts[2] + parts[3])
@@ -429,18 +439,24 @@
         out_ref[peer * GATHER_ROWS : (peer + 1) * GATHER_ROWS, :] = rows
 
 
-def summed(received, root):
-    def body(in_ref, out_ref):
-        sum_kernel(root, in_ref, out_ref)
+def summed(received, core, root):
+    def body(core_ref, in_ref, out_ref, kinds_ref):
+        sum_kernel(root, core_ref, in_ref, out_ref, kinds_ref)
 
     return pl.pallas_call(
         body,
-        out_shape=jax.ShapeDtypeStruct((64 * GATHER_ROWS, 128), bf16),
-        in_specs=[pl.BlockSpec(memory_space=pltpu.VMEM)],
-        out_specs=pl.BlockSpec(memory_space=pltpu.VMEM),
+        out_shape=[
+            jax.ShapeDtypeStruct((64 * GATHER_ROWS, 128), bf16),
+            jax.ShapeDtypeStruct((8, 128), jnp.int32),
+        ],
+        in_specs=[
+            pl.BlockSpec(memory_space=pltpu.SMEM),
+            pl.BlockSpec(memory_space=pltpu.VMEM),
+        ],
+        out_specs=[pl.BlockSpec(memory_space=pltpu.VMEM)] * 2,
         compiler_params=pltpu.CompilerParams(vmem_limit_bytes=VMEM),
         name="sums",
-    )(received)
+    )(core, received)
 
 
 def spread_kernel(
@@ -459,7 +475,7 @@
     tails,
     p,
 ):
-    core = scal_ref[32]
+    core = scal_ref[0, 8]
     half = 64 * GATHER_ROWS
     g[pl.ds(pl.multiple_of(core * half, half), half), :] = own_ref[...].astype(f32)
     g[pl.ds(pl.multiple_of((1 - core) * half, half), half), :] = other_ref[...].astype(f32)
@@ -469,7 +485,7 @@
     tails[3] = jnp.concatenate([e[:, 90:120] for e in extra] + [jnp.zeros((128, 38), f32)], axis=1)
     for lat in range(4):
         for w in range(8):
-            kind = scal_ref[lat * 8 + w]
+            kind = scal_ref[lat, w]
             for q in range(16):
                 e = q * 8 + w
                 src = e * GATHER_ROWS + lat * 9
@@ -571,7 +587,7 @@
         out_shape=[jax.ShapeDtypeStruct(*o) for o in shapes],
         in_specs=[pl.BlockSpec(memory_space=pltpu.VMEM)] * 3,
         out_specs=[pl.BlockSpec(memory_space=pltpu.VMEM)] * 4,
-        compiler_params=pltpu.CompilerParams(vmem_limit_bytes=VMEM // 4),
+        compiler_params=pltpu.CompilerParams(vmem_limit_bytes=VMEM),
         name="pack",
     )(x, u, ids)
 
@@ -608,21 +624,12 @@
     south = moved(south, 0, -1)
     diag = moved(diag, -1, -1)
 
-    lats = lax.axis_size("lat")
-    mine_at = lax.axis_index("lat")
-    kinds = jnp.zeros((lats, 8), jnp.int32)
-    for by in range(lats):
-        theirs = window_kinds if by == 0 else moved(window_kinds, 0, -by)
-        owner = lax.rem(mine_at + by, lats)
-        kinds = jnp.where((jnp.arange(lats) == owner)[:, None], theirs[None], kinds)
-    kinds = kinds.reshape(32)
-
     last_lat = (lax.axis_index("lat") == lax.axis_size("lat") - 1).astype(jnp.int32)
     scal = jnp.concatenate([window_kinds, last_lat.reshape(1)])
     bias = expand_bias(bias_table.transpose(1, 0, 2), scal)
 
-    bias, kinds = lax.optimization_barrier((bias, kinds))
     own, east_out, south_out, diag_out, send = attend(
+        scal,
         x,
         u,
         east,
@@ -651,17 +658,17 @@
         ],
         axis=0,
     )
-    received, grad_x = lax.optimization_barrier((received, grad_x))
-    part = summed(received.reshape(128 * SEND_ROWS, 128), root)
+    core = (lax.axis_index("lat") % 2).reshape(1)
+    part, kinds = summed(received.reshape(128 * SEND_ROWS, 128), core, root)
+    part, grad_x = lax.optimization_barrier((part, grad_x))
     same_core = [[d for d in range(128) if d % 2 == core] for core in range(2)]
     mine = lax.all_to_all(
         part.reshape(64, GATHER_ROWS, 128), BOTH, 0, 0, axis_index_groups=same_core
     )
     other = lax.ppermute(mine, BOTH, [(d, d ^ 1) for d in range(128)])
     flat = (64 * GATHER_ROWS, 128)
-    scal = jnp.concatenate([kinds, (lax.axis_index("lat") % 2).reshape(1)])
     table, grad_class, grad_gain, grad_nb, grad_wqkv, grad_bqkv, grad_wout, grad_bout = spread(
-        mine.reshape(flat), other.reshape(flat), scal
+        mine.reshape(flat), other.reshape(flat), kinds
     )
 
     return (

time: 120 us -> 111 us (0.925)
  starting transfers between devices: 29.4 us -> 23.1 us
  local copies, waits for them, and re-layouts: 6.07 us -> 2.57 us
  Pallas kernels: 37.2 us -> 39.2 us
    ppermute x9 -> x6, starting transfers between devices: 21.4 us -> 16.4 us  [moved(): return lax.ppermute(array, BOTH, pairs)]
    unnamed x22 -> x12, local copies, waits for them, and re-layouts: 5.98 us -> 2.57 us
    pallas_call x1, Pallas kernels: 0.19 us -> 2.21 us  [pack(): pl.pallas_call(pack_kernel, out_shape=[jax.ShapeDtypeStruct(*o) for o in...]
    ppermute x9 -> x6, waiting for transfers between devices: 21.1 us -> 19.4 us  [moved(): return lax.ppermute(array, BOTH, pairs)]
    all_to_all x1, starting transfers between devices: 6.44 us -> 5.14 us  [shards(): received = lax.all_to_all(send.reshape(128, SEND_ROWS, 128), BOTH, 0, 0)]
  transfers between devices with their start and end apart: 11 -> 8, of which waited for: 3 -> 3; matrix products, arithmetic and copies ran while one was open for 3% -> 3% of each run, Pallas kernels for 7% -> 8%
where the time goes in v4:
time: 111 us; the launch traced here: 110 us
  Pallas kernels  39.2 us (35%)
  starting transfers between devices  23.1 us (21%)
  waiting for transfers between devices  21.4 us (19%)
  blocking collectives  20.3 us (18%)
  other arithmetic  3.11 us (3%)
  local copies, waits for them, and re-layouts  2.57 us (2%)
    pallas_call x1, Pallas kernels, attend(): pl.pallas_call(window_kernel, grid=(8 // PER_STEP,), out_shape=[jax.Shape...  20.7 us
    all_to_all x1, blocking collectives, shards(): lax.all_to_all(part.reshape(64, GATHER_ROWS, 128), BOTH, 0, 0, axis_index...  20.3 us
    ppermute x6, waiting for transfers between devices, moved(): return lax.ppermute(array, BOTH, pairs)  19.4 us
    ppermute x6, starting transfers between devices, moved(): return lax.ppermute(array, BOTH, pairs)  16.4 us
    pallas_call x1, Pallas kernels, expand_bias(): pl.pallas_call(bias_kernel, out_shape=jax.ShapeDtypeStruct((8, PAIRS, WIN...  8.38 us
    pallas_call x1, Pallas kernels, spread(): pl.pallas_call(spread_kernel, out_shape=[jax.ShapeDtypeStruct(o, f32) for...  5.64 us
    all_to_all x1, starting transfers between devices, shards(): received = lax.all_to_all(send.reshape(128, SEND_ROWS, 128), BOTH, 0, 0)  5.14 us
    unnamed x12, local copies, waits for them, and re-layouts  2.57 us
  transfers between devices with their start and end apart: 8, of which 3 were waited for; matrix products, arithmetic and copies ran while one was open for 3% of the time, Pallas kernels for 8%

profile of v4, /device:TPU:1, one launch (start us, length us, event | category | flops | bytes accessed | tf_op | source)
XLA Modules:
  0.0 110.3 jit_solution(12822925150821916824)
XLA Ops:
  0.6 2.2 %pack.1 = (bf16[440,384]{1,0:T(8,128)(2,1)}, bf16[152,384]{1,0:T(8,128)(2,1)}, bf16[152,384]{1,0:T(8,128)(2,1)}, f32[8,384]{1,0:T(8,128)}) custom-call(bf16[1152,192]{1,0:T(8,128)(2,1)} %bitcast.34, bf16[1152,192]{1,0:T(8,128)(2,1)} %bitcast.36, s32[12,12]{1,0:T(8,128)} %ids_ref.1), custom_call_target="tpu_custom_call" | custom-call | tf_op jit(solution)/shard_map/pack/pallas_call | solution.py:585
  2.8 8.0 %collective-permute-start = (bf16[440,384]{1,0:T(8,128)(2,1)}, bf16[440,384]{1,0:T(8,128)(2,1)S(1)}, u32[]{:S(2)}, u32[]{:S(2)}) collective-permute-start(bf16[440,384]{1,0:T(8,128)(2,1)} %get-tuple-element.30), channel_id=1, source_target_pairs={{0,124},{1,125},{2,126},{3,127},{4,0},{5,1},{6,2},{7,3},{8,4},{9,5... | collective-permute-start | bytes 1013768 | tf_op jit(solution)/shard_map/ppermute | solution.py:602
  10.8 1.0 collective-permute-start.1
  11.8 1.7 %collective-permute-start.2 = (bf16[152,384]{1,0:T(8,128)(2,1)}, bf16[152,384]{1,0:T(8,128)(2,1)S(1)}, u32[]{:S(2)}, u32[]{:S(2)}) collective-permute-start(bf16[152,384]{1,0:T(8,128)(2,1)} %get-tuple-element.32), channel_id=1, source_target_pairs={{0,127},{1,124},{2,125},{3,126},{4,3},{5,0},{6,1},{7,2},{8,7},{9,4... | collective-permute-start | bytes 350216 | tf_op jit(solution)/shard_map/ppermute | solution.py:602
  13.5 1.2 %pad_add_fusion.scal_ref = s32[9]{0:T(128)} fusion(s32[1]{0:T(128)} %bitcast.1, s32[8]{0:T(128)} %param.14), kind=kLoop, calls=%fused_computation.1 | loop fusion | flops 9 | bytes 72 | tf_op jit(solution)/shard_map/concatenate | solution.py:628
  14.7 8.4 %bias.1.b_ref = f32[8,864,144]{2,1,0:T(8,128)} custom-call(s32[9]{0:T(128)} %pad_add_fusion.scal_ref, f32[6,32,3312]{2,1,0:T(8,128)} %bitcast.30), custom_call_target="tpu_custom_call" | custom-call | flops 2000000000 | bytes 7000000 | tf_op jit(solution)/shard_map/bias/pallas_call | solution.py:113
  23.1 2.2 %collective-permute-done.1.s_ref = bf16[152,384]{1,0:T(8,128)(2,1)S(1)} collective-permute-done((bf16[152,384]{1,0:T(8,128)(2,1)}, bf16[152,384]{1,0:T(8,128)(2,1)S(1)}, u32[]{:S(2)}, u32[]{:S(2)}) %collective-permute-start.1) | collective-permute-done | bytes 116768 | tf_op jit(solution)/shard_map/ppermute | solution.py:602
  25.4 0.0 copy-start.4
  25.4 0.0 collective-permute-done.2.d_ref
  25.4 0.0 collective-permute-done.e_ref
  25.4 0.0 copy-start.3
  25.4 0.6 copy-done.4
  26.0 0.0 copy-done.5
  26.0 0.1 copy-done.3
  26.2 20.7 %windows.1 = (bf16[432,192]{1,0:T(8,128)(2,1)}, bf16[432,192]{1,0:T(8,128)(2,1)}, bf16[144,192]{1,0:T(8,128)(2,1)}, bf16[144,192]{1,0:T(8,128)(2,1)}, bf16[3072,128]{1,0:T(8,128)(2,1)}) custom-call(s32[9]{0:T(128)} %pad_add_fusion.scal_ref, bf16[1152,192]{1,0:T(8,128)(2,1)} %bitcast.35, bf16[1152,192]{1,0:T(8,128)(2,1)} %bitcast.37, ...), custom_call_target="tpu_custom_call" | custom-call | flops 4000000000 | bytes 8000000 | tf_op jit(solution)/shard_map/windows/pallas_call | solution.py:386
  46.9 5.1 %all-to-all-start = ((bf16[128,24,128]{2,1,0:T(8,128)(2,1)}), bf16[128,24,128]{2,1,0:T(8,128)(2,1)S(1)}, u32[]{:S(2)}, u32[]{:S(2)}) async-start(bf16[128,24,128]{2,1,0:T(8,128)(2,1)} %bitcast.31), calls=%async_computation | async-start | bytes 1572864 | tf_op jit(solution)/shard_map/all_to_all | solution.py:653
  52.0 1.5 %collective-permute-start.5 = (bf16[432,192]{1,0:T(8,128)(2,1)}, bf16[432,192]{1,0:T(8,128)(2,1)S(1)}, u32[]{:S(2)}, u32[]{:S(2)}) collective-permute-start(bf16[432,192]{1,0:T(8,128)(2,1)} %get-tuple-element.38), channel_id=1, source_target_pairs={{0,4},{1,5},{2,6},{3,7},{4,8},{5,9},{6,10},{7,11},{8,12},{9,13},{1... | collective-permute-start | bytes 497672 | tf_op jit(solution)/shard_map/ppermute | solution.py:602
  53.5 3.4 %collective-permute-start.3 = (bf16[144,192]{1,0:T(8,128)(2,1)}, bf16[144,192]{1,0:T(8,128)(2,1)S(1)}, u32[]{:S(2)}, u32[]{:S(2)}) collective-permute-start(bf16[144,192]{1,0:T(8,128)(2,1)} %get-tuple-element.36), channel_id=1, source_target_pairs={{0,5},{1,6},{2,7},{3,4},{4,9},{5,10},{6,11},{7,8},{8,13},{9,14},{1... | collective-permute-start | bytes 165896 | tf_op jit(solution)/shard_map/ppermute | solution.py:602
  56.9 0.9 collective-permute-start.4
  57.8 17.2 %collective-permute-done.3 = bf16[144,192]{1,0:T(8,128)(2,1)S(1)} collective-permute-done((bf16[144,192]{1,0:T(8,128)(2,1)}, bf16[144,192]{1,0:T(8,128)(2,1)S(1)}, u32[]{:S(2)}, u32[]{:S(2)}) %collective-permute-start.3) | collective-permute-done | bytes 55328 | tf_op jit(solution)/shard_map/ppermute | solution.py:602
  75.0 0.0 collective-permute-done.4
  75.0 0.0 collective-permute-done.5
  75.0 1.9 %maximum_maximum_fusion = bf16[12,12,8,192]{3,2,1,0:T(8,128)(2,1)} fusion(bf16[9,6,8,192]{3,2,1,0:T(8,128)(2,1)} %bitcast.39, bf16[9,6,8,192]{3,2,1,0:T(8,128)(2,1)S(1)} %bitcast.40, bf16[3,6,8,192]{3,2,1,0:T(8,128)(2,1)S(1)} %bitcast.42, bf16[3,6,8,192]{3,2,1,0:T(8,128)(2,1)S(1)} %bitcast.41), kind=kLoop, calls=%fused_computation | loop fusion | flops 663552 | bytes 884736 | tf_op jit(solution)/shard_map/concatenate | solution.py:654
  76.9 0.0 all-to-all-done
  76.9 0.9 copy-done
  77.8 2.2 %sums.1 = (bf16[3072,128]{1,0:T(8,128)(2,1)}, s32[8,128]{1,0:T(8,128)}) custom-call(s32[1]{0:T(128)} %bitcast.core_ref, bf16[3072,128]{1,0:T(8,128)(2,1)} %bitcast.28), custom_call_target="tpu_custom_call" | custom-call | tf_op jit(solution)/shard_map/sums/pallas_call | solution.py:446
  80.0 20.3 %all_to_all.10 = bf16[64,48,128]{2,1,0:T(8,128)(2,1)S(1)} all-to-all(bf16[64,48,128]{2,1,0:T(8,128)(2,1)} %bitcast.33), channel_id=1, replica_groups={{0,2,4,6,8,10,12,14,16,18,20,22,24,26,28,30,32,34,36,38,40,42,44,46,48,..., dimensions={0} | all-to-all | bytes 1572864 | tf_op jit(solution)/shard_map/all_to_all | solution.py:665
  100.3 1.5 %collective-permute-start.6 = (bf16[64,48,128]{2,1,0:T(8,128)(2,1)S(1)}, bf16[64,48,128]{2,1,0:T(8,128)(2,1)S(1)}, u32[]{:S(2)}, u32[]{:S(2)}) collective-permute-start(bf16[64,48,128]{2,1,0:T(8,128)(2,1)S(1)} %all_to_all.10), channel_id=1, source_target_pairs={{0,1},{1,0},{2,3},{3,2},{4,5},{5,4},{6,7},{7,6},{8,9},{9,8},{10,11... | collective-permute-start | bytes 2359304 | tf_op jit(solution)/shard_map/ppermute | solution.py:668
  101.8 1.9 %collective-permute-done.6 = bf16[64,48,128]{2,1,0:T(8,128)(2,1)S(1)} collective-permute-done((bf16[64,48,128]{2,1,0:T(8,128)(2,1)S(1)}, bf16[64,48,128]{2,1,0:T(8,128)(2,1)S(1)}, u32[]{:S(2)}, u32[]{:S(2)}) %collective-permute-start.6) | collective-permute-done | bytes 786464 | tf_op jit(solution)/shard_map/ppermute | solution.py:668
  103.7 0.0 copy-done.1
  103.7 0.9 copy-done.2
  104.6 5.6 %spread.1 = (f32[6,32,3312]{2,1,0:T(8,128)}, f32[4,192]{1,0:T(4,128)}, f32[192]{0:T(256)}, f32[192]{0:T(256)}, f32[192,576]{1,0:T(8,128)}, /*index=5*/f32[576]{0:T(1024)}, f32[192,192]{1,0:T(8,128)}, f32[192]{0:T(256)}) custom-call(s32[8,128]{1,0:T(8,128)} %get-tuple-element.41.scal_ref, bf16[3072,128]{1,0:T(8,128)(2,1)} %bitcast.29, bf16[3072,128]{1,0:T(8,128)(2,1)} %bitcast.32), custom_call_target="tpu_custom_call" | custom-call | tf_op jit(solution)/shard_map/spread/pallas_call | solution.py:530
  (4 shorter events, 0.0 us)
Async XLA Ops:
  2.8 22.5 %collective-permute-start = (bf16[440,384]{1,0:T(8,128)(2,1)}, bf16[440,384]{1,0:T(8,128)(2,1)S(1)}, u32[]{:S(2)}, u32[]{:S(2)}) collective-permute-start(bf16[440,384]{1,0:T(8,128)(2,1)} %get-tuple-element.30), channel_id=1, source_target_pairs={{0,124},{1,125},{2,126},{3,127},{4,0},{5,1},{6,2},{7,3},{8,4},{9,5... | collective-permute-start | bytes 1013768 | tf_op jit(solution)/shard_map/ppermute | solution.py:602
  10.8 14.5 %collective-permute-start.1 = (bf16[152,384]{1,0:T(8,128)(2,1)}, bf16[152,384]{1,0:T(8,128)(2,1)S(1)}, u32[]{:S(2)}, u32[]{:S(2)}) collective-permute-start(bf16[152,384]{1,0:T(8,128)(2,1)} %get-tuple-element.31), channel_id=1, source_target_pairs={{0,3},{1,0},{2,1},{3,2},{4,7},{5,4},{6,5},{7,6},{8,11},{9,8},{10,9... | collective-permute-start | bytes 350216 | tf_op jit(solution)/shard_map/ppermute | solution.py:602
  11.8 13.6 %collective-permute-start.2 = (bf16[152,384]{1,0:T(8,128)(2,1)}, bf16[152,384]{1,0:T(8,128)(2,1)S(1)}, u32[]{:S(2)}, u32[]{:S(2)}) collective-permute-start(bf16[152,384]{1,0:T(8,128)(2,1)} %get-tuple-element.32), channel_id=1, source_target_pairs={{0,127},{1,124},{2,125},{3,126},{4,3},{5,0},{6,1},{7,2},{8,7},{9,4... | collective-permute-start | bytes 350216 | tf_op jit(solution)/shard_map/ppermute | solution.py:602
  25.4 0.6 copy-start.4
  25.4 0.7 copy-start.5
  25.4 0.8 copy-start.3
  46.9 30.0 %all-to-all-start = ((bf16[128,24,128]{2,1,0:T(8,128)(2,1)}), bf16[128,24,128]{2,1,0:T(8,128)(2,1)S(1)}, u32[]{:S(2)}, u32[]{:S(2)}) async-start(bf16[128,24,128]{2,1,0:T(8,128)(2,1)} %bitcast.31), calls=%async_computation | async-start | bytes 1572864 | tf_op jit(solution)/shard_map/all_to_all | solution.py:653
  52.0 23.0 %collective-permute-start.5 = (bf16[432,192]{1,0:T(8,128)(2,1)}, bf16[432,192]{1,0:T(8,128)(2,1)S(1)}, u32[]{:S(2)}, u32[]{:S(2)}) collective-permute-start(bf16[432,192]{1,0:T(8,128)(2,1)} %get-tuple-element.38), channel_id=1, source_target_pairs={{0,4},{1,5},{2,6},{3,7},{4,8},{5,9},{6,10},{7,11},{8,12},{9,13},{1... | collective-permute-start | bytes 497672 | tf_op jit(solution)/shard_map/ppermute | solution.py:602
  53.5 21.5 %collective-permute-start.3 = (bf16[144,192]{1,0:T(8,128)(2,1)}, bf16[144,192]{1,0:T(8,128)(2,1)S(1)}, u32[]{:S(2)}, u32[]{:S(2)}) collective-permute-start(bf16[144,192]{1,0:T(8,128)(2,1)} %get-tuple-element.36), channel_id=1, source_target_pairs={{0,5},{1,6},{2,7},{3,4},{4,9},{5,10},{6,11},{7,8},{8,13},{9,14},{1... | collective-permute-start | bytes 165896 | tf_op jit(solution)/shard_map/ppermute | solution.py:602
  56.9 18.1 %collective-permute-start.4 = (bf16[144,192]{1,0:T(8,128)(2,1)}, bf16[144,192]{1,0:T(8,128)(2,1)S(1)}, u32[]{:S(2)}, u32[]{:S(2)}) collective-permute-start(bf16[144,192]{1,0:T(8,128)(2,1)} %get-tuple-element.37), channel_id=1, source_target_pairs={{0,1},{1,2},{2,3},{3,0},{4,5},{5,6},{6,7},{7,4},{8,9},{9,10},{10,1... | collective-permute-start | bytes 165896 | tf_op jit(solution)/shard_map/ppermute | solution.py:602
  76.9 0.9 copy-start
  100.3 3.5 %copy-start.1 = (bf16[64,48,128]{2,1,0:T(8,128)(2,1)}, bf16[64,48,128]{2,1,0:T(8,128)(2,1)S(1)}, u32[]{:S(2)}) copy-start(bf16[64,48,128]{2,1,0:T(8,128)(2,1)S(1)} %all_to_all.10) | copy-start | bytes 2359300
  100.3 3.4 %collective-permute-start.6 = (bf16[64,48,128]{2,1,0:T(8,128)(2,1)S(1)}, bf16[64,48,128]{2,1,0:T(8,128)(2,1)S(1)}, u32[]{:S(2)}, u32[]{:S(2)}) collective-permute-start(bf16[64,48,128]{2,1,0:T(8,128)(2,1)S(1)} %all_to_all.10), channel_id=1, source_target_pairs={{0,1},{1,0},{2,3},{3,2},{4,5},{5,4},{6,7},{7,6},{8,9},{9,8},{10,11... | collective-permute-start | bytes 2359304 | tf_op jit(solution)/shard_map/ppermute | solution.py:668
  103.7 0.9 copy-start.2

commit v5 on v4

--- a/solution.py
+++ b/solution.py
@@ -474,6 +474,8 @@
     g,
     tails,
     p,
+    stage,
+    sems,
 ):
     core = scal_ref[0, 8]
     half = 64 * GATHER_ROWS
@@ -492,14 +494,17 @@
                 to = pl.multiple_of((q * 32 + kind) * 16, 16)
                 p[pl.ds(to, 9), :] = g[src : src + 9, :]
                 p[pl.ds(to + 9, 1), :] = tails[lat, e : e + 1, :]
-    for m in range(144):
-        k, q = m // 16, m % 16
-        lu, c = m // 72, m % 72
-        h, la = c // 12, c % 12
-        at = (((la // 6) * 2 + lu) * 6 + la % 6) * GROUP
-        tab_ref[h, :, at : at + 128] = p[pl.ds(q * 512 + k, 32, stride=16), :]
-        tail = p[pl.ds(q * 512 + 9, 32, stride=16), :]
-        tab_ref[h, :, at + 128 : at + GROUP] = tail[:, k * 10 : k * 10 + 10]
+    copies = []
+    for h in range(HEADS):
+        for m in range(24):
+            lu, la = m // 12, m % 12
+            k, q = divmod(lu * 72 + h * 12 + la, 16)
+            at = (((la // 6) * 2 + lu) * 6 + la % 6) * GROUP
+            stage[h, :, at : at + 128] = p[pl.ds(q * 512 + k, 32, stride=16), :]
+            tail = p[pl.ds(q * 512 + 9, 32, stride=16), :]
+            stage[h, :, at + 128 : at + GROUP] = tail[:, k * 10 : k * 10 + 10]
+        copies.append(pltpu.make_async_copy(stage.at[h], tab_ref.at[h], sems.at[h]))
+        copies[-1].start()
     weights = jnp.concatenate(
         [g[pl.ds(36 + k, 128, stride=GATHER_ROWS), :] for k in range(9)], axis=0
     )
@@ -514,6 +519,8 @@
     grad_bqkv = jnp.concatenate([small[6:7], small[7:8], small[8:9]], axis=1)
     bqkv_ref[...] = grad_bqkv.reshape(3 * WIDTH)
     bo_ref[...] = small[9:10].reshape(WIDTH)
+    for copy in copies:
+        copy.wait()
 
 
 def spread(own, other, scal):
@@ -535,13 +542,17 @@
             pl.BlockSpec(memory_space=pltpu.VMEM),
             pl.BlockSpec(memory_space=pltpu.VMEM),
         ],
-        out_specs=[pl.BlockSpec(memory_space=pltpu.VMEM)] * len(outs),
+        out_specs=[pl.BlockSpec(memory_space=pl.ANY)]
+        + [pl.BlockSpec(memory_space=pltpu.VMEM)] * (len(outs) - 1),
         scratch_shapes=[
             pltpu.VMEM((128 * GATHER_ROWS, 128), f32),
             pltpu.VMEM((4, 128, 128), f32),
             pltpu.VMEM((16 * 32 * 16, 128), f32),
+            pltpu.VMEM((HEADS, 32, POSITIONS), f32),
+            pltpu.SemaphoreType.DMA((HEADS,)),
         ],
         compiler_params=pltpu.CompilerParams(vmem_limit_bytes=VMEM),
+        cost_estimate=pl.CostEstimate(flops=10**10, bytes_accessed=10**7, transcendentals=0),
         name="spread",
     )(scal, own, other)
 
@@ -651,24 +662,26 @@
 
     root = math.sqrt(inputs.size // WIDTH * lax.axis_size("lon") * lax.axis_size("lat"))
     received = lax.all_to_all(send.reshape(128, SEND_ROWS, 128), BOTH, 0, 0)
+    core = (lax.axis_index("lat") % 2).reshape(1)
+    part, kinds = summed(received.reshape(128 * SEND_ROWS, 128), core, root)
+    same_core = [[d for d in range(128) if d % 2 == core] for core in range(2)]
+    mine = lax.all_to_all(
+        part.reshape(64, GATHER_ROWS, 128), BOTH, 0, 0, axis_index_groups=same_core
+    )
+    other = lax.ppermute(mine, BOTH, [(d, d ^ 1) for d in range(128)])
+    flat = (64 * GATHER_ROWS, 128)
+    table, grad_class, grad_gain, grad_nb, grad_wqkv, grad_bqkv, grad_wout, grad_bout = spread(
+        mine.reshape(flat), other.reshape(flat), kinds
+    )
+    table, east_back, south_back, diag_back = lax.optimization_barrier(
+        (table, east_back, south_back, diag_back)
+    )
     grad_x = jnp.concatenate(
         [
             jnp.concatenate([diag_back, south_back], axis=1),
             jnp.concatenate([east_back, own], axis=1),
         ],
         axis=0,
-    )
-    core = (lax.axis_index("lat") % 2).reshape(1)
-    part, kinds = summed(received.reshape(128 * SEND_ROWS, 128), core, root)
-    part, grad_x = lax.optimization_barrier((part, grad_x))
-    same_core = [[d for d in range(128) if d % 2 == core] for core in range(2)]
-    mine = lax.all_to_all(
-        part.reshape(64, GATHER_ROWS, 128), BOTH, 0, 0, axis_index_groups=same_core
-    )
-    other = lax.ppermute(mine, BOTH, [(d, d ^ 1) for d in range(128)])
-    flat = (64 * GATHER_ROWS, 128)
-    table, grad_class, grad_gain, grad_nb, grad_wqkv, grad_bqkv, grad_wout, grad_bout = spread(
-        mine.reshape(flat), other.reshape(flat), kinds
     )
 
     return (

time: 111 us -> 108 us (0.973)
  starting transfers between devices: 23.1 us -> 18.4 us
  waiting for transfers between devices: 21.4 us -> 24 us
    all_to_all x1, waiting for transfers between devices: 0.01 us -> 16.3 us  [shards(): received = lax.all_to_all(send.reshape(128, SEND_ROWS, 128), BOTH, 0, 0)]
    ppermute x6, waiting for transfers between devices: 19.4 us -> 6.8 us  [moved(): return lax.ppermute(array, BOTH, pairs)]
    ppermute x6, starting transfers between devices: 16.4 us -> 11.6 us  [moved(): return lax.ppermute(array, BOTH, pairs)]
    concatenate x1 -> x0, other arithmetic: 1.87 us -> none  [shards(): jnp.concatenate([jnp.concatenate([diag_back, south_back], axis=1), jnp.co...]
    unnamed x12 -> x20, local copies, waits for them, and re-layouts: 2.57 us -> 2.59 us
  transfers between devices with their start and end apart: 8 -> 8, of which waited for: 3 -> 5; matrix products, arithmetic and copies ran while one was open for 3% -> 1% of each run, Pallas kernels for 8% -> 13%
where the time goes in v5:
time: 108 us; the launch traced here: 107 us
  Pallas kernels  39 us (36%)
  waiting for transfers between devices  24 us (22%)
  blocking collectives  20.4 us (19%)
  starting transfers between devices  18.4 us (17%)
  local copies, waits for them, and re-layouts  2.59 us (2%)
  other arithmetic  2.17 us (2%)
    pallas_call x1, Pallas kernels, attend(): pl.pallas_call(window_kernel, grid=(8 // PER_STEP,), out_shape=[jax.Shape...  20.7 us
    all_to_all x1, blocking collectives, shards(): lax.all_to_all(part.reshape(64, GATHER_ROWS, 128), BOTH, 0, 0, axis_index...  20.4 us
    all_to_all x1, waiting for transfers between devices, shards(): received = lax.all_to_all(send.reshape(128, SEND_ROWS, 128), BOTH, 0, 0)  16.3 us
    ppermute x6, starting transfers between devices, moved(): return lax.ppermute(array, BOTH, pairs)  11.6 us
    pallas_call x1, Pallas kernels, expand_bias(): pl.pallas_call(bias_kernel, out_shape=jax.ShapeDtypeStruct((8, PAIRS, WIN...  8.38 us
    ppermute x6, waiting for transfers between devices, moved(): return lax.ppermute(array, BOTH, pairs)  6.8 us
    pallas_call x1, Pallas kernels, spread(): pl.pallas_call(spread_kernel, out_shape=[jax.ShapeDtypeStruct(o, f32) for...  5.48 us
    all_to_all x1, starting transfers between devices, shards(): received = lax.all_to_all(send.reshape(128, SEND_ROWS, 128), BOTH, 0, 0)  5.15 us
  transfers between devices with their start and end apart: 8, of which 5 were waited for; matrix products, arithmetic and copies ran while one was open for 1% of the time, Pallas kernels for 13%

profile of v5, /device:TPU:1, one launch (start us, length us, event | category | flops | bytes accessed | tf_op | source)
XLA Modules:
  0.0 107.2 jit_solution(10980104383908736137)
XLA Ops:
  0.6 2.2 %pack.1 = (bf16[440,384]{1,0:T(8,128)(2,1)}, bf16[152,384]{1,0:T(8,128)(2,1)}, bf16[152,384]{1,0:T(8,128)(2,1)}, f32[8,384]{1,0:T(8,128)}) custom-call(bf16[1152,192]{1,0:T(8,128)(2,1)} %bitcast.34, bf16[1152,192]{1,0:T(8,128)(2,1)} %bitcast.36, s32[12,12]{1,0:T(8,128)} %ids_ref.1), custom_call_target="tpu_custom_call" | custom-call | tf_op jit(solution)/shard_map/pack/pallas_call | solution.py:596
  2.8 8.0 %collective-permute-start = (bf16[440,384]{1,0:T(8,128)(2,1)}, bf16[440,384]{1,0:T(8,128)(2,1)S(1)}, u32[]{:S(2)}, u32[]{:S(2)}) collective-permute-start(bf16[440,384]{1,0:T(8,128)(2,1)} %get-tuple-element.32), channel_id=1, source_target_pairs={{0,124},{1,125},{2,126},{3,127},{4,0},{5,1},{6,2},{7,3},{8,4},{9,5... | collective-permute-start | bytes 1013768 | tf_op jit(solution)/shard_map/ppermute | solution.py:613
  10.8 1.0 collective-permute-start.1
  11.8 1.7 %collective-permute-start.2 = (bf16[152,384]{1,0:T(8,128)(2,1)}, bf16[152,384]{1,0:T(8,128)(2,1)S(1)}, u32[]{:S(2)}, u32[]{:S(2)}) collective-permute-start(bf16[152,384]{1,0:T(8,128)(2,1)} %get-tuple-element.34), channel_id=1, source_target_pairs={{0,127},{1,124},{2,125},{3,126},{4,3},{5,0},{6,1},{7,2},{8,7},{9,4... | collective-permute-start | bytes 350216 | tf_op jit(solution)/shard_map/ppermute | solution.py:613
  13.5 1.2 %pad_add_fusion.scal_ref = s32[9]{0:T(128)} fusion(s32[1]{0:T(128)} %bitcast.1, s32[8]{0:T(128)} %param.14), kind=kLoop, calls=%fused_computation.1 | loop fusion | flops 9 | bytes 72 | tf_op jit(solution)/shard_map/concatenate | solution.py:639
  14.7 8.4 %bias.1.b_ref = f32[8,864,144]{2,1,0:T(8,128)} custom-call(s32[9]{0:T(128)} %pad_add_fusion.scal_ref, f32[6,32,3312]{2,1,0:T(8,128)} %bitcast.30), custom_call_target="tpu_custom_call" | custom-call | flops 2000000000 | bytes 7000000 | tf_op jit(solution)/shard_map/bias/pallas_call | solution.py:113
  23.1 2.2 %collective-permute-done.1.s_ref = bf16[152,384]{1,0:T(8,128)(2,1)S(1)} collective-permute-done((bf16[152,384]{1,0:T(8,128)(2,1)}, bf16[152,384]{1,0:T(8,128)(2,1)S(1)}, u32[]{:S(2)}, u32[]{:S(2)}) %collective-permute-start.1) | collective-permute-done | bytes 116768 | tf_op jit(solution)/shard_map/ppermute | solution.py:613
  25.4 0.0 collective-permute-done.2.d_ref
  25.4 0.0 collective-permute-done.e_ref
  25.4 0.0 copy-start.4
  25.4 0.6 copy-done.6
  26.0 0.0 copy-done.7
  26.0 0.1 copy-done.4
  26.2 20.7 %windows.1 = (bf16[432,192]{1,0:T(8,128)(2,1)}, bf16[432,192]{1,0:T(8,128)(2,1)}, bf16[144,192]{1,0:T(8,128)(2,1)}, bf16[144,192]{1,0:T(8,128)(2,1)}, bf16[3072,128]{1,0:T(8,128)(2,1)}) custom-call(s32[9]{0:T(128)} %pad_add_fusion.scal_ref, bf16[1152,192]{1,0:T(8,128)(2,1)} %bitcast.35, bf16[1152,192]{1,0:T(8,128)(2,1)} %bitcast.37, ...), custom_call_target="tpu_custom_call" | custom-call | flops 4000000000 | bytes 8000000 | tf_op jit(solution)/shard_map/windows/pallas_call | solution.py:386
  46.9 0.0 copy-start.8
  46.9 5.1 %all-to-all-start = ((bf16[128,24,128]{2,1,0:T(8,128)(2,1)}), bf16[128,24,128]{2,1,0:T(8,128)(2,1)S(1)}, u32[]{:S(2)}, u32[]{:S(2)}) async-start(bf16[128,24,128]{2,1,0:T(8,128)(2,1)} %bitcast.31), calls=%async_computation | async-start | bytes 1572864 | tf_op jit(solution)/shard_map/all_to_all | solution.py:664
  52.1 16.3 %all-to-all-done = bf16[128,24,128]{2,1,0:T(8,128)(2,1)S(1)} async-done(((bf16[128,24,128]{2,1,0:T(8,128)(2,1)}), bf16[128,24,128]{2,1,0:T(8,128)(2,1)S(1)}, u32[]{:S(2)}, u32[]{:S(2)}) %all-to-all-start) | async-done | bytes 786464 | tf_op jit(solution)/shard_map/all_to_all | solution.py:664
  68.4 0.9 copy-done
  69.2 2.2 %sums.1 = (bf16[3072,128]{1,0:T(8,128)(2,1)}, s32[8,128]{1,0:T(8,128)}) custom-call(s32[1]{0:T(128)} %bitcast.core_ref, bf16[3072,128]{1,0:T(8,128)(2,1)} %bitcast.29), custom_call_target="tpu_custom_call" | custom-call | tf_op jit(solution)/shard_map/sums/pallas_call | solution.py:446
  71.5 20.4 %all_to_all.10 = bf16[64,48,128]{2,1,0:T(8,128)(2,1)S(1)} all-to-all(bf16[64,48,128]{2,1,0:T(8,128)(2,1)} %bitcast.33), channel_id=1, replica_groups={{0,2,4,6,8,10,12,14,16,18,20,22,24,26,28,30,32,34,36,38,40,42,44,46,48,..., dimensions={0} | all-to-all | bytes 1572864 | tf_op jit(solution)/shard_map/all_to_all | solution.py:668
  91.8 1.6 %collective-permute-start.3 = (bf16[64,48,128]{2,1,0:T(8,128)(2,1)S(1)}, bf16[64,48,128]{2,1,0:T(8,128)(2,1)S(1)}, u32[]{:S(2)}, u32[]{:S(2)}) collective-permute-start(bf16[64,48,128]{2,1,0:T(8,128)(2,1)S(1)} %all_to_all.10), channel_id=1, source_target_pairs={{0,1},{1,0},{2,3},{3,2},{4,5},{5,4},{6,7},{7,6},{8,9},{9,8},{10,11... | collective-permute-start | bytes 2359304 | tf_op jit(solution)/shard_map/ppermute | solution.py:671
  93.4 0.8 collective-permute-start.5
  94.2 0.0 collective-permute-start.6
  94.2 0.2 collective-permute-start.4
  94.4 0.9 collective-permute-done.3
  95.3 0.0 copy-done.1
  95.3 0.9 copy-done.3
  96.2 5.5 %spread.1 = (f32[6,32,3312]{2,1,0:T(8,128)}, f32[4,192]{1,0:T(4,128)}, f32[192]{0:T(256)}, f32[192]{0:T(256)}, f32[192,576]{1,0:T(8,128)}, /*index=5*/f32[576]{0:T(1024)}, f32[192,192]{1,0:T(8,128)}, f32[192]{0:T(256)}) custom-call(s32[8,128]{1,0:T(8,128)} %get-tuple-element.37.scal_ref, bf16[3072,128]{1,0:T(8,128)(2,1)} %bitcast.32, bf16[3072,128]{1,0:T(8,128)(2,1)} %bitcast.42), custom_call_target="tpu_custom_call" | custom-call | flops 10000000000 | bytes 10000000 | tf_op jit(solution)/shard_map/spread/pallas_call | solution.py:537
  101.7 0.0 collective-permute-done.5
  101.7 2.0 %collective-permute-done.6 = bf16[144,192]{1,0:T(8,128)(2,1)S(1)} collective-permute-done((bf16[144,192]{1,0:T(8,128)(2,1)S(1)}, bf16[144,192]{1,0:T(8,128)(2,1)S(1)}, u32[]{:S(2)}, u32[]{:S(2)}) %collective-permute-start.6) | collective-permute-done | bytes 55328 | tf_op jit(solution)/shard_map/ppermute | solution.py:613
  103.7 2.5 %collective-permute-done.4 = bf16[432,192]{1,0:T(8,128)(2,1)S(1)} collective-permute-done((bf16[432,192]{1,0:T(8,128)(2,1)S(1)}, bf16[432,192]{1,0:T(8,128)(2,1)S(1)}, u32[]{:S(2)}, u32[]{:S(2)}) %collective-permute-start.4) | collective-permute-done | bytes 165920 | tf_op jit(solution)/shard_map/ppermute | solution.py:613
  106.3 0.9 maximum_bitcast_fusion
  (12 shorter events, 0.0 us)
Async XLA Ops:
  2.8 22.5 %collective-permute-start = (bf16[440,384]{1,0:T(8,128)(2,1)}, bf16[440,384]{1,0:T(8,128)(2,1)S(1)}, u32[]{:S(2)}, u32[]{:S(2)}) collective-permute-start(bf16[440,384]{1,0:T(8,128)(2,1)} %get-tuple-element.32), channel_id=1, source_target_pairs={{0,124},{1,125},{2,126},{3,127},{4,0},{5,1},{6,2},{7,3},{8,4},{9,5... | collective-permute-start | bytes 1013768 | tf_op jit(solution)/shard_map/ppermute | solution.py:613
  10.8 14.5 %collective-permute-start.1 = (bf16[152,384]{1,0:T(8,128)(2,1)}, bf16[152,384]{1,0:T(8,128)(2,1)S(1)}, u32[]{:S(2)}, u32[]{:S(2)}) collective-permute-start(bf16[152,384]{1,0:T(8,128)(2,1)} %get-tuple-element.33), channel_id=1, source_target_pairs={{0,3},{1,0},{2,1},{3,2},{4,7},{5,4},{6,5},{7,6},{8,11},{9,8},{10,9... | collective-permute-start | bytes 350216 | tf_op jit(solution)/shard_map/ppermute | solution.py:613
  11.8 13.6 %collective-permute-start.2 = (bf16[152,384]{1,0:T(8,128)(2,1)}, bf16[152,384]{1,0:T(8,128)(2,1)S(1)}, u32[]{:S(2)}, u32[]{:S(2)}) collective-permute-start(bf16[152,384]{1,0:T(8,128)(2,1)} %get-tuple-element.34), channel_id=1, source_target_pairs={{0,127},{1,124},{2,125},{3,126},{4,3},{5,0},{6,1},{7,2},{8,7},{9,4... | collective-permute-start | bytes 350216 | tf_op jit(solution)/shard_map/ppermute | solution.py:613
  25.4 0.6 copy-start.6
  25.4 0.7 copy-start.7
  25.4 0.8 copy-start.4
  46.9 46.5 %copy-start.9 = (bf16[144,192]{1,0:T(8,128)(2,1)S(1)}, bf16[144,192]{1,0:T(8,128)(2,1)}, u32[]{:S(2)}) copy-start(bf16[144,192]{1,0:T(8,128)(2,1)} %get-tuple-element.41) | copy-start | bytes 165892
  46.9 47.3 %copy-start.8 = (bf16[144,192]{1,0:T(8,128)(2,1)S(1)}, bf16[144,192]{1,0:T(8,128)(2,1)}, u32[]{:S(2)}) copy-start(bf16[144,192]{1,0:T(8,128)(2,1)} %get-tuple-element.42) | copy-start | bytes 165892
  46.9 47.3 %copy-start.5 = (bf16[432,192]{1,0:T(8,128)(2,1)S(1)}, bf16[432,192]{1,0:T(8,128)(2,1)}, u32[]{:S(2)}) copy-start(bf16[432,192]{1,0:T(8,128)(2,1)} %get-tuple-element.40) | copy-start | bytes 497668
  46.9 21.4 %all-to-all-start = ((bf16[128,24,128]{2,1,0:T(8,128)(2,1)}), bf16[128,24,128]{2,1,0:T(8,128)(2,1)S(1)}, u32[]{:S(2)}, u32[]{:S(2)}) async-start(bf16[128,24,128]{2,1,0:T(8,128)(2,1)} %bitcast.31), calls=%async_computation | async-start | bytes 1572864 | tf_op jit(solution)/shard_map/all_to_all | solution.py:664
  68.3 0.9 copy-start
  91.8 3.5 %copy-start.1 = (bf16[64,48,128]{2,1,0:T(8,128)(2,1)}, bf16[64,48,128]{2,1,0:T(8,128)(2,1)S(1)}, u32[]{:S(2)}) copy-start(bf16[64,48,128]{2,1,0:T(8,128)(2,1)S(1)} %all_to_all.10) | copy-start | bytes 2359300
  91.8 3.5 %collective-permute-start.3 = (bf16[64,48,128]{2,1,0:T(8,128)(2,1)S(1)}, bf16[64,48,128]{2,1,0:T(8,128)(2,1)S(1)}, u32[]{:S(2)}, u32[]{:S(2)}) collective-permute-start(bf16[64,48,128]{2,1,0:T(8,128)(2,1)S(1)} %all_to_all.10), channel_id=1, source_target_pairs={{0,1},{1,0},{2,3},{3,2},{4,5},{5,4},{6,7},{7,6},{8,9},{9,8},{10,11... | collective-permute-start | bytes 2359304 | tf_op jit(solution)/shard_map/ppermute | solution.py:671
  93.4 8.3 %collective-permute-start.5 = (bf16[144,192]{1,0:T(8,128)(2,1)S(1)}, bf16[144,192]{1,0:T(8,128)(2,1)S(1)}, u32[]{:S(2)}, u32[]{:S(2)}) collective-permute-start(bf16[144,192]{1,0:T(8,128)(2,1)S(1)} %copy-done.9), channel_id=1, source_target_pairs={{0,1},{1,2},{2,3},{3,0},{4,5},{5,6},{6,7},{7,4},{8,9},{9,10},{10,1... | collective-permute-start | bytes 165896 | tf_op jit(solution)/shard_map/ppermute | solution.py:613
  94.2 9.5 %collective-permute-start.6 = (bf16[144,192]{1,0:T(8,128)(2,1)S(1)}, bf16[144,192]{1,0:T(8,128)(2,1)S(1)}, u32[]{:S(2)}, u32[]{:S(2)}) collective-permute-start(bf16[144,192]{1,0:T(8,128)(2,1)S(1)} %copy-done.8), channel_id=1, source_target_pairs={{0,5},{1,6},{2,7},{3,4},{4,9},{5,10},{6,11},{7,8},{8,13},{9,14},{1... | collective-permute-start | bytes 165896 | tf_op jit(solution)/shard_map/ppermute | solution.py:613
  94.2 12.0 %collective-permute-start.4 = (bf16[432,192]{1,0:T(8,128)(2,1)S(1)}, bf16[432,192]{1,0:T(8,128)(2,1)S(1)}, u32[]{:S(2)}, u32[]{:S(2)}) collective-permute-start(bf16[432,192]{1,0:T(8,128)(2,1)S(1)} %copy-done.5), channel_id=1, source_target_pairs={{0,4},{1,5},{2,6},{3,7},{4,8},{5,9},{6,10},{7,11},{8,12},{9,13},{1... | collective-permute-start | bytes 497672 | tf_op jit(solution)/shard_map/ppermute | solution.py:613
  95.3 0.9 copy-start.3
  96.2 10.0 %copy-start.2 = (bf16[432,192]{1,0:T(8,128)(2,1)S(1)}, bf16[432,192]{1,0:T(8,128)(2,1)}, u32[]{:S(2)}) copy-start(bf16[432,192]{1,0:T(8,128)(2,1)} %get-tuple-element.46) | copy-start | bytes 497668

commit v6 on v5

--- a/solution.py
+++ b/solution.py
@@ -21,7 +21,7 @@
 NORM_EPS = 1e-05
 LOG2E = 1.4426950408889634
 SCALE = HEAD_DIM ** (-0.5)
-VMEM = 56 * 1024 * 1024
+MIB = 1024 * 1024
 SEND_ROWS = 24
 GATHER_ROWS = 48
 BOTH = ("lon", "lat")
@@ -125,7 +125,7 @@
             pltpu.VMEM((8, PAIRS, WIN_TOKENS), f32),
             pltpu.SemaphoreType.DMA((8,)),
         ],
-        compiler_params=pltpu.CompilerParams(vmem_limit_bytes=VMEM),
+        compiler_params=pltpu.CompilerParams(vmem_limit_bytes=28 * MIB),
         cost_estimate=pl.CostEstimate(flops=2 * 10**9, bytes_accessed=7 * 10**6, transcendentals=0),
         name="bias",
     )(scal, table)
@@ -406,7 +406,7 @@
             pltpu.VMEM((128 * SEND_ROWS, 128), f32),
         ],
         compiler_params=pltpu.CompilerParams(
-            vmem_limit_bytes=VMEM, dimension_semantics=("arbitrary",)
+            vmem_limit_bytes=34 * MIB, dimension_semantics=("arbitrary",)
         ),
         cost_estimate=pl.CostEstimate(flops=4 * 10**9, bytes_accessed=8 * 10**6, transcendentals=10**6),
         name="windows",
@@ -454,7 +454,7 @@
             pl.BlockSpec(memory_space=pltpu.VMEM),
         ],
         out_specs=[pl.BlockSpec(memory_space=pltpu.VMEM)] * 2,
-        compiler_params=pltpu.CompilerParams(vmem_limit_bytes=VMEM),
+        compiler_params=pltpu.CompilerParams(vmem_limit_bytes=10 * MIB),
         name="sums",
     )(core, received)
 
@@ -551,8 +551,8 @@
             pltpu.VMEM((HEADS, 32, POSITIONS), f32),
             pltpu.SemaphoreType.DMA((HEADS,)),
         ],
-        compiler_params=pltpu.CompilerParams(vmem_limit_bytes=VMEM),
-        cost_estimate=pl.CostEstimate(flops=10**10, bytes_accessed=10**7, transcendentals=0),
+        compiler_params=pltpu.CompilerParams(vmem_limit_bytes=24 * MIB),
+        cost_estimate=pl.CostEstimate(flops=10**9, bytes_accessed=10**7, transcendentals=0),
         name="spread",
     )(scal, own, other)
 
@@ -598,7 +598,7 @@
         out_shape=[jax.ShapeDtypeStruct(*o) for o in shapes],
         in_specs=[pl.BlockSpec(memory_space=pltpu.VMEM)] * 3,
         out_specs=[pl.BlockSpec(memory_space=pltpu.VMEM)] * 4,
-        compiler_params=pltpu.CompilerParams(vmem_limit_bytes=VMEM),
+        compiler_params=pltpu.CompilerParams(vmem_limit_bytes=56 * MIB),
         name="pack",
     )(x, u, ids)
 
@@ -668,13 +668,13 @@
     mine = lax.all_to_all(
         part.reshape(64, GATHER_ROWS, 128), BOTH, 0, 0, axis_index_groups=same_core
     )
+    mine, east_back, south_back, diag_back = lax.optimization_barrier(
+        (mine, east_back, south_back, diag_back)
+    )
     other = lax.ppermute(mine, BOTH, [(d, d ^ 1) for d in range(128)])
     flat = (64 * GATHER_ROWS, 128)
     table, grad_class, grad_gain, grad_nb, grad_wqkv, grad_bqkv, grad_wout, grad_bout = spread(
         mine.reshape(flat), other.reshape(flat), kinds
-    )
-    table, east_back, south_back, diag_back = lax.optimization_barrier(
-        (table, east_back, south_back, diag_back)
     )
     grad_x = jnp.concatenate(
         [

time: 108 us -> 102 us (0.944)
  blocking collectives: 20.4 us -> 0 us
  waiting for transfers between devices: 24 us -> 36.3 us
  starting transfers between devices: 18.4 us -> 25.8 us
  Pallas kernels: 39 us -> 35.2 us
    all_to_all x1 -> x0, blocking collectives: 20.4 us -> none  [shards(): lax.all_to_all(part.reshape(64, GATHER_ROWS, 128), BOTH, 0, 0, axis_index...]
    ppermute x6, waiting for transfers between devices: 6.8 us -> 18.7 us  [moved(): return lax.ppermute(array, BOTH, pairs)]
    all_to_all x0 -> x1, starting transfers between devices: none -> 4.99 us  [shards(): lax.all_to_all(part.reshape(64, GATHER_ROWS, 128), BOTH, 0, 0, axis_index...]
    ppermute x6, starting transfers between devices: 11.6 us -> 15.6 us  [moved(): return lax.ppermute(array, BOTH, pairs)]
    pallas_call x1, Pallas kernels: 20.7 us -> 18.9 us  [attend(): pl.pallas_call(window_kernel, grid=(8 // PER_STEP,), out_shape=[jax.Shape...]
    ppermute x1, starting transfers between devices: 1.58 us -> 0.01 us  [shards(): other = lax.ppermute(mine, BOTH, [(d, d ^ 1) for d in range(128)])]
    pallas_call x1, Pallas kernels: 2.22 us -> 1.08 us  [summed(): pl.pallas_call(body, out_shape=[jax.ShapeDtypeStruct((64 * GATHER_ROWS, 1...]
  transfers between devices with their start and end apart: 8 -> 9, of which waited for: 5 -> 5; matrix products, arithmetic and copies ran while one was open for 1% -> 2% of each run, Pallas kernels for 13% -> 8%
where the time goes in v6:
time: 102 us
  waiting for transfers between devices  36.3 us (36%)
  Pallas kernels  35.2 us (35%)
  starting transfers between devices  25.8 us (25%)
  local copies, waits for them, and re-layouts  1.77 us (2%)
  other arithmetic  1.66 us (2%)
    pallas_call x1, Pallas kernels, attend(): pl.pallas_call(window_kernel, grid=(8 // PER_STEP,), out_shape=[jax.Shape...  18.9 us
    ppermute x6, waiting for transfers between devices, moved(): return lax.ppermute(array, BOTH, pairs)  18.7 us
    all_to_all x1, waiting for transfers between devices, shards(): received = lax.all_to_all(send.reshape(128, SEND_ROWS, 128), BOTH, 0, 0)  16.3 us
    ppermute x6, starting transfers between devices, moved(): return lax.ppermute(array, BOTH, pairs)  15.6 us
    pallas_call x1, Pallas kernels, expand_bias(): pl.pallas_call(bias_kernel, out_shape=jax.ShapeDtypeStruct((8, PAIRS, WIN...  8.41 us
    all_to_all x1, starting transfers between devices, shards(): received = lax.all_to_all(send.reshape(128, SEND_ROWS, 128), BOTH, 0, 0)  5.17 us
    all_to_all x1, starting transfers between devices, shards(): lax.all_to_all(part.reshape(64, GATHER_ROWS, 128), BOTH, 0, 0, axis_index...  4.99 us
    pallas_call x1, Pallas kernels, spread(): pl.pallas_call(spread_kernel, out_shape=[jax.ShapeDtypeStruct(o, f32) for...  4.66 us
  transfers between devices with their start and end apart: 9, of which 5 were waited for; matrix products, arithmetic and copies ran while one was open for 2% of the time, Pallas kernels for 8%

profile of v6, /device:TPU:1, one launch (start us, length us, event | category | flops | bytes accessed | tf_op | source)
XLA Modules:
  0.0 101.7 jit_solution(16891817855050421796)
XLA Ops:
  0.6 2.2 %pack.1 = (bf16[440,384]{1,0:T(8,128)(2,1)}, bf16[152,384]{1,0:T(8,128)(2,1)}, bf16[152,384]{1,0:T(8,128)(2,1)}, f32[8,384]{1,0:T(8,128)}) custom-call(bf16[1152,192]{1,0:T(8,128)(2,1)} %bitcast.32, bf16[1152,192]{1,0:T(8,128)(2,1)} %bitcast.34, s32[12,12]{1,0:T(8,128)} %ids_ref.1), custom_call_target="tpu_custom_call" | custom-call | tf_op jit(solution)/shard_map/pack/pallas_call | solution.py:596
  2.8 8.0 %collective-permute-start = (bf16[440,384]{1,0:T(8,128)(2,1)}, bf16[440,384]{1,0:T(8,128)(2,1)S(1)}, u32[]{:S(2)}, u32[]{:S(2)}) collective-permute-start(bf16[440,384]{1,0:T(8,128)(2,1)} %get-tuple-element.32), channel_id=1, source_target_pairs={{0,124},{1,125},{2,126},{3,127},{4,0},{5,1},{6,2},{7,3},{8,4},{9,5... | collective-permute-start | bytes 1013768 | tf_op jit(solution)/shard_map/ppermute | solution.py:613
  10.8 1.0 collective-permute-start.1
  11.8 1.7 %collective-permute-start.2 = (bf16[152,384]{1,0:T(8,128)(2,1)}, bf16[152,384]{1,0:T(8,128)(2,1)S(1)}, u32[]{:S(2)}, u32[]{:S(2)}) collective-permute-start(bf16[152,384]{1,0:T(8,128)(2,1)} %get-tuple-element.34), channel_id=1, source_target_pairs={{0,127},{1,124},{2,125},{3,126},{4,3},{5,0},{6,1},{7,2},{8,7},{9,4... | collective-permute-start | bytes 350216 | tf_op jit(solution)/shard_map/ppermute | solution.py:613
  13.5 0.7 pad_add_fusion.scal_ref
  14.2 1.7 %copy-done = f32[32,6,3312]{2,0,1:T(8,128)S(1)} copy-done((f32[32,6,3312]{2,0,1:T(8,128)S(1)}, f32[32,6,3312]{2,0,1:T(8,128)}, u32[]{:S(2)}) %copy-start) | copy-done | bytes 2543640
  15.9 0.0 copy-start.5
  16.0 0.0 copy-start.6
  16.0 0.0 copy-start.7
  16.0 0.0 copy-start.8
  16.0 0.0 copy-start.9
  16.0 8.4 %bias.1.b_ref = f32[8,864,144]{2,1,0:T(8,128)S(1)} custom-call(s32[9]{0:T(128)S(1)} %pad_add_fusion.scal_ref, f32[6,32,3312]{2,1,0:T(8,128)S(1)} %bitcast.30), custom_call_target="tpu_custom_call" | custom-call | flops 2000000000 | bytes 7000000 | tf_op jit(solution)/shard_map/bias/pallas_call | solution.py:113
  24.4 0.9 collective-permute-done.1.s_ref
  25.4 0.0 collective-permute-done.2.d_ref
  25.4 0.0 collective-permute-done.e_ref
  25.4 0.0 copy-done.1
  25.5 18.9 %windows.1 = (bf16[432,192]{1,0:T(8,128)(2,1)S(1)}, bf16[432,192]{1,0:T(8,128)(2,1)S(1)}, bf16[144,192]{1,0:T(8,128)(2,1)S(1)}, bf16[144,192]{1,0:T(8,128)(2,1)S(1)}, bf16[3072,128]{1,0:T(8,128)(2,1)}) custom-call(s32[9]{0:T(128)S(1)} %pad_add_fusion.scal_ref, bf16[1152,192]{1,0:T(8,128)(2,1)S(1)} %bitcast.33, bf16[1152,192]{1,0:T(8,128)(2,1)S(1)} %bitcast.35, ...), custom_call_target="tpu_custom_call" | custom-call | flops 4000000000 | bytes 8000000 | tf_op jit(solution)/shard_map/windows/pallas_call | solution.py:386
  44.3 5.2 %all-to-all-start = ((bf16[128,24,128]{2,1,0:T(8,128)(2,1)}), bf16[128,24,128]{2,1,0:T(8,128)(2,1)S(1)}, u32[]{:S(2)}, u32[]{:S(2)}) async-start(bf16[128,24,128]{2,1,0:T(8,128)(2,1)} %bitcast.15), calls=%async_computation | async-start | bytes 1572864 | tf_op jit(solution)/shard_map/all_to_all | solution.py:664
  49.5 16.3 %all-to-all-done = bf16[128,24,128]{2,1,0:T(8,128)(2,1)S(1)} async-done(((bf16[128,24,128]{2,1,0:T(8,128)(2,1)}), bf16[128,24,128]{2,1,0:T(8,128)(2,1)S(1)}, u32[]{:S(2)}, u32[]{:S(2)}) %all-to-all-start) | async-done | bytes 786464 | tf_op jit(solution)/shard_map/all_to_all | solution.py:664
  65.8 1.1 %sums.1 = (bf16[3072,128]{1,0:T(8,128)(2,1)}, s32[8,128]{1,0:T(8,128)S(1)}) custom-call(s32[1]{0:T(128)} %bitcast.core_ref, bf16[3072,128]{1,0:T(8,128)(2,1)S(1)} %bitcast.29), custom_call_target="tpu_custom_call" | custom-call | tf_op jit(solution)/shard_map/sums/pallas_call | solution.py:446
  66.9 5.0 %all-to-all-start.1 = ((bf16[64,48,128]{2,1,0:T(8,128)(2,1)}), bf16[64,48,128]{2,1,0:T(8,128)(2,1)S(1)}, u32[]{:S(2)}, u32[]{:S(2)}) async-start(bf16[64,48,128]{2,1,0:T(8,128)(2,1)} %bitcast.17), calls=%async_computation.1 | async-start | bytes 1572864 | tf_op jit(solution)/shard_map/all_to_all | solution.py:668
  71.9 1.1 %collective-permute-start.3 = (bf16[432,192]{1,0:T(8,128)(2,1)S(1)}, bf16[432,192]{1,0:T(8,128)(2,1)S(1)}, u32[]{:S(2)}, u32[]{:S(2)}) collective-permute-start(bf16[432,192]{1,0:T(8,128)(2,1)S(1)} %get-tuple-element.38), channel_id=1, source_target_pairs={{0,4},{1,5},{2,6},{3,7},{4,8},{5,9},{6,10},{7,11},{8,12},{9,13},{1... | collective-permute-start | bytes 497672 | tf_op jit(solution)/shard_map/ppermute | solution.py:613
  72.9 3.6 %collective-permute-start.4 = (bf16[144,192]{1,0:T(8,128)(2,1)S(1)}, bf16[144,192]{1,0:T(8,128)(2,1)S(1)}, u32[]{:S(2)}, u32[]{:S(2)}) collective-permute-start(bf16[144,192]{1,0:T(8,128)(2,1)S(1)} %get-tuple-element.39), channel_id=1, source_target_pairs={{0,1},{1,2},{2,3},{3,0},{4,5},{5,6},{6,7},{7,4},{8,9},{9,10},{10,1... | collective-permute-start | bytes 165896 | tf_op jit(solution)/shard_map/ppermute | solution.py:613
  76.5 0.3 collective-permute-start.5
  76.8 9.1 %collective-permute-done.4 = bf16[144,192]{1,0:T(8,128)(2,1)S(1)} collective-permute-done((bf16[144,192]{1,0:T(8,128)(2,1)S(1)}, bf16[144,192]{1,0:T(8,128)(2,1)S(1)}, u32[]{:S(2)}, u32[]{:S(2)}) %collective-permute-start.4) | collective-permute-done | bytes 55328 | tf_op jit(solution)/shard_map/ppermute | solution.py:613
  85.9 8.7 %collective-permute-done.5 = bf16[144,192]{1,0:T(8,128)(2,1)S(1)} collective-permute-done((bf16[144,192]{1,0:T(8,128)(2,1)S(1)}, bf16[144,192]{1,0:T(8,128)(2,1)S(1)}, u32[]{:S(2)}, u32[]{:S(2)}) %collective-permute-start.5) | collective-permute-done | bytes 55328 | tf_op jit(solution)/shard_map/ppermute | solution.py:613
  94.6 0.0 collective-permute-done.3
  94.6 0.0 all-to-all-done.1
  94.6 0.0 collective-permute-start.6
  94.6 0.9 maximum_bitcast_fusion
  95.6 1.3 %collective-permute-done.6 = bf16[64,48,128]{2,1,0:T(8,128)(2,1)S(1)} collective-permute-done((bf16[64,48,128]{2,1,0:T(8,128)(2,1)S(1)}, bf16[64,48,128]{2,1,0:T(8,128)(2,1)S(1)}, u32[]{:S(2)}, u32[]{:S(2)}) %collective-permute-start.6) | collective-permute-done | bytes 786464 | tf_op jit(solution)/shard_map/ppermute | solution.py:674
  96.9 4.7 %spread.1 = (f32[6,32,3312]{2,1,0:T(8,128)}, f32[4,192]{1,0:T(4,128)}, f32[192]{0:T(256)}, f32[192]{0:T(256)}, f32[192,576]{1,0:T(8,128)}, /*index=5*/f32[576]{0:T(1024)}, f32[192,192]{1,0:T(8,128)}, f32[192]{0:T(256)}) custom-call(s32[8,128]{1,0:T(8,128)S(1)} %get-tuple-element.45.scal_ref, bf16[3072,128]{1,0:T(8,128)(2,1)S(1)} %bitcast.31, ...), custom_call_target="tpu_custom_call" | custom-call | flops 1000000000 | bytes 10000000 | tf_op jit(solution)/shard_map/spread/pallas_call | solution.py:537
  (13 shorter events, 0.0 us)
Async XLA Ops:
  2.8 22.5 %collective-permute-start = (bf16[440,384]{1,0:T(8,128)(2,1)}, bf16[440,384]{1,0:T(8,128)(2,1)S(1)}, u32[]{:S(2)}, u32[]{:S(2)}) collective-permute-start(bf16[440,384]{1,0:T(8,128)(2,1)} %get-tuple-element.32), channel_id=1, source_target_pairs={{0,124},{1,125},{2,126},{3,127},{4,0},{5,1},{6,2},{7,3},{8,4},{9,5... | collective-permute-start | bytes 1013768 | tf_op jit(solution)/shard_map/ppermute | solution.py:613
  10.8 14.5 %collective-permute-start.1 = (bf16[152,384]{1,0:T(8,128)(2,1)}, bf16[152,384]{1,0:T(8,128)(2,1)S(1)}, u32[]{:S(2)}, u32[]{:S(2)}) collective-permute-start(bf16[152,384]{1,0:T(8,128)(2,1)} %get-tuple-element.33), channel_id=1, source_target_pairs={{0,3},{1,0},{2,1},{3,2},{4,7},{5,4},{6,5},{7,6},{8,11},{9,8},{10,9... | collective-permute-start | bytes 350216 | tf_op jit(solution)/shard_map/ppermute | solution.py:613
  11.8 13.6 %collective-permute-start.2 = (bf16[152,384]{1,0:T(8,128)(2,1)}, bf16[152,384]{1,0:T(8,128)(2,1)S(1)}, u32[]{:S(2)}, u32[]{:S(2)}) collective-permute-start(bf16[152,384]{1,0:T(8,128)(2,1)} %get-tuple-element.34), channel_id=1, source_target_pairs={{0,127},{1,124},{2,125},{3,126},{4,3},{5,0},{6,1},{7,2},{8,7},{9,4... | collective-permute-start | bytes 350216 | tf_op jit(solution)/shard_map/ppermute | solution.py:613
  14.2 1.7 %copy-start = (f32[32,6,3312]{2,0,1:T(8,128)S(1)}, f32[32,6,3312]{2,0,1:T(8,128)}, u32[]{:S(2)}) copy-start(f32[32,6,3312]{2,0,1:T(8,128)} %param.21) | copy-start | bytes 7630852
  15.9 9.4 %copy-start.1 = (bf16[1,8,12,12,192]{4,1,3,2,0:T(8,128)(2,1)S(1)}, bf16[1,8,12,12,192]{4,1,3,2,0:T(8,128)(2,1)}, u32[]{:S(2)}) copy-start(bf16[1,8,12,12,192]{4,1,3,2,0:T(8,128)(2,1)} %param.11) | copy-start | bytes 1327108
  15.9 9.4 %copy-start.2 = (bf16[1,8,12,12,192]{4,1,3,2,0:T(8,128)(2,1)S(1)}, bf16[1,8,12,12,192]{4,1,3,2,0:T(8,128)(2,1)}, u32[]{:S(2)}) copy-start(bf16[1,8,12,12,192]{4,1,3,2,0:T(8,128)(2,1)} %param.12) | copy-start | bytes 1327108
  15.9 9.4 %copy-start.3 = (bf16[192,576]{1,0:T(8,128)(2,1)S(1)}, bf16[192,576]{1,0:T(8,128)(2,1)}, u32[]{:S(2)}) copy-start(bf16[192,576]{1,0:T(8,128)(2,1)} %w_ref.1) | copy-start | bytes 663556
  15.9 9.4 %copy-start.4 = (bf16[192,192]{1,0:T(8,128)(2,1)S(1)}, bf16[192,192]{1,0:T(8,128)(2,1)}, u32[]{:S(2)}) copy-start(bf16[192,192]{1,0:T(8,128)(2,1)} %wo_ref.1) | copy-start | bytes 221188
  15.9 9.5 %copy-start.5 = (f32[8,384]{1,0:T(8,128)S(1)}, f32[8,384]{1,0:T(8,128)}, u32[]{:S(2)}) copy-start(f32[8,384]{1,0:T(8,128)} %get-tuple-element.35.ids_ref) | copy-start | bytes 36868
  16.0 9.5 %copy-start.6 = (f32[4,192]{1,0:T(4,128)S(1)}, f32[4,192]{1,0:T(4,128)}, u32[]{:S(2)}) copy-start(f32[4,192]{1,0:T(4,128)} %ct_ref.1) | copy-start | bytes 9220
  16.0 9.5 %copy-start.7 = (f32[576]{0:T(1024)S(1)}, f32[576]{0:T(1024)}, u32[]{:S(2)}) copy-start(f32[576]{0:T(1024)} %bq_ref.1) | copy-start | bytes 6916
  16.0 9.4 %copy-start.8 = (f32[192]{0:T(256)S(1)}, f32[192]{0:T(256)}, u32[]{:S(2)}) copy-start(f32[192]{0:T(256)} %param.16) | copy-start | bytes 2308
  16.0 9.4 %copy-start.9 = (f32[192]{0:T(256)S(1)}, f32[192]{0:T(256)}, u32[]{:S(2)}) copy-start(f32[192]{0:T(256)} %param.17) | copy-start | bytes 2308
  44.3 21.4 %all-to-all-start = ((bf16[128,24,128]{2,1,0:T(8,128)(2,1)}), bf16[128,24,128]{2,1,0:T(8,128)(2,1)S(1)}, u32[]{:S(2)}, u32[]{:S(2)}) async-start(bf16[128,24,128]{2,1,0:T(8,128)(2,1)} %bitcast.15), calls=%async_computation | async-start | bytes 1572864 | tf_op jit(solution)/shard_map/all_to_all | solution.py:664
  66.9 27.7 %all-to-all-start.1 = ((bf16[64,48,128]{2,1,0:T(8,128)(2,1)}), bf16[64,48,128]{2,1,0:T(8,128)(2,1)S(1)}, u32[]{:S(2)}, u32[]{:S(2)}) async-start(bf16[64,48,128]{2,1,0:T(8,128)(2,1)} %bitcast.17), calls=%async_computation.1 | async-start | bytes 1572864 | tf_op jit(solution)/shard_map/all_to_all | solution.py:668
  71.9 22.7 %collective-permute-start.3 = (bf16[432,192]{1,0:T(8,128)(2,1)S(1)}, bf16[432,192]{1,0:T(8,128)(2,1)S(1)}, u32[]{:S(2)}, u32[]{:S(2)}) collective-permute-start(bf16[432,192]{1,0:T(8,128)(2,1)S(1)} %get-tuple-element.38), channel_id=1, source_target_pairs={{0,4},{1,5},{2,6},{3,7},{4,8},{5,9},{6,10},{7,11},{8,12},{9,13},{1... | collective-permute-start | bytes 497672 | tf_op jit(solution)/shard_map/ppermute | solution.py:613
  72.9 13.0 %collective-permute-start.4 = (bf16[144,192]{1,0:T(8,128)(2,1)S(1)}, bf16[144,192]{1,0:T(8,128)(2,1)S(1)}, u32[]{:S(2)}, u32[]{:S(2)}) collective-permute-start(bf16[144,192]{1,0:T(8,128)(2,1)S(1)} %get-tuple-element.39), channel_id=1, source_target_pairs={{0,1},{1,2},{2,3},{3,0},{4,5},{5,6},{6,7},{7,4},{8,9},{9,10},{10,1... | collective-permute-start | bytes 165896 | tf_op jit(solution)/shard_map/ppermute | solution.py:613
  76.5 18.1 %collective-permute-start.5 = (bf16[144,192]{1,0:T(8,128)(2,1)S(1)}, bf16[144,192]{1,0:T(8,128)(2,1)S(1)}, u32[]{:S(2)}, u32[]{:S(2)}) collective-permute-start(bf16[144,192]{1,0:T(8,128)(2,1)S(1)} %get-tuple-element.40), channel_id=1, source_target_pairs={{0,5},{1,6},{2,7},{3,4},{4,9},{5,10},{6,11},{7,8},{8,13},{9,14},{1... | collective-permute-start | bytes 165896 | tf_op jit(solution)/shard_map/ppermute | solution.py:613
  94.6 2.3 %collective-permute-start.6 = (bf16[64,48,128]{2,1,0:T(8,128)(2,1)S(1)}, bf16[64,48,128]{2,1,0:T(8,128)(2,1)S(1)}, u32[]{:S(2)}, u32[]{:S(2)}) collective-permute-start(bf16[64,48,128]{2,1,0:T(8,128)(2,1)S(1)} %all-to-all-done.1), channel_id=1, source_target_pairs={{0,1},{1,0},{2,3},{3,2},{4,5},{5,4},{6,7},{7,6},{8,9},{9,8},{10,11... | collective-permute-start | bytes 2359304 | tf_op jit(solution)/shard_map/ppermute | solution.py:674

commit v7 on v6

--- a/solution.py
+++ b/solution.py
@@ -552,7 +552,7 @@
             pltpu.SemaphoreType.DMA((HEADS,)),
         ],
         compiler_params=pltpu.CompilerParams(vmem_limit_bytes=24 * MIB),
-        cost_estimate=pl.CostEstimate(flops=10**9, bytes_accessed=10**7, transcendentals=0),
+        cost_estimate=pl.CostEstimate(flops=10**10, bytes_accessed=10**7, transcendentals=0),
         name="spread",
     )(scal, own, other)
 
@@ -655,11 +655,6 @@
         out_weight,
         bias,
     )
-    east_back = moved(east_out, 1, 0).reshape(9, 6, 8, WIDTH)
-    south_back = moved(south_out, 0, 1).reshape(3, 6, 8, WIDTH)
-    diag_back = moved(diag_out, 1, 1).reshape(3, 6, 8, WIDTH)
-    own = own.reshape(9, 6, 8, WIDTH)
-
     root = math.sqrt(inputs.size // WIDTH * lax.axis_size("lon") * lax.axis_size("lat"))
     received = lax.all_to_all(send.reshape(128, SEND_ROWS, 128), BOTH, 0, 0)
     core = (lax.axis_index("lat") % 2).reshape(1)
@@ -668,13 +663,20 @@
     mine = lax.all_to_all(
         part.reshape(64, GATHER_ROWS, 128), BOTH, 0, 0, axis_index_groups=same_core
     )
-    mine, east_back, south_back, diag_back = lax.optimization_barrier(
-        (mine, east_back, south_back, diag_back)
-    )
     other = lax.ppermute(mine, BOTH, [(d, d ^ 1) for d in range(128)])
+    other, east_out, south_out, diag_out = lax.optimization_barrier(
+        (other, east_out, south_out, diag_out)
+    )
+    east_back = moved(east_out, 1, 0).reshape(9, 6, 8, WIDTH)
+    south_back = moved(south_out, 0, 1).reshape(3, 6, 8, WIDTH)
+    diag_back = moved(diag_out, 1, 1).reshape(3, 6, 8, WIDTH)
+    own = own.reshape(9, 6, 8, WIDTH)
     flat = (64 * GATHER_ROWS, 128)
     table, grad_class, grad_gain, grad_nb, grad_wqkv, grad_bqkv, grad_wout, grad_bout = spread(
         mine.reshape(flat), other.reshape(flat), kinds
+    )
+    table, east_back, south_back, diag_back = lax.optimization_barrier(
+        (table, east_back, south_back, diag_back)
     )
     grad_x = jnp.concatenate(
         [

time: 102 us -> 104 us (1.020)
  blocking collectives: 0 us -> 20.4 us
  waiting for transfers between devices: 36.3 us -> 26.3 us
  starting transfers between devices: 25.8 us -> 18.6 us
    all_to_all x0 -> x1, blocking collectives: none -> 20.4 us  [shards(): lax.all_to_all(part.reshape(64, GATHER_ROWS, 128), BOTH, 0, 0, axis_index...]
    ppermute x6, waiting for transfers between devices: 18.7 us -> 8.1 us  [moved(): return lax.ppermute(array, BOTH, pairs)]
    all_to_all x1 -> x0, starting transfers between devices: 4.99 us -> none  [shards(): lax.all_to_all(part.reshape(64, GATHER_ROWS, 128), BOTH, 0, 0, axis_index...]
    ppermute x6, starting transfers between devices: 15.6 us -> 11.9 us  [moved(): return lax.ppermute(array, BOTH, pairs)]
    ppermute x1, starting transfers between devices: 0.01 us -> 1.54 us  [shards(): other = lax.ppermute(mine, BOTH, [(d, d ^ 1) for d in range(128)])]
  transfers between devices with their start and end apart: 9 -> 8, of which waited for: 5 -> 5; matrix products, arithmetic and copies ran while one was open for 2% -> 1% of each run, Pallas kernels for 8% -> 13%
where the time goes in v7:
time: 104 us
  Pallas kernels  34.4 us (33%)
  waiting for transfers between devices  26.3 us (25%)
  blocking collectives  20.4 us (20%)
  starting transfers between devices  18.6 us (18%)
  local copies, waits for them, and re-layouts  1.77 us (2%)
  other arithmetic  1.66 us (2%)
    all_to_all x1, blocking collectives, shards(): lax.all_to_all(part.reshape(64, GATHER_ROWS, 128), BOTH, 0, 0, axis_index...  20.4 us
    pallas_call x1, Pallas kernels, attend(): pl.pallas_call(window_kernel, grid=(8 // PER_STEP,), out_shape=[jax.Shape...  18.9 us
    all_to_all x1, waiting for transfers between devices, shards(): received = lax.all_to_all(send.reshape(128, SEND_ROWS, 128), BOTH, 0, 0)  16.3 us
    ppermute x6, starting transfers between devices, moved(): return lax.ppermute(array, BOTH, pairs)  11.9 us
    pallas_call x1, Pallas kernels, expand_bias(): pl.pallas_call(bias_kernel, out_shape=jax.ShapeDtypeStruct((8, PAIRS, WIN...  8.41 us
    ppermute x6, waiting for transfers between devices, moved(): return lax.ppermute(array, BOTH, pairs)  8.1 us
    all_to_all x1, starting transfers between devices, shards(): received = lax.all_to_all(send.reshape(128, SEND_ROWS, 128), BOTH, 0, 0)  5.17 us
    pallas_call x1, Pallas kernels, spread(): pl.pallas_call(spread_kernel, out_shape=[jax.ShapeDtypeStruct(o, f32) for...  4.66 us
  transfers between devices with their start and end apart: 8, of which 5 were waited for; matrix products, arithmetic and copies ran while one was open for 1% of the time, Pallas kernels for 13%

profile of v7, /device:TPU:1, one launch (start us, length us, event | category | flops | bytes accessed | tf_op | source)
XLA Modules:
  0.0 103.8 jit_solution(13090080614496783756)
XLA Ops:
  0.6 2.2 %pack.1 = (bf16[440,384]{1,0:T(8,128)(2,1)}, bf16[152,384]{1,0:T(8,128)(2,1)}, bf16[152,384]{1,0:T(8,128)(2,1)}, f32[8,384]{1,0:T(8,128)}) custom-call(bf16[1152,192]{1,0:T(8,128)(2,1)} %bitcast.33, bf16[1152,192]{1,0:T(8,128)(2,1)} %bitcast.35, s32[12,12]{1,0:T(8,128)} %ids_ref.1), custom_call_target="tpu_custom_call" | custom-call | tf_op jit(solution)/shard_map/pack/pallas_call | solution.py:596
  2.8 8.0 %collective-permute-start = (bf16[440,384]{1,0:T(8,128)(2,1)}, bf16[440,384]{1,0:T(8,128)(2,1)S(1)}, u32[]{:S(2)}, u32[]{:S(2)}) collective-permute-start(bf16[440,384]{1,0:T(8,128)(2,1)} %get-tuple-element.36), channel_id=1, source_target_pairs={{0,124},{1,125},{2,126},{3,127},{4,0},{5,1},{6,2},{7,3},{8,4},{9,5... | collective-permute-start | bytes 1013768 | tf_op jit(solution)/shard_map/ppermute | solution.py:613
  10.8 1.0 collective-permute-start.1
  11.8 1.7 %collective-permute-start.2 = (bf16[152,384]{1,0:T(8,128)(2,1)}, bf16[152,384]{1,0:T(8,128)(2,1)S(1)}, u32[]{:S(2)}, u32[]{:S(2)}) collective-permute-start(bf16[152,384]{1,0:T(8,128)(2,1)} %get-tuple-element.38), channel_id=1, source_target_pairs={{0,127},{1,124},{2,125},{3,126},{4,3},{5,0},{6,1},{7,2},{8,7},{9,4... | collective-permute-start | bytes 350216 | tf_op jit(solution)/shard_map/ppermute | solution.py:613
  13.5 0.7 pad_add_fusion.scal_ref
  14.2 1.7 %copy-done = f32[32,6,3312]{2,0,1:T(8,128)S(1)} copy-done((f32[32,6,3312]{2,0,1:T(8,128)S(1)}, f32[32,6,3312]{2,0,1:T(8,128)}, u32[]{:S(2)}) %copy-start) | copy-done | bytes 2543640
  15.9 0.0 copy-start.5
  16.0 0.0 copy-start.6
  16.0 0.0 copy-start.7
  16.0 0.0 copy-start.8
  16.0 0.0 copy-start.9
  16.0 8.4 %bias.1.b_ref = f32[8,864,144]{2,1,0:T(8,128)S(1)} custom-call(s32[9]{0:T(128)S(1)} %pad_add_fusion.scal_ref, f32[6,32,3312]{2,1,0:T(8,128)S(1)} %bitcast.30), custom_call_target="tpu_custom_call" | custom-call | flops 2000000000 | bytes 7000000 | tf_op jit(solution)/shard_map/bias/pallas_call | solution.py:113
  24.4 0.9 collective-permute-done.1.s_ref
  25.4 0.0 collective-permute-done.2.d_ref
  25.4 0.0 collective-permute-done.e_ref
  25.4 0.0 copy-done.1
  25.4 0.0 copy-done.2
  25.5 18.9 %windows.1 = (bf16[432,192]{1,0:T(8,128)(2,1)S(1)}, bf16[432,192]{1,0:T(8,128)(2,1)S(1)}, bf16[144,192]{1,0:T(8,128)(2,1)S(1)}, bf16[144,192]{1,0:T(8,128)(2,1)S(1)}, bf16[3072,128]{1,0:T(8,128)(2,1)}) custom-call(s32[9]{0:T(128)S(1)} %pad_add_fusion.scal_ref, bf16[1152,192]{1,0:T(8,128)(2,1)S(1)} %bitcast.34, bf16[1152,192]{1,0:T(8,128)(2,1)S(1)} %bitcast.36, ...), custom_call_target="tpu_custom_call" | custom-call | flops 4000000000 | bytes 8000000 | tf_op jit(solution)/shard_map/windows/pallas_call | solution.py:386
  44.3 5.2 %all-to-all-start = ((bf16[128,24,128]{2,1,0:T(8,128)(2,1)}), bf16[128,24,128]{2,1,0:T(8,128)(2,1)S(1)}, u32[]{:S(2)}, u32[]{:S(2)}) async-start(bf16[128,24,128]{2,1,0:T(8,128)(2,1)} %bitcast.15), calls=%async_computation | async-start | bytes 1572864 | tf_op jit(solution)/shard_map/all_to_all | solution.py:659
  49.5 16.3 %all-to-all-done = bf16[128,24,128]{2,1,0:T(8,128)(2,1)S(1)} async-done(((bf16[128,24,128]{2,1,0:T(8,128)(2,1)}), bf16[128,24,128]{2,1,0:T(8,128)(2,1)S(1)}, u32[]{:S(2)}, u32[]{:S(2)}) %all-to-all-start) | async-done | bytes 786464 | tf_op jit(solution)/shard_map/all_to_all | solution.py:659
  65.8 0.2 sums.1
  66.0 20.4 %all_to_all.10 = bf16[64,48,128]{2,1,0:T(8,128)(2,1)S(1)} all-to-all(bf16[64,48,128]{2,1,0:T(8,128)(2,1)S(1)} %bitcast.32), channel_id=1, replica_groups={{0,2,4,6,8,10,12,14,16,18,20,22,24,26,28,30,32,34,36,38,40,42,44,46,48,..., dimensions={0} | all-to-all | bytes 1572864 | tf_op jit(solution)/shard_map/all_to_all | solution.py:663
  86.4 1.5 %collective-permute-start.3 = (bf16[64,48,128]{2,1,0:T(8,128)(2,1)S(1)}, bf16[64,48,128]{2,1,0:T(8,128)(2,1)S(1)}, u32[]{:S(2)}, u32[]{:S(2)}) collective-permute-start(bf16[64,48,128]{2,1,0:T(8,128)(2,1)S(1)} %all_to_all.10), channel_id=1, source_target_pairs={{0,1},{1,0},{2,3},{3,2},{4,5},{5,4},{6,7},{7,6},{8,9},{9,8},{10,11... | collective-permute-start | bytes 2359304 | tf_op jit(solution)/shard_map/ppermute | solution.py:666
  87.9 1.9 %collective-permute-done.3 = bf16[64,48,128]{2,1,0:T(8,128)(2,1)S(1)} collective-permute-done((bf16[64,48,128]{2,1,0:T(8,128)(2,1)S(1)}, bf16[64,48,128]{2,1,0:T(8,128)(2,1)S(1)}, u32[]{:S(2)}, u32[]{:S(2)}) %collective-permute-start.3) | collective-permute-done | bytes 786464 | tf_op jit(solution)/shard_map/ppermute | solution.py:666
  89.8 1.1 %collective-permute-start.5 = (bf16[144,192]{1,0:T(8,128)(2,1)S(1)}, bf16[144,192]{1,0:T(8,128)(2,1)S(1)}, u32[]{:S(2)}, u32[]{:S(2)}) collective-permute-start(bf16[144,192]{1,0:T(8,128)(2,1)S(1)} %get-tuple-element.49), channel_id=1, source_target_pairs={{0,1},{1,2},{2,3},{3,0},{4,5},{5,6},{6,7},{7,4},{8,9},{9,10},{10,1... | collective-permute-start | bytes 165896 | tf_op jit(solution)/shard_map/ppermute | solution.py:613
  90.9 0.0 collective-permute-start.6
  90.9 0.1 collective-permute-start.4
  91.0 4.7 %spread.1 = (f32[6,32,3312]{2,1,0:T(8,128)}, f32[4,192]{1,0:T(4,128)}, f32[192]{0:T(256)}, f32[192]{0:T(256)}, f32[192,576]{1,0:T(8,128)}, /*index=5*/f32[576]{0:T(1024)}, f32[192,192]{1,0:T(8,128)}, f32[192]{0:T(256)}) custom-call(s32[8,128]{1,0:T(8,128)S(1)} %get-tuple-element.41.scal_ref, bf16[3072,128]{1,0:T(8,128)(2,1)S(1)} %bitcast.31, ...), custom_call_target="tpu_custom_call" | custom-call | flops 10000000000 | bytes 10000000 | tf_op jit(solution)/shard_map/spread/pallas_call | solution.py:537
  95.7 0.0 collective-permute-done.5
  95.7 4.7 %collective-permute-done.6 = bf16[144,192]{1,0:T(8,128)(2,1)S(1)} collective-permute-done((bf16[144,192]{1,0:T(8,128)(2,1)S(1)}, bf16[144,192]{1,0:T(8,128)(2,1)S(1)}, u32[]{:S(2)}, u32[]{:S(2)}) %collective-permute-start.6) | collective-permute-done | bytes 55328 | tf_op jit(solution)/shard_map/ppermute | solution.py:613
  100.4 2.4 %collective-permute-done.4 = bf16[432,192]{1,0:T(8,128)(2,1)S(1)} collective-permute-done((bf16[432,192]{1,0:T(8,128)(2,1)S(1)}, bf16[432,192]{1,0:T(8,128)(2,1)S(1)}, u32[]{:S(2)}, u32[]{:S(2)}) %collective-permute-start.4) | collective-permute-done | bytes 165920 | tf_op jit(solution)/shard_map/ppermute | solution.py:613
  102.9 0.9 maximum_bitcast_fusion
  (12 shorter events, 0.0 us)
Async XLA Ops:
  2.8 22.5 %collective-permute-start = (bf16[440,384]{1,0:T(8,128)(2,1)}, bf16[440,384]{1,0:T(8,128)(2,1)S(1)}, u32[]{:S(2)}, u32[]{:S(2)}) collective-permute-start(bf16[440,384]{1,0:T(8,128)(2,1)} %get-tuple-element.36), channel_id=1, source_target_pairs={{0,124},{1,125},{2,126},{3,127},{4,0},{5,1},{6,2},{7,3},{8,4},{9,5... | collective-permute-start | bytes 1013768 | tf_op jit(solution)/shard_map/ppermute | solution.py:613
  10.8 14.5 %collective-permute-start.1 = (bf16[152,384]{1,0:T(8,128)(2,1)}, bf16[152,384]{1,0:T(8,128)(2,1)S(1)}, u32[]{:S(2)}, u32[]{:S(2)}) collective-permute-start(bf16[152,384]{1,0:T(8,128)(2,1)} %get-tuple-element.37), channel_id=1, source_target_pairs={{0,3},{1,0},{2,1},{3,2},{4,7},{5,4},{6,5},{7,6},{8,11},{9,8},{10,9... | collective-permute-start | bytes 350216 | tf_op jit(solution)/shard_map/ppermute | solution.py:613
  11.8 13.6 %collective-permute-start.2 = (bf16[152,384]{1,0:T(8,128)(2,1)}, bf16[152,384]{1,0:T(8,128)(2,1)S(1)}, u32[]{:S(2)}, u32[]{:S(2)}) collective-permute-start(bf16[152,384]{1,0:T(8,128)(2,1)} %get-tuple-element.38), channel_id=1, source_target_pairs={{0,127},{1,124},{2,125},{3,126},{4,3},{5,0},{6,1},{7,2},{8,7},{9,4... | collective-permute-start | bytes 350216 | tf_op jit(solution)/shard_map/ppermute | solution.py:613
  14.2 1.7 %copy-start = (f32[32,6,3312]{2,0,1:T(8,128)S(1)}, f32[32,6,3312]{2,0,1:T(8,128)}, u32[]{:S(2)}) copy-start(f32[32,6,3312]{2,0,1:T(8,128)} %param.21) | copy-start | bytes 7630852
  15.9 9.4 %copy-start.1 = (bf16[1,8,12,12,192]{4,1,3,2,0:T(8,128)(2,1)S(1)}, bf16[1,8,12,12,192]{4,1,3,2,0:T(8,128)(2,1)}, u32[]{:S(2)}) copy-start(bf16[1,8,12,12,192]{4,1,3,2,0:T(8,128)(2,1)} %param.11) | copy-start | bytes 1327108
  15.9 9.4 %copy-start.2 = (bf16[1,8,12,12,192]{4,1,3,2,0:T(8,128)(2,1)S(1)}, bf16[1,8,12,12,192]{4,1,3,2,0:T(8,128)(2,1)}, u32[]{:S(2)}) copy-start(bf16[1,8,12,12,192]{4,1,3,2,0:T(8,128)(2,1)} %param.12) | copy-start | bytes 1327108
  15.9 9.4 %copy-start.3 = (bf16[192,576]{1,0:T(8,128)(2,1)S(1)}, bf16[192,576]{1,0:T(8,128)(2,1)}, u32[]{:S(2)}) copy-start(bf16[192,576]{1,0:T(8,128)(2,1)} %w_ref.1) | copy-start | bytes 663556
  15.9 9.4 %copy-start.4 = (bf16[192,192]{1,0:T(8,128)(2,1)S(1)}, bf16[192,192]{1,0:T(8,128)(2,1)}, u32[]{:S(2)}) copy-start(bf16[192,192]{1,0:T(8,128)(2,1)} %wo_ref.1) | copy-start | bytes 221188
  15.9 9.5 %copy-start.5 = (f32[8,384]{1,0:T(8,128)S(1)}, f32[8,384]{1,0:T(8,128)}, u32[]{:S(2)}) copy-start(f32[8,384]{1,0:T(8,128)} %get-tuple-element.39.ids_ref) | copy-start | bytes 36868
  16.0 9.5 %copy-start.6 = (f32[4,192]{1,0:T(4,128)S(1)}, f32[4,192]{1,0:T(4,128)}, u32[]{:S(2)}) copy-start(f32[4,192]{1,0:T(4,128)} %ct_ref.1) | copy-start | bytes 9220
  16.0 9.5 %copy-start.7 = (f32[576]{0:T(1024)S(1)}, f32[576]{0:T(1024)}, u32[]{:S(2)}) copy-start(f32[576]{0:T(1024)} %bq_ref.1) | copy-start | bytes 6916
  16.0 9.4 %copy-start.8 = (f32[192]{0:T(256)S(1)}, f32[192]{0:T(256)}, u32[]{:S(2)}) copy-start(f32[192]{0:T(256)} %param.16) | copy-start | bytes 2308
  16.0 9.4 %copy-start.9 = (f32[192]{0:T(256)S(1)}, f32[192]{0:T(256)}, u32[]{:S(2)}) copy-start(f32[192]{0:T(256)} %param.17) | copy-start | bytes 2308
  44.3 21.4 %all-to-all-start = ((bf16[128,24,128]{2,1,0:T(8,128)(2,1)}), bf16[128,24,128]{2,1,0:T(8,128)(2,1)S(1)}, u32[]{:S(2)}, u32[]{:S(2)}) async-start(bf16[128,24,128]{2,1,0:T(8,128)(2,1)} %bitcast.15), calls=%async_computation | async-start | bytes 1572864 | tf_op jit(solution)/shard_map/all_to_all | solution.py:659
  86.4 3.5 %collective-permute-start.3 = (bf16[64,48,128]{2,1,0:T(8,128)(2,1)S(1)}, bf16[64,48,128]{2,1,0:T(8,128)(2,1)S(1)}, u32[]{:S(2)}, u32[]{:S(2)}) collective-permute-start(bf16[64,48,128]{2,1,0:T(8,128)(2,1)S(1)} %all_to_all.10), channel_id=1, source_target_pairs={{0,1},{1,0},{2,3},{3,2},{4,5},{5,4},{6,7},{7,6},{8,9},{9,8},{10,11... | collective-permute-start | bytes 2359304 | tf_op jit(solution)/shard_map/ppermute | solution.py:666
  89.8 5.9 %collective-permute-start.5 = (bf16[144,192]{1,0:T(8,128)(2,1)S(1)}, bf16[144,192]{1,0:T(8,128)(2,1)S(1)}, u32[]{:S(2)}, u32[]{:S(2)}) collective-permute-start(bf16[144,192]{1,0:T(8,128)(2,1)S(1)} %get-tuple-element.49), channel_id=1, source_target_pairs={{0,1},{1,2},{2,3},{3,0},{4,5},{5,6},{6,7},{7,4},{8,9},{9,10},{10,1... | collective-permute-start | bytes 165896 | tf_op jit(solution)/shard_map/ppermute | solution.py:613
  90.9 9.5 %collective-permute-start.6 = (bf16[144,192]{1,0:T(8,128)(2,1)S(1)}, bf16[144,192]{1,0:T(8,128)(2,1)S(1)}, u32[]{:S(2)}, u32[]{:S(2)}) collective-permute-start(bf16[144,192]{1,0:T(8,128)(2,1)S(1)} %get-tuple-element.50), channel_id=1, source_target_pairs={{0,5},{1,6},{2,7},{3,4},{4,9},{5,10},{6,11},{7,8},{8,13},{9,14},{1... | collective-permute-start | bytes 165896 | tf_op jit(solution)/shard_map/ppermute | solution.py:613
  90.9 12.0 %collective-permute-start.4 = (bf16[432,192]{1,0:T(8,128)(2,1)S(1)}, bf16[432,192]{1,0:T(8,128)(2,1)S(1)}, u32[]{:S(2)}, u32[]{:S(2)}) collective-permute-start(bf16[432,192]{1,0:T(8,128)(2,1)S(1)} %get-tuple-element.48), channel_id=1, source_target_pairs={{0,4},{1,5},{2,6},{3,7},{4,8},{5,9},{6,10},{7,11},{8,12},{9,13},{1... | collective-permute-start | bytes 497672 | tf_op jit(solution)/shard_map/ppermute | solution.py:613
